TPU v7x, 32 devices: a whole 2x2x4 slice. The times are simulated.
32 devices in a mesh: ctx: 8 (over y, x, core), shard: 4 (over z).
Axes of the slice: x: 2, y: 2, z: 4, core: 2. Of those that a mesh axis runs over, the one named last changes fastest.
Arguments:
- layer_input: bfloat16 [2, 4096, 768], P(None, ('ctx', 'shard')), may hold values from -6 to 6
- attn_gain: bfloat16 [768], P('shard'), may hold values from 0.099609375 to 1.8984375
- attn_shift: bfloat16 [768], P('shard'), may hold values from -3 to 3
- qkv_weight: bfloat16 [768, 2304], P('shard'), may hold values from -0.3125 to 0.3125
- query_bias: bfloat16 [768], P('shard'), may hold values from -3 to 3
- value_bias: bfloat16 [768], P('shard'), may hold values from -3 to 3
- proj_weight: bfloat16 [768, 768], P('shard'), may hold values from -3.5 to 3.5
- proj_bias: bfloat16 [768], P('shard'), may hold values from -1.75 to 1.75
- mlp_gain: bfloat16 [768], P('shard'), may hold values from 0.099609375 to 1.8984375
- mlp_shift: bfloat16 [768], P('shard'), may hold values from -3 to 3
- fc_weight: bfloat16 [768, 3072], P('shard'), may hold values from -0.21875 to 0.21875
- fc_bias: bfloat16 [3072], P('shard'), may hold values from -3 to 3
- out_weight: bfloat16 [3072, 768], P('shard'), may hold values from -0.109375 to 0.109375
- out_bias: bfloat16 [768], P('shard'), may hold values from -1.75 to 1.75
- grad_output: bfloat16 [2, 4096, 768], P(None, ('ctx', 'shard')), may hold values from -6 to 6
Outputs:
- layer_output: bfloat16 [2, 4096, 768], P(None, ('ctx', 'shard'))
- input_grad: bfloat16 [2, 4096, 768], P(None, ('ctx', 'shard'))
- attn_gain_grad: float32 [768], P('shard')
- attn_shift_grad: float32 [768], P('shard')
- qkv_weight_grad: float32 [768, 2304], P('shard')
- query_bias_grad: float32 [768], P('shard')
- value_bias_grad: float32 [768], P('shard')
- proj_weight_grad: float32 [768, 768], P('shard')
- proj_bias_grad: float32 [768], P('shard')
- mlp_gain_grad: float32 [768], P('shard')
- mlp_shift_grad: float32 [768], P('shard')
- fc_weight_grad: float32 [768, 3072], P('shard')
- fc_bias_grad: float32 [3072], P('shard')
- out_weight_grad: float32 [3072, 768], P('shard')
- out_bias_grad: float32 [768], P('shard')
All inputs are finite; a program needn't handle non-finite values.
Results may differ from a plain program's by a relative error of at most 0.014.
The roundings to bfloat16 on the way count: a program that leaves them out, or rounds other values in their place, can miss the bound.
Values may be sent and summed in bfloat16 or wider, within the bound.
No kernel may reach another device: no remote copies, remote signals or barrier semaphores. Data moves between devices by JAX's collectives and lax.ppermute only.
A program may use at most 256 MiB of HBM per device.

v0:
```python
import functools

import jax
import jax.numpy as jnp
from jax import lax
from jax.experimental import pallas as pl
from jax.experimental.pallas import tpu as pltpu
from jax.sharding import PartitionSpec as P

HEADS = 12
HEAD = 64
TILE = 512
EXP2_SCALE = 0.125 * 1.4426950408889634
f32 = jnp.float32
bf16 = jnp.bfloat16
FC_BIT = 1
OUT_BIT = 2
VMEM_LIMIT = 56 * 1024 * 1024


def normalized(values):
    centered = values - jnp.mean(values, axis=-1, keepdims=True)
    variance = jnp.mean(centered * centered, axis=-1, keepdims=True)
    return centered * lax.rsqrt(variance + 1e-05)


def layer_norm(values, gain, shift):
    return normalized(values) * gain + shift


def gelu_tanh(values):
    return jax.nn.gelu(values, approximate=True)


def swapped(block, bit):
    n = lax.axis_size("ctx")
    return lax.ppermute(block, "ctx", [(i, i ^ (1 << bit)) for i in range(n)])


def tree_pairs(aparts, bit, later, late, back):
    n = lax.axis_size("ctx")
    reach = [0]
    for other in later:
        reach += [r ^ (1 << other) for r in reach]
    pairs = []
    for i in range(n):
        target = i ^ (1 << bit)
        queries = [n - 1 - (target ^ r) if late else target ^ r for r in reach]
        if any(i ^ apart <= max(queries) for apart in aparts):
            pairs.append((target, i) if back else (i, target))
    return pairs


def spread(own, order, late, before):
    held, aparts = own[None], [0]
    for bit in order[:-2]:
        pairs = tree_pairs(aparts, bit, order[order.index(bit) + 1 :], late, False)
        held = jnp.concatenate([held, lax.ppermute(held, "ctx", pairs)])
        aparts = aparts + [apart ^ (1 << bit) for apart in aparts]
    bit = order[-2]
    held = after(held, *before)
    received = lax.ppermute(held, "ctx", tree_pairs(aparts, bit, order[-1:], late, False))
    aparts = aparts + [apart ^ (1 << bit) for apart in aparts]
    blocks = [held, received, swapped(held, 0), swapped(received, 0)]
    return blocks, aparts + [apart ^ 1 for apart in aparts]


def added(first, second):
    return (first.astype(f32) + second.astype(f32)).astype(bf16)


def returned(near, middle, far, aparts, order, late):
    received = swapped(far, 0)
    count = near.shape[0]
    middle = added(middle, received[count:])
    pairs = tree_pairs(aparts[:count], order[-2], order[-1:], late, True)
    near = added(added(near, received[:count]), lax.ppermute(middle, "ctx", pairs))
    for bit in order[:-2][::-1]:
        count = near.shape[0] // 2
        pairs = tree_pairs(aparts[:count], bit, order[order.index(bit) + 1 :], late, True)
        near = added(near[:count], lax.ppermute(near[count:], "ctx", pairs))
    return near[0]


def after(value, *others):
    return lax.optimization_barrier((value,) + others)[0]


def mirrored(block):
    n = lax.axis_size("ctx")
    return lax.ppermute(block, "ctx", [(i, n - 1 - i) for i in range(n)])


def shifted(block, distance):
    n = lax.axis_size("shard")
    return lax.ppermute(block, "shard", [(i, (i + distance) % n) for i in range(n)])


def dot(a, b, contract):
    return lax.dot_general(a, b, ((contract[0], contract[1]), ((), ())), preferred_element_type=f32)


def summed_over_chips(part, bits):
    for bit in bits:
        low = part.astype(bf16)
        part = low.astype(f32) + swapped(low, bit).astype(f32)
    return part


def joined(half, bit, side):
    other = swapped(half, bit)
    return jnp.where(side, other, half), jnp.where(side, half, other)


def pair_joined(half, odd):
    return joined(half, 0, odd)


def load_blocks(refs, held, sems):
    each = refs[0].shape[0]
    copies = [
        pltpu.make_async_copy(ref, held.at[pl.ds(i * each, each)], sems.at[i])
        for i, ref in enumerate(refs)
    ]
    for copy in copies:
        copy.start()
    return copies


def slot_of(place, here, order):
    apart = place ^ here
    return sum(((apart >> bit) & 1) << k for k, bit in enumerate(order))


def forward_kernel(heads, shards, order, info, q_ref, *refs):
    kv_refs = refs[:4]
    att_ref, out_ref, lse_ref, held, sems, m_ref, l_ref, acc_ref = refs[4:]
    rows, width = q_ref.shape
    piece = rows // shards
    tile = min(TILE, rows)
    per = rows // tile
    copies = load_blocks(kv_refs, held, sems)
    key_places = lax.broadcasted_iota(jnp.int32, (rows, 1), 0)
    query_places = lax.broadcasted_iota(jnp.int32, (1, rows), 1)
    for copy in copies:
        copy.wait()
    for part in range(per):
        span = slice(part * tile, (part + 1) * tile)

        def step(slot, key_part, masked, start):
            keys_at = slice(key_part * tile, (key_part + 1) * tile)
            allowed = key_places[keys_at] <= query_places[:, span] if masked else None
            for h in range(heads):
                lanes = slice(h * HEAD, (h + 1) * HEAD)
                lanes_v = slice(width + h * HEAD, width + (h + 1) * HEAD)
                q = q_ref[span, lanes]
                k = held[slot, keys_at, lanes]
                v = held[slot, keys_at, lanes_v]
                s = dot(k, q, ((1,), (1,))) * EXP2_SCALE
                if masked:
                    s = jnp.where(allowed, s, -1e30)
                m = jnp.max(s, axis=0, keepdims=True)
                if start:
                    p = jnp.exp2(s - m)
                    l_ref[h] = jnp.sum(p, axis=0, keepdims=True)
                    acc_ref[h] = dot(v, p.astype(bf16), ((0,), (0,)))
                else:
                    old = m_ref[h]
                    m = jnp.maximum(old, m)
                    p = jnp.exp2(s - m)
                    factor = jnp.exp2(old - m)
                    l_ref[h] = l_ref[h] * factor + jnp.sum(p, axis=0, keepdims=True)
                    acc_ref[h] = acc_ref[h] * factor + dot(v, p.astype(bf16), ((0,), (0,)))
                m_ref[h] = m

        for key_part in range(per):
            step(slot_of(info[0], info[1], order), key_part, True, key_part == 0)

        @pl.loop(0, info[0])
        def _(j):
            for key_part in range(per):
                step(slot_of(j, info[1], order), key_part, False, False)

        for h in range(heads):
            total = l_ref[h]
            done = acc_ref[h] / total
            out_ref[h * HEAD : (h + 1) * HEAD, span] = done
            lse_ref[h, :, span] = m_ref[h] + jnp.log2(total)
            low = done.astype(bf16)
            for z in range(tile // piece):
                att_ref[part * (tile // piece) + z, h * HEAD : (h + 1) * HEAD, :] = low[
                    :, z * piece : (z + 1) * piece
                ]


def backward_kernel(heads, shards, order, first, info, q_ref, out_ref, lse_ref, go_ref, *refs):
    kv_refs = refs[:4]
    dq_ref, near_ref, middle_ref, far_ref, held, sums, sems, end_sems, acc_ref = refs[4:]
    count = held.shape[0]
    rows, width = q_ref.shape
    piece = rows // shards
    tile = min(TILE, rows)
    per = rows // tile
    copies = load_blocks(kv_refs, held, sems)
    key_places = lax.broadcasted_iota(jnp.int32, (rows, 1), 0)
    query_places = lax.broadcasted_iota(jnp.int32, (1, rows), 1)

    @pl.loop(info[0] + 1, count)
    def _(j):
        sums[slot_of(j, info[1], order)] = jnp.zeros((rows, 2 * width), bf16)

    for copy in copies:
        copy.wait()
    for part in range(per):
        span = slice(part * tile, (part + 1) * tile)
        pieces = range(part * (tile // piece), (part + 1) * (tile // piece))
        go_all = jnp.concatenate(
            [go_ref[z, :, first : first + piece] for z in pieces], axis=1
        )
        deltas = []
        for h in range(heads):
            lanes = slice(h * HEAD, (h + 1) * HEAD)
            deltas.append(
                jnp.sum(go_all[lanes].astype(f32) * out_ref[lanes, span], axis=0, keepdims=True)
            )

        def step(slot, key_part, masked, start):
            keys_at = slice(key_part * tile, (key_part + 1) * tile)
            allowed = key_places[keys_at] <= query_places[:, span] if masked else None
            for h in range(heads):
                lanes = slice(h * HEAD, (h + 1) * HEAD)
                lanes_v = slice(width + h * HEAD, width + (h + 1) * HEAD)
                q = q_ref[span, lanes]
                go = go_all[lanes]
                k = held[slot, keys_at, lanes]
                v = held[slot, keys_at, lanes_v]
                p = jnp.exp2(dot(k, q, ((1,), (1,))) * EXP2_SCALE - lse_ref[h, :, span])
                if masked:
                    p = jnp.where(allowed, p, 0.0)
                pulled = dot(v, go, ((1,), (0,)))
                slopes = (p * (pulled - deltas[h])).astype(bf16)
                dv = dot(p.astype(bf16), go, ((1,), (1,)))
                dk = dot(slopes, q, ((1,), (0,))) * 0.125
                if part:
                    dk = dk + sums[slot, keys_at, lanes].astype(f32)
                    dv = dv + sums[slot, keys_at, lanes_v].astype(f32)
                sums[slot, keys_at, lanes] = dk.astype(bf16)
                sums[slot, keys_at, lanes_v] = dv.astype(bf16)
                dq = dot(k, slopes, ((0,), (0,)))
                if start:
                    acc_ref[h] = dq
                else:
                    acc_ref[h] += dq

        for key_part in range(per):
            step(slot_of(info[0], info[1], order), key_part, True, key_part == 0)

        @pl.loop(0, info[0])
        def _(j):
            for key_part in range(per):
                step(slot_of(j, info[1], order), key_part, False, False)

        for h in range(heads):
            dq_ref[span, h * HEAD : (h + 1) * HEAD] = (acc_ref[h] * 0.125).T.astype(bf16)
    copies = []
    base = 0
    for i, ref in enumerate((near_ref, middle_ref, far_ref)):
        copies.append(
            pltpu.make_async_copy(sums.at[pl.ds(base, ref.shape[0])], ref, end_sems.at[i])
        )
        base += ref.shape[0]
    for copy in copies:
        copy.start()
    for copy in copies:
        copy.wait()


SMEM = pl.BlockSpec(memory_space=pltpu.SMEM)
VMEM = pl.BlockSpec(memory_space=pltpu.VMEM)
ANY = pl.BlockSpec(memory_space=pl.ANY)


def attend(shards, order, info, queries, blocks):
    rows, width = queries.shape
    heads = width // HEAD
    count = 4 * blocks[0].shape[0]
    tile = min(TILE, rows)
    scores = heads * rows * rows * (count + 1) // 2
    return pl.pallas_call(
        functools.partial(forward_kernel, heads, shards, order),
        out_shape=(
            jax.ShapeDtypeStruct((shards, width, rows // shards), bf16),
            jax.ShapeDtypeStruct((width, rows), f32),
            jax.ShapeDtypeStruct((heads, 1, rows), f32),
        ),
        in_specs=[SMEM, VMEM] + [ANY] * 4,
        out_specs=(VMEM, VMEM, VMEM),
        scratch_shapes=[
            pltpu.VMEM((count, rows, 2 * width), bf16),
            pltpu.SemaphoreType.DMA((4,)),
            pltpu.VMEM((heads, 1, tile), f32),
            pltpu.VMEM((heads, 1, tile), f32),
            pltpu.VMEM((heads, HEAD, tile), f32),
        ],
        compiler_params=pltpu.CompilerParams(vmem_limit_bytes=VMEM_LIMIT),
        cost_estimate=pl.CostEstimate(
            flops=scores * 16 * HEAD,
            bytes_accessed=4 * rows * width * (count + 2),
            transcendentals=scores,
        ),
        name="attention_forward",
    )(info, queries, *blocks)


def attend_back(shards, order, first, info, queries, out, lse, grads, blocks):
    rows, width = queries.shape
    heads = width // HEAD
    count = 4 * blocks[0].shape[0]
    tile = min(TILE, rows)
    scores = heads * rows * rows * (count + 1) // 2
    return pl.pallas_call(
        functools.partial(backward_kernel, heads, shards, order, first),
        out_shape=[jax.ShapeDtypeStruct((rows, width), bf16)]
        + [
            jax.ShapeDtypeStruct((share, rows, 2 * width), bf16)
            for share in (count // 4, count // 4, count // 2)
        ],
        in_specs=[SMEM] + [VMEM] * 4 + [ANY] * 4,
        out_specs=[VMEM] + [ANY] * 3,
        scratch_shapes=[
            pltpu.VMEM((count, rows, 2 * width), bf16),
            pltpu.VMEM((count, rows, 2 * width), bf16),
            pltpu.SemaphoreType.DMA((4,)),
            pltpu.SemaphoreType.DMA((3,)),
            pltpu.VMEM((heads, HEAD, tile), f32),
        ],
        compiler_params=pltpu.CompilerParams(vmem_limit_bytes=VMEM_LIMIT),
        cost_estimate=pl.CostEstimate(
            flops=scores * 40 * HEAD,
            bytes_accessed=8 * rows * width * (count + 2),
            transcendentals=scores,
        ),
        name="attention_backward",
    )(info, queries, out, lse, grads, *blocks)


def body(
    layer_input,
    attn_gain,
    attn_shift,
    qkv_weight,
    query_bias,
    value_bias,
    proj_weight,
    proj_bias,
    mlp_gain,
    mlp_shift,
    fc_weight,
    fc_bias,
    out_weight,
    out_bias,
    grad_output,
):
    seqs, piece, width = layer_input.shape
    cycle = lax.axis_size("ctx")
    shards = lax.axis_size("shard")
    here = lax.axis_index("ctx")
    shard_at = lax.axis_index("shard")
    odd = here & 1
    chip_bits = list(range(1, cycle.bit_length() - 1))
    rows = shards * piece
    local_width = qkv_weight.shape[0]
    local_hidden = out_weight.shape[0]
    half_width = local_width // 2
    half_hidden = local_hidden // 2
    quarter = half_hidden // 2
    group = -(-HEADS // shards) * HEAD
    padded = group * shards
    late = [seq >= (seqs + 1) // 2 for seq in range(seqs)]
    tokens = seqs * piece

    gathered = lax.all_gather(layer_input, "shard", axis=0)

    def by_heads(weight):
        parts = []
        for third in range(3):
            part = weight[:, third * width : (third + 1) * width]
            parts.append(jnp.pad(part, ((0, 0), (0, padded - width))))
        return jnp.stack(
            [
                jnp.concatenate([part[:, z * group : (z + 1) * group] for part in parts], axis=1)
                for z in range(shards)
            ]
        )

    weight_half = lax.dynamic_slice_in_dim(qkv_weight, odd * half_width, half_width, 0)
    packed = jnp.concatenate(
        [
            jnp.stack(
                [attn_gain, attn_shift, query_bias, value_bias, proj_bias, mlp_gain, mlp_shift, out_bias]
            ),
            fc_bias.reshape(-1, local_width),
        ]
    )
    vector_rows = packed.shape[0]
    packed = jnp.pad(packed, ((0, 16 - vector_rows), (0, 3 * group - local_width)))
    moved = lax.all_to_all(
        jnp.concatenate(
            [by_heads(weight_half), jnp.broadcast_to(packed, (shards,) + packed.shape)], axis=1
        ),
        "shard",
        0,
        0,
        tiled=True,
    )
    small = moved[:, half_width : half_width + vector_rows, :local_width].astype(f32)
    qkv_own = jnp.stack(pair_joined(moved[:, :half_width], odd), axis=1).reshape(width, 3 * group)
    q_weight = qkv_own[:, :group]
    kv_weight = qkv_own[:, group:]

    vectors = [small[:, i].reshape(-1) for i in range(8)]
    gain_one, shift_one, query_add, value_add, proj_add, gain_two, shift_two, out_add = vectors
    fc_add = lax.dynamic_index_in_dim(
        small[:, 8:].reshape(shards, 2, half_hidden), odd, 1, False
    ).reshape(-1)

    def own_heads(vector):
        return lax.dynamic_slice_in_dim(
            jnp.pad(vector, (0, padded - width)), shard_at * group, group, 0
        )

    kv_add = jnp.concatenate([jnp.zeros((group,), f32), own_heads(value_add)])
    query_add = own_heads(query_add)

    fc_side = (here >> FC_BIT) & 1
    out_side = (here >> OUT_BIT) & 1
    proj_half = lax.dynamic_slice_in_dim(proj_weight, odd * half_width, half_width, 0)
    fc_quarter = jnp.concatenate(
        [
            lax.dynamic_slice_in_dim(
                fc_weight,
                (fc_side * (shards // 2) + z) * local_hidden + odd * half_hidden,
                half_hidden,
                1,
            )
            for z in range(shards // 2)
        ],
        axis=1,
    )
    moved = lax.all_gather(jnp.concatenate([proj_half, fc_quarter]), "shard", axis=0)
    proj_half = pair_joined(moved[:, :half_width], odd)
    proj_full = jnp.stack(proj_half, axis=1).reshape(width, width)
    fc_quarter = moved[:, half_width:].reshape(width, -1)
    fc_half = jnp.concatenate(joined(fc_quarter, FC_BIT, fc_side), axis=1)
    out_quarter = lax.all_gather(
        lax.dynamic_slice_in_dim(
            out_weight, odd * half_hidden + out_side * quarter, quarter, 0
        ),
        "shard",
        axis=0,
    )
    out_half = jnp.stack(joined(out_quarter, OUT_BIT, out_side), axis=1).reshape(-1, width)
    orders = [chip_bits + [0], chip_bits[::-1] + [0]]
    orders = [orders[s % 2] for s in range(seqs)]
    group_norms, normed_one, own_blocks, queries, infos = [], [], [], [], []
    for s in range(seqs):
        norm = normalized(gathered[:, s].reshape(rows, width).astype(f32))
        normed = (norm * gain_one + shift_one).astype(bf16)
        group_norms.append(norm)
        normed_one.append(normed)
        own_blocks.append((dot(normed, kv_weight, ((1,), (0,))) + kv_add).astype(bf16))
        queries.append((dot(normed, q_weight, ((1,), (0,))) + query_add).astype(bf16))
        infos.append(jnp.stack([cycle - 1 - here if late[s] else here, here]).astype(jnp.int32))
    spreads = [spread(own_blocks[s], orders[s], late[s], queries) for s in range(seqs)]
    queries = [mirrored(queries[s]) if late[s] else queries[s] for s in range(seqs)]
    blocks = [blocks for blocks, _ in spreads]
    aparts = [apart for _, apart in spreads]
    saved = [None] * seqs
    attended_parts = [None] * seqs
    for s in reversed(range(seqs)):
        att, *saved[s] = attend(shards, orders[s], infos[s], queries[s], blocks[s])
        attended_parts[s] = mirrored(att) if late[s] else att
    attended = lax.all_to_all(
        jnp.concatenate(attended_parts, axis=2), "shard", 0, 0, tiled=True
    ).reshape(padded, tokens)[:width]

    inputs32 = layer_input.reshape(tokens, width).astype(f32)
    grads_own = grad_output.reshape(tokens, width)
    grads32 = grads_own.astype(f32)
    middle = inputs32 + dot(attended, proj_full, ((0,), (0,))) + proj_add
    normed_two = layer_norm(middle, gain_two, shift_two).astype(bf16)

    normed_pair = jnp.concatenate([normed_two, swapped(normed_two, 0)])
    grads_pair = jnp.concatenate([grads_own, swapped(grads_own, 0)])
    preactivation = dot(normed_pair, fc_half, ((1,), (0,))) + fc_add
    hidden = gelu_tanh(preactivation).astype(bf16)
    out_part = dot(hidden, out_half, ((1,), (0,)))
    layer_output = middle + (out_part[:tokens] + swapped(out_part[tokens:], 0)) + out_add
    layer_output = layer_output.astype(bf16)
    grad_hidden = dot(grads_pair, out_half, ((1,), (1,)))
    grad_pre = jax.vjp(gelu_tanh, preactivation)[1](grad_hidden)[0].astype(bf16)
    normed_part = dot(grad_pre, fc_half, ((1,), (1,)))
    grad_normed_two = normed_part[:tokens] + swapped(normed_part[tokens:], 0)
    grad_mid_part, gain_two_grad, shift_two_grad = jax.vjp(
        layer_norm, middle, gain_two, shift_two
    )[1](grad_normed_two)
    grad_middle = grads32 + grad_mid_part
    grad_branch = grad_middle.astype(bf16)

    grad_attended = jnp.pad(
        dot(proj_full, grad_branch, ((1,), (1,))).astype(bf16), ((0, padded - width), (0, 0))
    ).reshape(shards, group, tokens)
    grad_heads = lax.all_to_all(grad_attended, "shard", 0, 0, tiled=True)
    flat = ((0,), (0,))

    def parted(first, second, side):
        return jnp.where(side, second, first), jnp.where(side, first, second)

    proj_grad = dot(attended, grad_branch, ((1,), (0,))).astype(bf16)
    proj_grad = proj_grad.reshape(shards, 2, half_width, width)
    mine, sent = parted(proj_grad[:, 0], proj_grad[:, 1], odd)
    proj_grad = added(mine, swapped(sent, 0))
    fc_grad = dot(normed_pair, grad_pre, flat).astype(bf16).reshape(shards, local_width, -1)
    column = fc_grad.shape[2] // 2
    fc_mine, fc_sent = parted(
        jnp.concatenate([fc_grad[..., :column], proj_grad[:, : half_width // 2]], axis=1),
        jnp.concatenate([fc_grad[..., column:], proj_grad[:, half_width // 2 :]], axis=1),
        fc_side,
    )
    out_grad = dot(hidden, grads_pair, flat).astype(bf16).reshape(shards, 2, quarter, width)
    out_mine, out_sent = parted(out_grad[:, 0], out_grad[:, 1], out_side)
    fc_received = swapped(fc_sent, FC_BIT)
    out_received = swapped(out_sent, OUT_BIT)

    query_low = [None] * seqs
    kv_parts = [None] * seqs
    grad_heads = after(grad_heads, fc_sent, out_sent)
    for s in range(seqs):
        heads_grad, first = grad_heads, s * piece
        if late[s]:
            heads_grad, first = mirrored(grad_heads[:, :, s * piece : (s + 1) * piece]), 0
        low, *kv_parts[s] = attend_back(
            shards, orders[s], first, infos[s], queries[s], *saved[s], heads_grad, blocks[s]
        )
        query_low[s] = mirrored(low) if late[s] else low

    ended = [part for parts in kv_parts for part in parts[:1]]
    scattered = jnp.concatenate(
        [
            added(fc_mine, after(fc_received, *ended)),
            added(out_mine, after(out_received, *ended)),
        ],
        axis=1,
    )
    both = lax.psum_scatter(scattered, "shard", scatter_dimension=0, tiled=False)

    kv_low = [None] * seqs
    normed_parts = []
    gain_one_grad = jnp.zeros((width,), f32)
    shift_one_grad = jnp.zeros((width,), f32)
    for s in range(seqs):
        kv_low[s] = returned(*kv_parts[s], aparts[s], orders[s], late[s])
        part = dot(query_low[s], q_weight, ((1,), (1,))) + dot(kv_low[s], kv_weight, ((1,), (1,)))
        gain_one_grad = gain_one_grad + jnp.sum(part * group_norms[s], axis=0)
        shift_one_grad = shift_one_grad + jnp.sum(part, axis=0)
        normed_parts.append(part.astype(bf16).reshape(shards, piece, width))
    fc_add_part = jnp.sum(grad_pre.astype(f32), axis=0).reshape(shards, 1, half_hidden)
    fc_add_part = jnp.where(jnp.arange(2)[None, :, None] == odd, fc_add_part, 0.0)

    def all_heads(vector):
        return lax.dynamic_update_slice_in_dim(
            jnp.zeros((padded,), f32), vector, shard_at * group, 0
        )[:width]

    query_sum = sum(jnp.sum(low.astype(f32), axis=0) for low in query_low)
    value_sum = sum(jnp.sum(low[:, group:].astype(f32), axis=0) for low in kv_low)
    vectors = jnp.stack(
        [
            gain_one_grad,
            shift_one_grad,
            all_heads(query_sum),
            all_heads(value_sum),
            jnp.sum(grad_branch.astype(f32), axis=0),
            gain_two_grad,
            shift_two_grad,
            jnp.sum(grads32, axis=0),
        ]
    )
    vectors = jnp.concatenate(
        [
            vectors.reshape(8, shards, local_width).transpose(1, 0, 2),
            fc_add_part.reshape(shards, -1, local_width),
        ],
        axis=1,
    ).astype(bf16)
    normed_parts = jnp.concatenate(
        normed_parts
        + [jnp.pad(vectors, ((0, 0), (0, 16 - vector_rows), (0, width - local_width)))],
        axis=1,
    )
    summed = lax.psum_scatter(normed_parts, "shard", scatter_dimension=0, tiled=False).astype(f32)
    pull = jax.vjp(lambda v: normalized(v) * gain_one, inputs32)[1]
    input_grad = (grad_middle + pull(summed[:tokens])[0]).astype(bf16)
    sums = summed[tokens : tokens + vector_rows, :local_width]
    for bit in range(cycle.bit_length() - 1):
        sums = sums + swapped(sums, bit)

    cut = both.shape[0] - quarter
    out_grad = summed_over_chips(both[cut:], [bit for bit in chip_bits if bit != OUT_BIT])
    out_grad = jnp.concatenate(joined(out_grad, OUT_BIT, out_side))
    out_grad = jnp.concatenate(pair_joined(out_grad, odd))
    rest = summed_over_chips(both[:cut], [bit for bit in chip_bits if bit != FC_BIT])
    first, second = joined(rest, FC_BIT, fc_side)
    proj_grad = jnp.concatenate([first[local_width:], second[local_width:]])
    proj_grad = jnp.concatenate(pair_joined(proj_grad, odd))
    fc_grad = jnp.concatenate([first[:local_width], second[:local_width]], axis=1)
    fc_halves = pair_joined(fc_grad, odd)
    fc_grad = jnp.concatenate(
        [
            fc_halves[h][:, z * half_hidden : (z + 1) * half_hidden]
            for z in range(shards)
            for h in range(2)
        ],
        axis=1,
    )

    grad = []
    for s in range(seqs):
        normed = after(normed_one[s], normed_parts)
        low = jnp.concatenate([query_low[s], kv_low[s]], axis=1)
        grad.append(dot(normed, low, flat))
    grad = sum(grad).astype(bf16).reshape(shards, 2, half_width, -1)
    mine, sent = parted(grad[:, 0], grad[:, 1], odd)
    grad = lax.all_to_all(added(mine, swapped(sent, 0)), "shard", 0, 0, tiled=True)
    grad = jnp.concatenate([grad[z] for z in range(shards)], axis=1)
    grad = jnp.concatenate(pair_joined(summed_over_chips(grad, chip_bits), odd))
    thirds = [
        jnp.concatenate(
            [
                grad[:, (3 * z + third) * group : (3 * z + third + 1) * group]
                for z in range(shards)
            ],
            axis=1,
        )[:, :width]
        for third in range(3)
    ]
    qkv_grad = jnp.concatenate(thirds, axis=1)

    return (
        layer_output.reshape(seqs, piece, width),
        input_grad.reshape(seqs, piece, width),
        sums[0],
        sums[1],
        qkv_grad,
        sums[2],
        sums[3],
        proj_grad,
        sums[4],
        sums[5],
        sums[6],
        fc_grad,
        sums[8:].reshape(-1),
        out_grad,
        sums[7],
    )


def solution(mesh):
    tokens = P(None, ("ctx", "shard"), None)
    vector = P("shard")
    matrix = P("shard", None)
    return jax.shard_map(
        body,
        mesh=mesh,
        in_specs=(
            tokens,
            vector,
            vector,
            matrix,
            vector,
            vector,
            matrix,
            vector,
            vector,
            vector,
            matrix,
            vector,
            matrix,
            vector,
            tokens,
        ),
        out_specs=(
            tokens,
            tokens,
            vector,
            vector,
            matrix,
            vector,
            vector,
            matrix,
            vector,
            vector,
            vector,
            matrix,
            vector,
            matrix,
            vector,
        ),
        check_vma=False,
    )
```

profile of v0, /device:TPU:0, one launch (start us, length us, event | category | flops | bytes accessed | tf_op | source)
XLA Modules:
  0.0 485.5 jit_solution(5596633810509637562)
XLA Ops:
  16.7 6.3 %all-to-all-start = ((bf16[4,112,576]{2,1,0:T(8,128)(2,1)}), bf16[4,112,576]{2,1,0:T(8,128)(2,1)S(1)}, u32[]{:S(2)}, u32[]{:S(2)}) async-start(bf16[4,112,576]{2,1,0:T(8,128)(2,1)} %pad_maximum_fusion.18), calls=%async_computation | async-start | bytes 1146880 | tf_op jit(solution)/shard_map/all_to_all | solution.py:407
  24.1 30.3 %all-to-all-done = bf16[4,112,576]{2,1,0:T(8,128)(2,1)S(1)} async-done(((bf16[4,112,576]{2,1,0:T(8,128)(2,1)}), bf16[4,112,576]{2,1,0:T(8,128)(2,1)S(1)}, u32[]{:S(2)}, u32[]{:S(2)}) %all-to-all-start) | async-done | bytes 516128 | tf_op jit(solution)/shard_map/all_to_all | solution.py:407
  56.8 5.0 %all-gather.7.cloned.1.call-done = bf16[8,128,768]{2,1,0:T(8,128)(2,1)} async-done(((bf16[2,128,768]{2,1,0:T(8,128)(2,1)}), bf16[8,128,768]{2,1,0:T(8,128)(2,1)}) %all-gather.7.cloned.1.call-update) | async-done | bytes 1572880 | tf_op jit(solution)/shard_map/all_gather | solution.py:382
  84.3 12.9 %collective-permute-done.7.refs_1_ = bf16[2,512,384]{2,1,0:T(8,128)(2,1)} collective-permute-done((bf16[2,512,384]{2,1,0:T(8,128)(2,1)}, bf16[2,512,384]{2,1,0:T(8,128)(2,1)}, u32[]{:S(2)}, u32[]{:S(2)}) %collective-permute-start.7) | collective-permute-done | bytes 786464 | tf_op jit(solution)/shard_map/ppermute | solution.py:62
  99.5 6.6 %collective-permute-done.5.q_ref = bf16[512,192]{1,0:T(8,128)(2,1)S(1)} collective-permute-done((bf16[512,192]{1,0:T(8,128)(2,1)S(1)}, bf16[512,192]{1,0:T(8,128)(2,1)S(1)}, u32[]{:S(2)}, u32[]{:S(2)}) %collective-permute-start.5) | collective-permute-done | bytes 196640 | tf_op jit(solution)/shard_map/ppermute | solution.py:91
  109.5 25.2 %all-gather.9.cloned.1.call-done = bf16[1152,768]{1,0:T(8,128)(2,1)} async-done(((bf16[288,768]{1,0:T(8,128)(2,1)}), bf16[1152,768]{1,0:T(8,128)(2,1)}) %all-gather.9.cloned.1.call-update) | async-done | bytes 1769488 | tf_op jit(solution)/shard_map/all_gather | solution.py:450
  138.7 16.9 %attention_forward.3 = (bf16[4,192,128]{2,1,0:T(8,128)(2,1)}, f32[192,512]{1,0:T(8,128)}, f32[3,1,512]{2,1,0:T(1,128)}) custom-call(s32[2]{0:T(128)} %pad_add_fusion.1.info, bf16[512,192]{1,0:T(8,128)(2,1)} %copy-done.54, bf16[2,512,384]{2,1,0:T(8,128)(2,1)} %pad_maximum_fusion.14.refs_0_, bf16[2,512,384]{2,1,0:T(8,128)(2,1)} %collective-permute-done.7.refs_1_, ...), custom_call_target="tpu_custom_call" | custom-call | flops 3623878656 | bytes 3932160 | tf_op jit(solution)/shard_map/attention_forward/pallas_call | solution.py:289
  155.8 5.2 %attention_forward.2 = (bf16[4,192,128]{2,1,0:T(8,128)(2,1)}, f32[192,512]{1,0:T(8,128)}, f32[3,1,512]{2,1,0:T(1,128)}) custom-call(s32[2]{0:T(128)} %pad_add_fusion.info, bf16[512,192]{1,0:T(8,128)(2,1)} %fusion.16.q_ref, bf16[2,512,384]{2,1,0:T(8,128)(2,1)} %pad_maximum_fusion.13.refs_0_, bf16[2,512,384]{2,1,0:T(8,128)(2,1)} %collective-permute-done.2.refs_1_, ...), custom_call_target="tpu_custom_call" | custom-call | flops 3623878656 | bytes 3932160 | tf_op jit(solution)/shard_map/attention_forward/pallas_call | solution.py:289
  161.0 23.1 %collective-permute-done.10 = bf16[4,192,128]{2,1,0:T(8,128)(2,1)S(1)} collective-permute-done((bf16[4,192,128]{2,1,0:T(8,128)(2,1)}, bf16[4,192,128]{2,1,0:T(8,128)(2,1)S(1)}, u32[]{:S(2)}, u32[]{:S(2)}) %collective-permute-start.10) | collective-permute-done | bytes 196640 | tf_op jit(solution)/shard_map/ppermute | solution.py:91
  195.6 4.3 all-to-all-done.1
  208.3 5.0 %convert_reduce_fusion = (bf16[1536]{0:T(1024)(128)(2,1)}, bf16[512,1536]{1,0:T(8,128)(2,1)S(1)}) fusion(f32[512,1536]{1,0:T(8,128)S(1)} %convolution_add_fusion, bf16[1536,768]{1,0:T(8,128)(2,1)S(1)} %bitcast.275, bf16[256,768]{1,0:T(8,128)(2,1)} %collective-permute-done.16, bf16[256,768]{1,0:T(8,128)(2,1)S(1)} %bitcast.268), kind=kOutput, calls=%fused_computation.34 | convolution fusion | flops 1226832384 | bytes 7867392 | tf_op jit(solution)/shard_map/dot_general | solution.py:100
  236.6 9.3 %all-to-all-done.2.go_ref = bf16[4,192,256]{2,1,0:T(8,128)(2,1)} async-done(((bf16[4,192,256]{2,1,0:T(8,128)(2,1)}), bf16[4,192,256]{2,1,0:T(8,128)(2,1)}, u32[]{:S(2)}, u32[]{:S(2)}) %all-to-all-start.2) | async-done | bytes 393248 | tf_op jit(solution)/shard_map/all_to_all | solution.py:513
  249.1 7.8 %attention_backward.2 = (bf16[512,192]{1,0:T(8,128)(2,1)}, bf16[2,512,384]{2,1,0:T(8,128)(2,1)}, bf16[2,512,384]{2,1,0:T(8,128)(2,1)}, bf16[4,512,384]{2,1,0:T(8,128)(2,1)}) custom-call(s32[2]{0:T(128)} %pad_add_fusion.info, bf16[512,192]{1,0:T(8,128)(2,1)} %fusion.16.q_ref, f32[192,512]{1,0:T(8,128)} %get-tuple-element.40.out_ref, ...), custom_call_target="tpu_custom_call" | custom-call | flops 9059696640 | bytes 7864320 | tf_op jit(solution)/shard_map/attention_backward/pallas_call | solution.py:321
  261.1 22.5 %attention_backward.3 = (bf16[512,192]{1,0:T(8,128)(2,1)}, bf16[2,512,384]{2,1,0:T(8,128)(2,1)}, bf16[2,512,384]{2,1,0:T(8,128)(2,1)}, bf16[4,512,384]{2,1,0:T(8,128)(2,1)}) custom-call(s32[2]{0:T(128)} %pad_add_fusion.1.info, bf16[512,192]{1,0:T(8,128)(2,1)} %copy-done.54, f32[192,512]{1,0:T(8,128)} %get-tuple-element.47.out_ref, ...), custom_call_target="tpu_custom_call" | custom-call | flops 9059696640 | bytes 7864320 | tf_op jit(solution)/shard_map/attention_backward/pallas_call | solution.py:321
  287.8 4.2 collective-permute-start.23
  299.2 14.5 %collective-permute-done.20 = bf16[2,512,384]{2,1,0:T(8,128)(2,1)} collective-permute-done((bf16[2,512,384]{2,1,0:T(8,128)(2,1)}, bf16[2,512,384]{2,1,0:T(8,128)(2,1)}, u32[]{:S(2)}, u32[]{:S(2)}) %collective-permute-start.20) | collective-permute-done | bytes 786464 | tf_op jit(solution)/shard_map/ppermute | solution.py:77
  322.2 7.2 %collective-permute-done.21 = bf16[1,512,384]{2,1,0:T(8,128)(2,1)} collective-permute-done((bf16[1,512,384]{2,1,0:T(8,128)(2,1)}, bf16[1,512,384]{2,1,0:T(8,128)(2,1)}, u32[]{:S(2)}, u32[]{:S(2)}) %collective-permute-start.21) | collective-permute-done | bytes 393248 | tf_op jit(solution)/shard_map/ppermute | solution.py:81
  342.9 22.9 %collective-permute-done.35 = bf16[4,192,768]{2,1,0:T(8,128)(2,1)} collective-permute-done((bf16[4,192,768]{2,1,0:T(8,128)(2,1)}, bf16[4,192,768]{2,1,0:T(8,128)(2,1)}, u32[]{:S(2)}, u32[]{:S(2)}) %collective-permute-start.35) | collective-permute-done | bytes 1179680 | tf_op jit(solution)/shard_map/ppermute | solution.py:37
  377.6 5.7 %all-to-all-done.3 = bf16[4,96,576]{2,1,0:T(8,128)(2,1)} async-done(((bf16[4,96,576]{2,1,0:T(8,128)(2,1)}), bf16[4,96,576]{2,1,0:T(8,128)(2,1)}, u32[]{:S(2)}, u32[]{:S(2)}) %all-to-all-start.3) | async-done | bytes 442400 | tf_op jit(solution)/shard_map/all_to_all | solution.py:634
  386.3 8.5 %collective-permute-done.31 = bf16[96,2304]{1,0:T(8,128)(2,1)S(1)} collective-permute-done((bf16[96,2304]{1,0:T(8,128)(2,1)S(1)}, bf16[96,2304]{1,0:T(8,128)(2,1)S(1)}, u32[]{:S(2)}, u32[]{:S(2)}) %collective-permute-start.31) | collective-permute-done | bytes 442400 | tf_op jit(solution)/shard_map/ppermute | solution.py:37
  397.5 8.4 %collective-permute-done.32 = bf16[96,2304]{1,0:T(8,128)(2,1)S(1)} collective-permute-done((bf16[96,2304]{1,0:T(8,128)(2,1)S(1)}, bf16[96,2304]{1,0:T(8,128)(2,1)S(1)}, u32[]{:S(2)}, u32[]{:S(2)}) %collective-permute-start.32) | collective-permute-done | bytes 442400 | tf_op jit(solution)/shard_map/ppermute | solution.py:37
  412.3 18.1 %reduce-scatter.5.cloned.1.call-done = bf16[1,432,768]{2,1,0:T(8,128)(2,1)} async-done(((bf16[4,432,768]{2,1,0:T(8,128)(2,1)}), bf16[1,432,768]{2,1,0:T(8,128)(2,1)}) %reduce-scatter.5.cloned.1.call-update) | async-done | bytes 663568 | tf_op jit(solution)/shard_map/reduce_scatter | solution.py:555
  435.9 4.2 collective-permute-done.40
  447.9 13.5 %collective-permute-done.28 = f32[12,192]{1,0:T(8,128)S(1)} collective-permute-done((f32[12,192]{1,0:T(8,128)S(1)}, f32[12,192]{1,0:T(8,128)S(1)}, u32[]{:S(2)}, u32[]{:S(2)}) %collective-permute-start.28) | collective-permute-done | bytes 9248 | tf_op jit(solution)/shard_map/ppermute | solution.py:37
  (394 shorter events, 182.3 us)
Async XLA Ops:
  7.2 54.5 %all-gather.7.cloned.1.call-start = ((), (), s32[]{:S(2)}) async-start(), calls=%async_computation.8 | async-start | bytes 1966080 | tf_op jit(solution)/shard_map/all_gather | solution.py:382
  7.9 91.6 %all-gather.11.cloned.1.call-start = ((), (), s32[]{:S(2)}) async-start(), calls=%async_computation.10 | async-start | bytes 1474560 | tf_op jit(solution)/shard_map/all_gather | solution.py:455
  16.7 37.7 %all-to-all-start = ((bf16[4,112,576]{2,1,0:T(8,128)(2,1)}), bf16[4,112,576]{2,1,0:T(8,128)(2,1)S(1)}, u32[]{:S(2)}, u32[]{:S(2)}) async-start(bf16[4,112,576]{2,1,0:T(8,128)(2,1)} %pad_maximum_fusion.18), calls=%async_computation | async-start | bytes 1146880 | tf_op jit(solution)/shard_map/all_to_all | solution.py:407
  23.0 111.7 %all-gather.9.cloned.1.call-start = ((), (), s32[]{:S(2)}) async-start(), calls=%async_computation.9 | async-start | bytes 2211840 | tf_op jit(solution)/shard_map/all_gather | solution.py:450
  77.5 19.8 %collective-permute-start.7 = (bf16[2,512,384]{2,1,0:T(8,128)(2,1)}, bf16[2,512,384]{2,1,0:T(8,128)(2,1)}, u32[]{:S(2)}, u32[]{:S(2)}) collective-permute-start(bf16[2,512,384]{2,1,0:T(8,128)(2,1)} %pad_maximum_fusion.14.refs_0_), channel_id=1, source_target_pairs={{0,8},{4,12},{8,0},{12,4},{16,24},{20,28},{24,16},{28,20},{1,9},{5... | collective-permute-start | bytes 2359304 | tf_op jit(solution)/shard_map/ppermute | solution.py:62
  84.3 53.8 %collective-permute-start.8 = (bf16[2,512,384]{2,1,0:T(8,128)(2,1)}, bf16[2,512,384]{2,1,0:T(8,128)(2,1)}, u32[]{:S(2)}, u32[]{:S(2)}) collective-permute-start(bf16[2,512,384]{2,1,0:T(8,128)(2,1)} %pad_maximum_fusion.14.refs_0_), channel_id=1, source_target_pairs={{0,4},{4,0},{8,12},{12,8},{16,20},{20,16},{24,28},{28,24},{1,5},{5... | collective-permute-start | bytes 2359304 | tf_op jit(solution)/shard_map/ppermute | solution.py:37
  97.2 40.9 %collective-permute-start.9 = (bf16[2,512,384]{2,1,0:T(8,128)(2,1)}, bf16[2,512,384]{2,1,0:T(8,128)(2,1)}, u32[]{:S(2)}, u32[]{:S(2)}) collective-permute-start(bf16[2,512,384]{2,1,0:T(8,128)(2,1)} %collective-permute-done.7.refs_1_), channel_id=1, source_target_pairs={{0,4},{4,0},{8,12},{12,8},{16,20},{20,16},{24,28},{28,24},{1,5},{5... | collective-permute-start | bytes 2359304 | tf_op jit(solution)/shard_map/ppermute | solution.py:37
  98.8 56.7 %collective-permute-start.3 = (bf16[2,512,384]{2,1,0:T(8,128)(2,1)}, bf16[2,512,384]{2,1,0:T(8,128)(2,1)}, u32[]{:S(2)}, u32[]{:S(2)}) collective-permute-start(bf16[2,512,384]{2,1,0:T(8,128)(2,1)} %pad_maximum_fusion.13.refs_0_), channel_id=1, source_target_pairs={{0,4},{4,0},{8,12},{12,8},{16,20},{20,16},{24,28},{28,24},{1,5},{5... | collective-permute-start | bytes 2359304 | tf_op jit(solution)/shard_map/ppermute | solution.py:37
  99.5 56.1 %collective-permute-start.4 = (bf16[2,512,384]{2,1,0:T(8,128)(2,1)}, bf16[2,512,384]{2,1,0:T(8,128)(2,1)}, u32[]{:S(2)}, u32[]{:S(2)}) collective-permute-start(bf16[2,512,384]{2,1,0:T(8,128)(2,1)} %collective-permute-done.2.refs_1_), channel_id=1, source_target_pairs={{0,4},{4,0},{8,12},{12,8},{16,20},{20,16},{24,28},{28,24},{1,5},{5... | collective-permute-start | bytes 2359304 | tf_op jit(solution)/shard_map/ppermute | solution.py:37
  106.1 83.8 %collective-permute-start.14 = (bf16[4,192,768]{2,1,0:T(8,128)(2,1)}, bf16[4,192,768]{2,1,0:T(8,128)(2,1)}, u32[]{:S(2)}, u32[]{:S(2)}) collective-permute-start(bf16[4,192,768]{2,1,0:T(8,128)(2,1)} %bitcast.276), channel_id=1, source_target_pairs={{0,16},{4,20},{8,24},{12,28},{16,0},{20,4},{24,8},{28,12},{1,17},{... | collective-permute-start | bytes 3538952 | tf_op jit(solution)/shard_map/ppermute | solution.py:37
  138.1 70.2 %collective-permute-start.16 = (bf16[256,768]{1,0:T(8,128)(2,1)S(1)}, bf16[256,768]{1,0:T(8,128)(2,1)}, u32[]{:S(2)}, u32[]{:S(2)}) collective-permute-start(bf16[256,768]{1,0:T(8,128)(2,1)S(1)} %bitcast.267), channel_id=1, source_target_pairs={{0,4},{4,0},{8,12},{12,8},{16,20},{20,16},{24,28},{28,24},{1,5},{5... | collective-permute-start | bytes 1179656 | tf_op jit(solution)/shard_map/ppermute | solution.py:37
  138.2 54.9 %collective-permute-start.11 = (bf16[4,96,768]{2,1,0:T(8,128)(2,1)}, bf16[4,96,768]{2,1,0:T(8,128)(2,1)}, u32[]{:S(2)}, u32[]{:S(2)}) collective-permute-start(bf16[4,96,768]{2,1,0:T(8,128)(2,1)} %slice.417), channel_id=1, source_target_pairs={{0,4},{4,0},{8,12},{12,8},{16,20},{20,16},{24,28},{28,24},{1,5},{5... | collective-permute-start | bytes 1769480 | tf_op jit(solution)/shard_map/ppermute | solution.py:37
  155.6 47.9 %collective-permute-start.13 = (bf16[768,768]{1,0:T(8,128)(2,1)S(1)}, bf16[768,768]{1,0:T(8,128)(2,1)}, u32[]{:S(2)}, u32[]{:S(2)}) collective-permute-start(bf16[768,768]{1,0:T(8,128)(2,1)S(1)} %bitcast.264), channel_id=1, source_target_pairs={{0,8},{4,12},{8,0},{12,4},{16,24},{20,28},{24,16},{28,20},{1,9},{5... | collective-permute-start | bytes 3538952 | tf_op jit(solution)/shard_map/ppermute | solution.py:37
  155.7 28.4 %collective-permute-start.10 = (bf16[4,192,128]{2,1,0:T(8,128)(2,1)}, bf16[4,192,128]{2,1,0:T(8,128)(2,1)S(1)}, u32[]{:S(2)}, u32[]{:S(2)}) collective-permute-start(bf16[4,192,128]{2,1,0:T(8,128)(2,1)} %get-tuple-element.39), channel_id=1, source_target_pairs={{0,28},{4,24},{8,20},{12,16},{16,12},{20,8},{24,4},{28,0},{1,29},{... | collective-permute-start | bytes 589832 | tf_op jit(solution)/shard_map/ppermute | solution.py:91
  233.2 177.5 %reduce-scatter.3.cloned.1.call-start = ((), (), s32[]{:S(2)}) async-start(), calls=%async_computation.6 | async-start | bytes 2088960 | tf_op jit(solution)/shard_map/reduce_scatter | solution.py:601
  256.9 26.7 %collective-permute-start.19 = (bf16[4,512,384]{2,1,0:T(8,128)(2,1)}, bf16[4,512,384]{2,1,0:T(8,128)(2,1)S(1)}, u32[]{:S(2)}, u32[]{:S(2)}) collective-permute-start(bf16[4,512,384]{2,1,0:T(8,128)(2,1)} %get-tuple-element.45), channel_id=1, source_target_pairs={{0,4},{4,0},{8,12},{12,8},{16,20},{20,16},{24,28},{28,24},{1,5},{5... | collective-permute-start | bytes 4718600 | tf_op jit(solution)/shard_map/ppermute | solution.py:37
  285.9 27.9 %collective-permute-start.20 = (bf16[2,512,384]{2,1,0:T(8,128)(2,1)}, bf16[2,512,384]{2,1,0:T(8,128)(2,1)}, u32[]{:S(2)}, u32[]{:S(2)}) collective-permute-start(bf16[2,512,384]{2,1,0:T(8,128)(2,1)} %add_convert_fusion.6), channel_id=1, source_target_pairs={{16,0},{20,4},{24,8},{28,12},{17,1},{21,5},{25,9},{29,13},{18,2},{... | collective-permute-start | bytes 2359304 | tf_op jit(solution)/shard_map/ppermute | solution.py:77
  294.5 25.7 %collective-permute-start.25 = (bf16[2,512,384]{2,1,0:T(8,128)(2,1)}, bf16[2,512,384]{2,1,0:T(8,128)(2,1)}, u32[]{:S(2)}, u32[]{:S(2)}) collective-permute-start(bf16[2,512,384]{2,1,0:T(8,128)(2,1)} %add_convert_fusion.3), channel_id=1, source_target_pairs={{8,0},{12,4},{0,8},{4,12},{24,16},{28,20},{16,24},{20,28},{9,1},{1... | collective-permute-start | bytes 2359304 | tf_op jit(solution)/shard_map/ppermute | solution.py:77
  339.1 26.8 %collective-permute-start.35 = (bf16[4,192,768]{2,1,0:T(8,128)(2,1)}, bf16[4,192,768]{2,1,0:T(8,128)(2,1)}, u32[]{:S(2)}, u32[]{:S(2)}) collective-permute-start(bf16[4,192,768]{2,1,0:T(8,128)(2,1)} %select_bitcast_fusion), channel_id=1, source_target_pairs={{0,16},{4,20},{8,24},{12,28},{16,0},{20,4},{24,8},{28,12},{1,17},{... | collective-permute-start | bytes 3538952 | tf_op jit(solution)/shard_map/ppermute | solution.py:37
  339.5 34.4 %collective-permute-start.34 = (bf16[4,240,768]{2,1,0:T(8,128)(2,1)}, bf16[4,240,768]{2,1,0:T(8,128)(2,1)}, u32[]{:S(2)}, u32[]{:S(2)}) collective-permute-start(bf16[4,240,768]{2,1,0:T(8,128)(2,1)} %broadcast_select_fusion), channel_id=1, source_target_pairs={{0,8},{4,12},{8,0},{12,4},{16,24},{20,28},{24,16},{28,20},{1,9},{5... | collective-permute-start | bytes 4423688 | tf_op jit(solution)/shard_map/ppermute | solution.py:37
  342.8 23.0 %collective-permute-start.30 = (bf16[4,96,576]{2,1,0:T(8,128)(2,1)S(1)}, bf16[4,96,576]{2,1,0:T(8,128)(2,1)S(1)}, u32[]{:S(2)}, u32[]{:S(2)}) collective-permute-start(bf16[4,96,576]{2,1,0:T(8,128)(2,1)S(1)} %fusion.33), channel_id=1, source_target_pairs={{0,4},{4,0},{8,12},{12,8},{16,20},{20,16},{24,28},{28,24},{1,5},{5... | collective-permute-start | bytes 1327112 | tf_op jit(solution)/shard_map/ppermute | solution.py:37
  371.0 59.4 %reduce-scatter.5.cloned.1.call-start = ((), (), s32[]{:S(2)}) async-start(), calls=%async_computation.7 | async-start | bytes 3317760 | tf_op jit(solution)/shard_map/reduce_scatter | solution.py:555
  411.8 34.2 %collective-permute-start.27 = (f32[12,192]{1,0:T(8,128)S(1)}, f32[12,192]{1,0:T(8,128)S(1)}, u32[]{:S(2)}, u32[]{:S(2)}) collective-permute-start(f32[12,192]{1,0:T(8,128)S(1)} %slice.447), channel_id=1, source_target_pairs={{0,4},{4,0},{8,12},{12,8},{16,20},{20,16},{24,28},{28,24},{1,5},{5... | collective-permute-start | bytes 27656 | tf_op jit(solution)/shard_map/ppermute | solution.py:37
  440.2 22.6 %collective-permute-start.41 = (f32[192,768]{1,0:T(8,128)S(1)}, f32[192,768]{1,0:T(8,128)S(1)}, u32[]{:S(2)}, u32[]{:S(2)}) collective-permute-start(f32[192,768]{1,0:T(8,128)S(1)} %convert_add_fusion.5), channel_id=1, source_target_pairs={{0,16},{4,20},{8,24},{12,28},{16,0},{20,4},{24,8},{28,12},{1,17},{... | collective-permute-start | bytes 1769480 | tf_op jit(solution)/shard_map/ppermute | solution.py:37
  (84 other events, 530.6 us)
Sparse Core Ops, SparseCore 0:
  9.6 52.0 all-gather.6
  63.9 29.2 all-gather.10
  95.3 39.4 all-gather.8
  339.2 34.4 reduce-scatter.2
  377.7 52.7 reduce-scatter.4
where the time goes:
time: 495 us; the launch traced here: 485 us
  waiting for transfers between devices  238 us (48%)
  starting transfers between devices  61.7 us (12%)
  other arithmetic  58.6 us (12%)
  Pallas kernels  52.3 us (11%)
  local copies, waits for them, and re-layouts  32.5 us (7%)
  matrix products  27.3 us (6%)
  between operations  15.3 us (3%)
    ppermute x31, waiting for transfers between devices, swapped(): return lax.ppermute(block, 'ctx', [(i, i ^ 1 << bit) for i in range(n)])  63.9 us
    ppermute x4, waiting for transfers between devices, mirrored(): return lax.ppermute(block, 'ctx', [(i, n - 1 - i) for i in range(n)])  33.2 us
    all_to_all x1, waiting for transfers between devices, body(): lax.all_to_all(jnp.concatenate([by_heads(weight_half), jnp.broadcast_to(p...  30.3 us
    pallas_call x2, Pallas kernels, attend_back(): pl.pallas_call(functools.partial(backward_kernel, heads, shards, order, f...  30.2 us
    dot_general x19, matrix products, dot(): lax.dot_general(a, b, ((contract[0], contract[1]), ((), ())), preferred_e...  27.3 us
    all_gather x1, waiting for transfers between devices, body(): lax.all_gather(jnp.concatenate([proj_half, fc_quarter]), 'shard', axis=0)  25.2 us
    pallas_call x2, Pallas kernels, attend(): pl.pallas_call(functools.partial(forward_kernel, heads, shards, order), o...  22.1 us
    ppermute x31, starting transfers between devices, swapped(): return lax.ppermute(block, 'ctx', [(i, i ^ 1 << bit) for i in range(n)])  20.3 us
  transfers between devices with their start and end apart: 52, of which 25 were waited for; matrix products, arithmetic and copies ran while one was open for 19% of the time, Pallas kernels for 11%

commit v1 on v0

--- a/solution.py
+++ b/solution.py
@@ -393,7 +393,11 @@
             ]
         )
 
-    weight_half = lax.dynamic_slice_in_dim(qkv_weight, odd * half_width, half_width, 0)
+    joins = chip_bits[::-1] + [0]
+    share = local_width // cycle
+    weight_share = lax.dynamic_slice_in_dim(
+        qkv_weight, sum(((here >> bit) & 1) << k for k, bit in enumerate(joins)) * share, share, 0
+    )
     packed = jnp.concatenate(
         [
             jnp.stack(
@@ -406,15 +410,18 @@
     packed = jnp.pad(packed, ((0, 16 - vector_rows), (0, 3 * group - local_width)))
     moved = lax.all_to_all(
         jnp.concatenate(
-            [by_heads(weight_half), jnp.broadcast_to(packed, (shards,) + packed.shape)], axis=1
+            [by_heads(weight_share), jnp.broadcast_to(packed, (shards,) + packed.shape)], axis=1
         ),
         "shard",
         0,
         0,
         tiled=True,
     )
-    small = moved[:, half_width : half_width + vector_rows, :local_width].astype(f32)
-    qkv_own = jnp.stack(pair_joined(moved[:, :half_width], odd), axis=1).reshape(width, 3 * group)
+    small = moved[:, share : share + vector_rows, :local_width].astype(f32)
+    qkv_own = moved[:, :share]
+    for bit in joins:
+        qkv_own = jnp.concatenate(joined(qkv_own, bit, (here >> bit) & 1), axis=1)
+    qkv_own = qkv_own.reshape(width, 3 * group)
     q_weight = qkv_own[:, :group]
     kv_weight = qkv_own[:, group:]
 
@@ -452,14 +459,11 @@
     proj_full = jnp.stack(proj_half, axis=1).reshape(width, width)
     fc_quarter = moved[:, half_width:].reshape(width, -1)
     fc_half = jnp.concatenate(joined(fc_quarter, FC_BIT, fc_side), axis=1)
-    out_quarter = lax.all_gather(
-        lax.dynamic_slice_in_dim(
-            out_weight, odd * half_hidden + out_side * quarter, quarter, 0
-        ),
-        "shard",
-        axis=0,
-    )
-    out_half = jnp.stack(joined(out_quarter, OUT_BIT, out_side), axis=1).reshape(-1, width)
+    out_quarter = lax.dynamic_slice_in_dim(
+        out_weight, odd * half_hidden + out_side * quarter, quarter, 0
+    )
+    out_quarter = lax.all_gather(after(out_quarter, gathered), "shard", axis=0)
+
     orders = [chip_bits + [0], chip_bits[::-1] + [0]]
     orders = [orders[s % 2] for s in range(seqs)]
     group_norms, normed_one, own_blocks, queries, infos = [], [], [], [], []
@@ -480,9 +484,10 @@
     for s in reversed(range(seqs)):
         att, *saved[s] = attend(shards, orders[s], infos[s], queries[s], blocks[s])
         attended_parts[s] = mirrored(att) if late[s] else att
-    attended = lax.all_to_all(
-        jnp.concatenate(attended_parts, axis=2), "shard", 0, 0, tiled=True
-    ).reshape(padded, tokens)[:width]
+    attended = after(jnp.concatenate(attended_parts, axis=2), fc_half)
+    attended = lax.all_to_all(attended, "shard", 0, 0, tiled=True).reshape(padded, tokens)[:width]
+    out_quarter = after(out_quarter, *attended_parts)
+    out_half = jnp.stack(joined(out_quarter, OUT_BIT, out_side), axis=1).reshape(-1, width)
 
     inputs32 = layer_input.reshape(tokens, width).astype(f32)
     grads_own = grad_output.reshape(tokens, width)
@@ -534,7 +539,8 @@
 
     query_low = [None] * seqs
     kv_parts = [None] * seqs
-    grad_heads = after(grad_heads, fc_sent, out_sent)
+    scattered = jnp.concatenate([added(fc_mine, fc_received), added(out_mine, out_received)], axis=1)
+    grad_heads = after(grad_heads, scattered)
     for s in range(seqs):
         heads_grad, first = grad_heads, s * piece
         if late[s]:
@@ -544,14 +550,6 @@
         )
         query_low[s] = mirrored(low) if late[s] else low
 
-    ended = [part for parts in kv_parts for part in parts[:1]]
-    scattered = jnp.concatenate(
-        [
-            added(fc_mine, after(fc_received, *ended)),
-            added(out_mine, after(out_received, *ended)),
-        ],
-        axis=1,
-    )
     both = lax.psum_scatter(scattered, "shard", scatter_dimension=0, tiled=False)
 
     kv_low = [None] * seqs
@@ -607,12 +605,12 @@
 
     cut = both.shape[0] - quarter
     out_grad = summed_over_chips(both[cut:], [bit for bit in chip_bits if bit != OUT_BIT])
-    out_grad = jnp.concatenate(joined(out_grad, OUT_BIT, out_side))
-    out_grad = jnp.concatenate(pair_joined(out_grad, odd))
+    out_grad = jnp.concatenate(joined(out_grad.astype(bf16), OUT_BIT, out_side))
+    out_grad = jnp.concatenate(pair_joined(out_grad, odd)).astype(f32)
     rest = summed_over_chips(both[:cut], [bit for bit in chip_bits if bit != FC_BIT])
-    first, second = joined(rest, FC_BIT, fc_side)
+    first, second = joined(rest.astype(bf16), FC_BIT, fc_side)
     proj_grad = jnp.concatenate([first[local_width:], second[local_width:]])
-    proj_grad = jnp.concatenate(pair_joined(proj_grad, odd))
+    proj_grad = jnp.concatenate(pair_joined(proj_grad, odd)).astype(f32)
     fc_grad = jnp.concatenate([first[:local_width], second[:local_width]], axis=1)
     fc_halves = pair_joined(fc_grad, odd)
     fc_grad = jnp.concatenate(
@@ -622,7 +620,7 @@
             for h in range(2)
         ],
         axis=1,
-    )
+    ).astype(f32)
 
     grad = []
     for s in range(seqs):

time: 495 us -> 473 us (0.956)
  waiting for transfers between devices: 238 us -> 169 us
  blocking collectives: 0 us -> 37.7 us
  local copies, waits for them, and re-layouts: 32.5 us -> 44 us
    all_to_all x3 -> x1, waiting for transfers between devices: 40.4 us -> 0.01 us  [body(): lax.all_to_all(attended, 'shard', 0, 0, tiled=True).reshape(padded, tokens)]
    all_to_all x0 -> x2, blocking collectives: none -> 37.7 us  [the longest x1 20.1 us: body(): lax.all_to_all(jnp.concatenate([by_heads(weight_share), jnp.broadcast_to(...]
    ppermute x31 -> x33, waiting for transfers between devices: 63.9 us -> 90.8 us  [swapped(): return lax.ppermute(block, 'ctx', [(i, i ^ 1 << bit) for i in range(n)])]
    ppermute x4, waiting for transfers between devices: 33.2 us -> 6.73 us  [mirrored(): return lax.ppermute(block, 'ctx', [(i, n - 1 - i) for i in range(n)])]
    all_gather x1, waiting for transfers between devices: 25.2 us -> 0.01 us  [body(): lax.all_gather(jnp.concatenate([proj_half, fc_quarter]), 'shard', axis=0)]
    all_gather x1, waiting for transfers between devices: 0.01 us -> 24.7 us  [body(): out_quarter = lax.all_gather(after(out_quarter, gathered), 'shard', axis=0)]
    reduce_scatter x1, waiting for transfers between devices: 18.1 us -> 0.01 us  [body(): lax.psum_scatter(scattered, 'shard', scatter_dimension=0, tiled=False)]
    all_gather x1, starting transfers between devices: 0.04 us -> 11.9 us  [body(): out_quarter = lax.all_gather(after(out_quarter, gathered), 'shard', axis=0)]
  transfers between devices with their start and end apart: 52 -> 52, of which waited for: 25 -> 26; matrix products, arithmetic and copies ran while one was open for 19% -> 24% of each run, Pallas kernels for 11% -> 11%
where the time goes in v1:
time: 473 us; the launch traced here: 467 us
  waiting for transfers between devices  169 us (36%)
  starting transfers between devices  60.8 us (13%)
  other arithmetic  56.4 us (12%)
  Pallas kernels  52.6 us (11%)
  local copies, waits for them, and re-layouts  44 us (9%)
  blocking collectives  37.7 us (8%)
  matrix products  31.2 us (7%)
  between operations  15.2 us (3%)
    ppermute x33, waiting for transfers between devices, swapped(): return lax.ppermute(block, 'ctx', [(i, i ^ 1 << bit) for i in range(n)])  90.8 us
    dot_general x19, matrix products, dot(): lax.dot_general(a, b, ((contract[0], contract[1]), ((), ())), preferred_e...  31.2 us
    pallas_call x2, Pallas kernels, attend_back(): pl.pallas_call(functools.partial(backward_kernel, heads, shards, order, f...  30.6 us
    all_gather x1, waiting for transfers between devices, body(): out_quarter = lax.all_gather(after(out_quarter, gathered), 'shard', axis=0)  24.7 us
    pallas_call x2, Pallas kernels, attend(): pl.pallas_call(functools.partial(forward_kernel, heads, shards, order), o...  22 us
    all_to_all x1, blocking collectives, body(): lax.all_to_all(jnp.concatenate([by_heads(weight_share), jnp.broadcast_to(...  20.1 us
    ppermute x33, starting transfers between devices, swapped(): return lax.ppermute(block, 'ctx', [(i, i ^ 1 << bit) for i in range(n)])  18.8 us
    all_to_all x1, blocking collectives, body(): lax.all_to_all(added(mine, swapped(sent, 0)), 'shard', 0, 0, tiled=True)  17.5 us
  transfers between devices with their start and end apart: 52, of which 26 were waited for; matrix products, arithmetic and copies ran while one was open for 24% of the time, Pallas kernels for 11%

profile of v1, /device:TPU:0, one launch (start us, length us, event | category | flops | bytes accessed | tf_op | source)
XLA Modules:
  0.0 466.9 jit_solution(3375072742342700439)
XLA Ops:
  15.3 20.1 %all_to_all.20 = bf16[4,40,576]{2,1,0:T(8,128)(2,1)S(1)} all-to-all(bf16[4,40,576]{2,1,0:T(8,128)(2,1)S(1)} %pad_maximum_fusion.23), channel_id=1, replica_groups=mesh['ctx'=8,'shard'=4] {'shard'}, dimensions={0} | all-to-all | bytes 368640 | tf_op jit(solution)/shard_map/all_to_all | solution.py:411
  43.1 3.7 collective-permute-done.1
  70.8 3.6 collective-permute-done.3
  77.5 12.3 %collective-permute-done.9.refs_1_ = bf16[2,512,384]{2,1,0:T(8,128)(2,1)} collective-permute-done((bf16[2,512,384]{2,1,0:T(8,128)(2,1)S(1)}, bf16[2,512,384]{2,1,0:T(8,128)(2,1)}, u32[]{:S(2)}, u32[]{:S(2)}) %collective-permute-start.9) | collective-permute-done | bytes 786464 | tf_op jit(solution)/shard_map/ppermute | solution.py:62
  91.5 4.4 collective-permute-start.7
  99.0 3.9 collective-permute-done.7.q_ref
  103.0 17.0 %attention_forward.3 = (bf16[4,192,128]{2,1,0:T(8,128)(2,1)}, f32[192,512]{1,0:T(8,128)}, f32[3,1,512]{2,1,0:T(1,128)}) custom-call(s32[2]{0:T(128)} %pad_add_fusion.1.info, bf16[512,192]{1,0:T(8,128)(2,1)} %collective-permute-done.7.q_ref, bf16[2,512,384]{2,1,0:T(8,128)(2,1)} %copy-done.31, bf16[2,512,384]{2,1,0:T(8,128)(2,1)} %collective-permute-done.9.refs_1_, ...), custom_call_target="tpu_custom_call" | custom-call | flops 3623878656 | bytes 3932160 | tf_op jit(solution)/shard_map/attention_forward/pallas_call | solution.py:289
  120.0 5.0 %attention_forward.2 = (bf16[4,192,128]{2,1,0:T(8,128)(2,1)}, f32[192,512]{1,0:T(8,128)}, f32[3,1,512]{2,1,0:T(1,128)}) custom-call(s32[2]{0:T(128)} %pad_add_fusion.info, bf16[512,192]{1,0:T(8,128)(2,1)} %fusion.15.q_ref, bf16[2,512,384]{2,1,0:T(8,128)(2,1)} %pad_maximum_fusion.8.refs_0_, bf16[2,512,384]{2,1,0:T(8,128)(2,1)} %collective-permute-done.4.refs_1_, ...), custom_call_target="tpu_custom_call" | custom-call | flops 3623878656 | bytes 3932160 | tf_op jit(solution)/shard_map/attention_forward/pallas_call | solution.py:289
  132.4 11.9 %all-gather.11.cloned.1.call-start = ((), (), s32[]{:S(2)}) async-start(), calls=%async_computation.10 | async-start | bytes 1474560 | tf_op jit(solution)/shard_map/all_gather | solution.py:465
  161.8 24.7 %all-gather.11.cloned.1.call-done = bf16[768,768]{1,0:T(8,128)(2,1)} async-done(((bf16[192,768]{1,0:T(8,128)(2,1)}), bf16[768,768]{1,0:T(8,128)(2,1)}) %all-gather.11.cloned.1.call-update) | async-done | bytes 1179664 | tf_op jit(solution)/shard_map/all_gather | solution.py:465
  195.0 18.8 %collective-permute-done.16 = bf16[4,192,768]{2,1,0:T(8,128)(2,1)S(1)} collective-permute-done((bf16[4,192,768]{2,1,0:T(8,128)(2,1)}, bf16[4,192,768]{2,1,0:T(8,128)(2,1)S(1)}, u32[]{:S(2)}, u32[]{:S(2)}) %collective-permute-start.16) | collective-permute-done | bytes 1179680 | tf_op jit(solution)/shard_map/ppermute | solution.py:37
  214.2 4.8 %convert_reduce_fusion = (bf16[1536]{0:T(1024)(128)(2,1)}, bf16[512,1536]{1,0:T(8,128)(2,1)S(1)}) fusion(f32[512,1536]{1,0:T(8,128)S(1)} %convolution_add_fusion, bf16[1536,768]{1,0:T(8,128)(2,1)S(1)} %bitcast.262, bf16[256,768]{1,0:T(8,128)(2,1)} %collective-permute-done.18, bf16[256,768]{1,0:T(8,128)(2,1)S(1)} %bitcast.256), kind=kOutput, calls=%fused_computation.34 | convolution fusion | flops 1226832384 | bytes 7867392 | tf_op jit(solution)/shard_map/dot_general | solution.py:100
  238.0 4.1 all-to-all-start.2
  242.2 10.3 %collective-permute-done.22 = bf16[4,192,768]{2,1,0:T(8,128)(2,1)} collective-permute-done((bf16[4,192,768]{2,1,0:T(8,128)(2,1)}, bf16[4,192,768]{2,1,0:T(8,128)(2,1)}, u32[]{:S(2)}, u32[]{:S(2)}) %collective-permute-start.22) | collective-permute-done | bytes 1179680 | tf_op jit(solution)/shard_map/ppermute | solution.py:37
  254.9 15.1 %collective-permute-done.21 = bf16[4,240,768]{2,1,0:T(8,128)(2,1)} collective-permute-done((bf16[4,240,768]{2,1,0:T(8,128)(2,1)}, bf16[4,240,768]{2,1,0:T(8,128)(2,1)}, u32[]{:S(2)}, u32[]{:S(2)}) %collective-permute-start.21) | collective-permute-done | bytes 1474592 | tf_op jit(solution)/shard_map/ppermute | solution.py:37
  275.0 8.2 %attention_backward.2 = (bf16[512,192]{1,0:T(8,128)(2,1)}, bf16[2,512,384]{2,1,0:T(8,128)(2,1)}, bf16[2,512,384]{2,1,0:T(8,128)(2,1)}, bf16[4,512,384]{2,1,0:T(8,128)(2,1)}) custom-call(s32[2]{0:T(128)} %pad_add_fusion.info, bf16[512,192]{1,0:T(8,128)(2,1)} %fusion.15.q_ref, f32[192,512]{1,0:T(8,128)} %get-tuple-element.44.out_ref, ...), custom_call_target="tpu_custom_call" | custom-call | flops 9059696640 | bytes 7864320 | tf_op jit(solution)/shard_map/attention_backward/pallas_call | solution.py:321
  287.2 22.4 %attention_backward.3 = (bf16[512,192]{1,0:T(8,128)(2,1)}, bf16[2,512,384]{2,1,0:T(8,128)(2,1)}, bf16[2,512,384]{2,1,0:T(8,128)(2,1)}, bf16[4,512,384]{2,1,0:T(8,128)(2,1)}) custom-call(s32[2]{0:T(128)} %pad_add_fusion.1.info, bf16[512,192]{1,0:T(8,128)(2,1)} %collective-permute-done.7.q_ref, f32[192,512]{1,0:T(8,128)} %get-tuple-element.51.out_ref, ...), custom_call_target="tpu_custom_call" | custom-call | flops 9059696640 | bytes 7864320 | tf_op jit(solution)/shard_map/attention_backward/pallas_call | solution.py:321
  324.4 15.5 %collective-permute-done.24 = bf16[2,512,384]{2,1,0:T(8,128)(2,1)} collective-permute-done((bf16[2,512,384]{2,1,0:T(8,128)(2,1)}, bf16[2,512,384]{2,1,0:T(8,128)(2,1)}, u32[]{:S(2)}, u32[]{:S(2)}) %collective-permute-start.24) | collective-permute-done | bytes 786464 | tf_op jit(solution)/shard_map/ppermute | solution.py:77
  348.9 7.5 %collective-permute-done.25 = bf16[1,512,384]{2,1,0:T(8,128)(2,1)} collective-permute-done((bf16[1,512,384]{2,1,0:T(8,128)(2,1)}, bf16[1,512,384]{2,1,0:T(8,128)(2,1)}, u32[]{:S(2)}, u32[]{:S(2)}) %collective-permute-start.25) | collective-permute-done | bytes 393248 | tf_op jit(solution)/shard_map/ppermute | solution.py:81
  376.0 17.5 %all_to_all.21 = bf16[4,96,576]{2,1,0:T(8,128)(2,1)S(1)} all-to-all(bf16[4,96,576]{2,1,0:T(8,128)(2,1)S(1)} %fusion.18), channel_id=1, replica_groups=mesh['ctx'=8,'shard'=4] {'shard'}, dimensions={0} | all-to-all | bytes 884736 | tf_op jit(solution)/shard_map/all_to_all | solution.py:632
  395.3 9.5 %collective-permute-done.35 = bf16[96,2304]{1,0:T(8,128)(2,1)S(1)} collective-permute-done((bf16[96,2304]{1,0:T(8,128)(2,1)S(1)}, bf16[96,2304]{1,0:T(8,128)(2,1)S(1)}, u32[]{:S(2)}, u32[]{:S(2)}) %collective-permute-start.35) | collective-permute-done | bytes 442400 | tf_op jit(solution)/shard_map/ppermute | solution.py:37
  405.1 9.8 %collective-permute-done.36 = bf16[96,2304]{1,0:T(8,128)(2,1)S(1)} collective-permute-done((bf16[96,2304]{1,0:T(8,128)(2,1)S(1)}, bf16[96,2304]{1,0:T(8,128)(2,1)S(1)}, u32[]{:S(2)}, u32[]{:S(2)}) %collective-permute-start.36) | collective-permute-done | bytes 442400 | tf_op jit(solution)/shard_map/ppermute | solution.py:37
  420.0 6.4 %collective-permute-done.42 = bf16[192,768]{1,0:T(8,128)(2,1)S(1)} collective-permute-done((bf16[192,768]{1,0:T(8,128)(2,1)S(1)}, bf16[192,768]{1,0:T(8,128)(2,1)S(1)}, u32[]{:S(2)}, u32[]{:S(2)}) %collective-permute-start.42) | collective-permute-done | bytes 294944 | tf_op jit(solution)/shard_map/ppermute | solution.py:37
  426.9 4.0 collective-permute-done.38
  (400 shorter events, 191.3 us)
Async XLA Ops:
  7.2 46.6 %all-gather.7.cloned.1.call-start = ((), (), s32[]{:S(2)}) async-start(), calls=%async_computation.8 | async-start | bytes 1966080 | tf_op jit(solution)/shard_map/all_gather | solution.py:382
  7.9 89.1 %all-gather.9.cloned.1.call-start = ((), (), s32[]{:S(2)}) async-start(), calls=%async_computation.9 | async-start | bytes 2211840 | tf_op jit(solution)/shard_map/all_gather | solution.py:457
  69.2 20.6 %collective-permute-start.9 = (bf16[2,512,384]{2,1,0:T(8,128)(2,1)S(1)}, bf16[2,512,384]{2,1,0:T(8,128)(2,1)}, u32[]{:S(2)}, u32[]{:S(2)}) collective-permute-start(bf16[2,512,384]{2,1,0:T(8,128)(2,1)S(1)} %pad_maximum_fusion.9.refs_0_), channel_id=1, source_target_pairs={{0,8},{4,12},{8,0},{12,4},{16,24},{20,28},{24,16},{28,20},{1,9},{5... | collective-permute-start | bytes 2359304 | tf_op jit(solution)/shard_map/ppermute | solution.py:62
  75.4 16.1 %collective-permute-start.4 = (bf16[2,512,384]{2,1,0:T(8,128)(2,1)}, bf16[2,512,384]{2,1,0:T(8,128)(2,1)}, u32[]{:S(2)}, u32[]{:S(2)}) collective-permute-start(bf16[2,512,384]{2,1,0:T(8,128)(2,1)} %pad_maximum_fusion.8.refs_0_), channel_id=1, source_target_pairs={{0,16},{4,20},{8,24},{12,28},{1,17},{5,21},{9,25},{13,29},{2,18},{... | collective-permute-start | bytes 2359304 | tf_op jit(solution)/shard_map/ppermute | solution.py:62
  77.5 25.4 %collective-permute-start.10 = (bf16[2,512,384]{2,1,0:T(8,128)(2,1)S(1)}, bf16[2,512,384]{2,1,0:T(8,128)(2,1)}, u32[]{:S(2)}, u32[]{:S(2)}) collective-permute-start(bf16[2,512,384]{2,1,0:T(8,128)(2,1)S(1)} %pad_maximum_fusion.9.refs_0_), channel_id=1, source_target_pairs={{0,4},{4,0},{8,12},{12,8},{16,20},{20,16},{24,28},{28,24},{1,5},{5... | collective-permute-start | bytes 2359304 | tf_op jit(solution)/shard_map/ppermute | solution.py:37
  89.8 30.2 %collective-permute-start.5 = (bf16[2,512,384]{2,1,0:T(8,128)(2,1)}, bf16[2,512,384]{2,1,0:T(8,128)(2,1)}, u32[]{:S(2)}, u32[]{:S(2)}) collective-permute-start(bf16[2,512,384]{2,1,0:T(8,128)(2,1)} %pad_maximum_fusion.8.refs_0_), channel_id=1, source_target_pairs={{0,4},{4,0},{8,12},{12,8},{16,20},{20,16},{24,28},{28,24},{1,5},{5... | collective-permute-start | bytes 2359304 | tf_op jit(solution)/shard_map/ppermute | solution.py:37
  91.5 28.6 %collective-permute-start.6 = (bf16[2,512,384]{2,1,0:T(8,128)(2,1)}, bf16[2,512,384]{2,1,0:T(8,128)(2,1)}, u32[]{:S(2)}, u32[]{:S(2)}) collective-permute-start(bf16[2,512,384]{2,1,0:T(8,128)(2,1)} %collective-permute-done.4.refs_1_), channel_id=1, source_target_pairs={{0,4},{4,0},{8,12},{12,8},{16,20},{20,16},{24,28},{28,24},{1,5},{5... | collective-permute-start | bytes 2359304 | tf_op jit(solution)/shard_map/ppermute | solution.py:37
  102.9 45.4 %collective-permute-start.14 = (bf16[4,96,768]{2,1,0:T(8,128)(2,1)}, bf16[4,96,768]{2,1,0:T(8,128)(2,1)}, u32[]{:S(2)}, u32[]{:S(2)}) collective-permute-start(bf16[4,96,768]{2,1,0:T(8,128)(2,1)} %slice.418), channel_id=1, source_target_pairs={{0,4},{4,0},{8,12},{12,8},{16,20},{20,16},{24,28},{28,24},{1,5},{5... | collective-permute-start | bytes 1769480 | tf_op jit(solution)/shard_map/ppermute | solution.py:37
  128.9 21.8 %all-to-all-start.1 = ((bf16[4,192,256]{2,1,0:T(8,128)(2,1)}), bf16[4,192,256]{2,1,0:T(8,128)(2,1)S(1)}, u32[]{:S(2)}, u32[]{:S(2)}) async-start(bf16[4,192,256]{2,1,0:T(8,128)(2,1)} %pad_maximum_fusion.21), calls=%async_computation.1 | async-start | bytes 786432 | tf_op jit(solution)/shard_map/all_to_all | solution.py:488
  132.4 54.1 %all-gather.11.cloned.1.call-start = ((), (), s32[]{:S(2)}) async-start(), calls=%async_computation.10 | async-start | bytes 1474560 | tf_op jit(solution)/shard_map/all_gather | solution.py:465
  148.2 39.7 %collective-permute-start.13 = (bf16[768,768]{1,0:T(8,128)(2,1)}, bf16[768,768]{1,0:T(8,128)(2,1)}, u32[]{:S(2)}, u32[]{:S(2)}) collective-permute-start(bf16[768,768]{1,0:T(8,128)(2,1)} %bitcast.18), channel_id=1, source_target_pairs={{0,8},{4,12},{8,0},{12,4},{16,24},{20,28},{24,16},{28,20},{1,9},{5... | collective-permute-start | bytes 3538952 | tf_op jit(solution)/shard_map/ppermute | solution.py:37
  154.5 35.3 %collective-permute-start.15 = (bf16[256,768]{1,0:T(8,128)(2,1)S(1)}, bf16[256,768]{1,0:T(8,128)(2,1)}, u32[]{:S(2)}, u32[]{:S(2)}) collective-permute-start(bf16[256,768]{1,0:T(8,128)(2,1)S(1)} %add_convert_fusion.14), channel_id=1, source_target_pairs={{0,4},{4,0},{8,12},{12,8},{16,20},{20,16},{24,28},{28,24},{1,5},{5... | collective-permute-start | bytes 1179656 | tf_op jit(solution)/shard_map/ppermute | solution.py:37
  154.6 37.6 %collective-permute-start.18 = (bf16[256,768]{1,0:T(8,128)(2,1)S(1)}, bf16[256,768]{1,0:T(8,128)(2,1)}, u32[]{:S(2)}, u32[]{:S(2)}) collective-permute-start(bf16[256,768]{1,0:T(8,128)(2,1)S(1)} %bitcast.254), channel_id=1, source_target_pairs={{0,4},{4,0},{8,12},{12,8},{16,20},{20,16},{24,28},{28,24},{1,5},{5... | collective-permute-start | bytes 1179656 | tf_op jit(solution)/shard_map/ppermute | solution.py:37
  186.5 27.3 %collective-permute-start.16 = (bf16[4,192,768]{2,1,0:T(8,128)(2,1)}, bf16[4,192,768]{2,1,0:T(8,128)(2,1)S(1)}, u32[]{:S(2)}, u32[]{:S(2)}) collective-permute-start(bf16[4,192,768]{2,1,0:T(8,128)(2,1)} %bitcast.265), channel_id=1, source_target_pairs={{0,16},{4,20},{8,24},{12,28},{16,0},{20,4},{24,8},{28,12},{1,17},{... | collective-permute-start | bytes 3538952 | tf_op jit(solution)/shard_map/ppermute | solution.py:37
  224.3 28.2 %collective-permute-start.22 = (bf16[4,192,768]{2,1,0:T(8,128)(2,1)}, bf16[4,192,768]{2,1,0:T(8,128)(2,1)}, u32[]{:S(2)}, u32[]{:S(2)}) collective-permute-start(bf16[4,192,768]{2,1,0:T(8,128)(2,1)} %select_bitcast_fusion), channel_id=1, source_target_pairs={{0,16},{4,20},{8,24},{12,28},{16,0},{20,4},{24,8},{28,12},{1,17},{... | collective-permute-start | bytes 3538952 | tf_op jit(solution)/shard_map/ppermute | solution.py:37
  235.3 34.7 %collective-permute-start.21 = (bf16[4,240,768]{2,1,0:T(8,128)(2,1)}, bf16[4,240,768]{2,1,0:T(8,128)(2,1)}, u32[]{:S(2)}, u32[]{:S(2)}) collective-permute-start(bf16[4,240,768]{2,1,0:T(8,128)(2,1)} %broadcast_select_fusion), channel_id=1, source_target_pairs={{0,8},{4,12},{8,0},{12,4},{16,24},{20,28},{24,16},{28,20},{1,9},{5... | collective-permute-start | bytes 4423688 | tf_op jit(solution)/shard_map/ppermute | solution.py:37
  238.0 35.6 %all-to-all-start.2 = ((bf16[4,192,256]{2,1,0:T(8,128)(2,1)}), bf16[4,192,256]{2,1,0:T(8,128)(2,1)}, u32[]{:S(2)}, u32[]{:S(2)}) async-start(bf16[4,192,256]{2,1,0:T(8,128)(2,1)} %bitcast.271), calls=%async_computation.2 | async-start | bytes 786432 | tf_op jit(solution)/shard_map/all_to_all | solution.py:518
  242.1 173.8 %reduce-scatter.5.cloned.1.call-start = ((), (), s32[]{:S(2)}) async-start(), calls=%async_computation.7 | async-start | bytes 3317760 | tf_op jit(solution)/shard_map/reduce_scatter | solution.py:553
  283.1 26.6 %collective-permute-start.23 = (bf16[4,512,384]{2,1,0:T(8,128)(2,1)}, bf16[4,512,384]{2,1,0:T(8,128)(2,1)S(1)}, u32[]{:S(2)}, u32[]{:S(2)}) collective-permute-start(bf16[4,512,384]{2,1,0:T(8,128)(2,1)} %get-tuple-element.49), channel_id=1, source_target_pairs={{0,4},{4,0},{8,12},{12,8},{16,20},{20,16},{24,28},{28,24},{1,5},{5... | collective-permute-start | bytes 4718600 | tf_op jit(solution)/shard_map/ppermute | solution.py:37
  312.0 27.9 %collective-permute-start.24 = (bf16[2,512,384]{2,1,0:T(8,128)(2,1)}, bf16[2,512,384]{2,1,0:T(8,128)(2,1)}, u32[]{:S(2)}, u32[]{:S(2)}) collective-permute-start(bf16[2,512,384]{2,1,0:T(8,128)(2,1)} %add_convert_fusion.6), channel_id=1, source_target_pairs={{16,0},{20,4},{24,8},{28,12},{17,1},{21,5},{25,9},{29,13},{18,2},{... | collective-permute-start | bytes 2359304 | tf_op jit(solution)/shard_map/ppermute | solution.py:77
  319.6 27.1 %collective-permute-start.29 = (bf16[2,512,384]{2,1,0:T(8,128)(2,1)}, bf16[2,512,384]{2,1,0:T(8,128)(2,1)}, u32[]{:S(2)}, u32[]{:S(2)}) collective-permute-start(bf16[2,512,384]{2,1,0:T(8,128)(2,1)} %add_convert_fusion.3), channel_id=1, source_target_pairs={{8,0},{12,4},{0,8},{4,12},{24,16},{28,20},{16,24},{20,28},{9,1},{1... | collective-permute-start | bytes 2359304 | tf_op jit(solution)/shard_map/ppermute | solution.py:77
  323.2 120.8 %reduce-scatter.3.cloned.1.call-start = ((), (), s32[]{:S(2)}) async-start(), calls=%async_computation.6 | async-start | bytes 2088960 | tf_op jit(solution)/shard_map/reduce_scatter | solution.py:599
  415.9 15.5 %collective-permute-start.37 = (f32[96,2304]{1,0:T(8,128)}, f32[96,2304]{1,0:T(8,128)}, u32[]{:S(2)}, u32[]{:S(2)}) collective-permute-start(f32[96,2304]{1,0:T(8,128)} %convert_add_fusion.3), channel_id=1, source_target_pairs={{0,4},{4,0},{8,12},{12,8},{16,20},{20,16},{24,28},{28,24},{1,5},{5... | collective-permute-start | bytes 2654216 | tf_op jit(solution)/shard_map/ppermute | solution.py:37
  438.5 16.6 %collective-permute-start.44 = (bf16[384,768]{1,0:T(8,128)(2,1)}, bf16[384,768]{1,0:T(8,128)(2,1)S(1)}, u32[]{:S(2)}, u32[]{:S(2)}) collective-permute-start(bf16[384,768]{1,0:T(8,128)(2,1)} %pad_maximum_fusion.13), channel_id=1, source_target_pairs={{0,4},{4,0},{8,12},{12,8},{16,20},{20,16},{24,28},{28,24},{1,5},{5... | collective-permute-start | bytes 1769480 | tf_op jit(solution)/shard_map/ppermute | solution.py:37
  (84 other events, 746.3 us)
Sparse Core Ops, SparseCore 0:
  9.6 44.1 all-gather.6
  56.0 39.0 all-gather.8
  145.2 41.2 all-gather.10
  323.3 50.6 reduce-scatter.4
  405.2 36.9 reduce-scatter.2

commit v2 on v1

--- a/solution.py
+++ b/solution.py
@@ -51,7 +51,7 @@
     return pairs
 
 
-def spread(own, order, late, before):
+def spread(own, order, late, before, beside):
     held, aparts = own[None], [0]
     for bit in order[:-2]:
         pairs = tree_pairs(aparts, bit, order[order.index(bit) + 1 :], late, False)
@@ -61,6 +61,7 @@
     held = after(held, *before)
     received = lax.ppermute(held, "ctx", tree_pairs(aparts, bit, order[-1:], late, False))
     aparts = aparts + [apart ^ (1 << bit) for apart in aparts]
+    received = after(received, *beside)
     blocks = [held, received, swapped(held, 0), swapped(received, 0)]
     return blocks, aparts + [apart ^ 1 for apart in aparts]
 
@@ -69,10 +70,10 @@
     return (first.astype(f32) + second.astype(f32)).astype(bf16)
 
 
-def returned(near, middle, far, aparts, order, late):
+def returned(near, middle, far, aparts, order, late, before):
     received = swapped(far, 0)
     count = near.shape[0]
-    middle = added(middle, received[count:])
+    middle = after(added(middle, received[count:]), *before)
     pairs = tree_pairs(aparts[:count], order[-2], order[-1:], late, True)
     near = added(added(near, received[:count]), lax.ppermute(middle, "ctx", pairs))
     for bit in order[:-2][::-1]:
@@ -336,7 +337,7 @@
         ],
         compiler_params=pltpu.CompilerParams(vmem_limit_bytes=VMEM_LIMIT),
         cost_estimate=pl.CostEstimate(
-            flops=scores * 40 * HEAD,
+            flops=scores * 10 * HEAD,
             bytes_accessed=8 * rows * width * (count + 2),
             transcendentals=scores,
         ),
@@ -420,6 +421,8 @@
     small = moved[:, share : share + vector_rows, :local_width].astype(f32)
     qkv_own = moved[:, :share]
     for bit in joins:
+        if bit == 0:
+            qkv_own = after(qkv_own, gathered)
         qkv_own = jnp.concatenate(joined(qkv_own, bit, (here >> bit) & 1), axis=1)
     qkv_own = qkv_own.reshape(width, 3 * group)
     q_weight = qkv_own[:, :group]
@@ -427,9 +430,8 @@
 
     vectors = [small[:, i].reshape(-1) for i in range(8)]
     gain_one, shift_one, query_add, value_add, proj_add, gain_two, shift_two, out_add = vectors
-    fc_add = lax.dynamic_index_in_dim(
-        small[:, 8:].reshape(shards, 2, half_hidden), odd, 1, False
-    ).reshape(-1)
+    bias_rows = half_hidden // local_width
+    fc_add = lax.dynamic_slice_in_dim(small, 8 + odd * bias_rows, bias_rows, 1).reshape(-1)
 
     def own_heads(vector):
         return lax.dynamic_slice_in_dim(
@@ -454,15 +456,12 @@
         ],
         axis=1,
     )
-    moved = lax.all_gather(jnp.concatenate([proj_half, fc_quarter]), "shard", axis=0)
-    proj_half = pair_joined(moved[:, :half_width], odd)
-    proj_full = jnp.stack(proj_half, axis=1).reshape(width, width)
-    fc_quarter = moved[:, half_width:].reshape(width, -1)
-    fc_half = jnp.concatenate(joined(fc_quarter, FC_BIT, fc_side), axis=1)
     out_quarter = lax.dynamic_slice_in_dim(
         out_weight, odd * half_hidden + out_side * quarter, quarter, 0
     )
-    out_quarter = lax.all_gather(after(out_quarter, gathered), "shard", axis=0)
+    weights = lax.all_gather(
+        jnp.concatenate([proj_half, fc_quarter, out_quarter]), "shard", axis=0
+    )
 
     orders = [chip_bits + [0], chip_bits[::-1] + [0]]
     orders = [orders[s % 2] for s in range(seqs)]
@@ -475,19 +474,30 @@
         own_blocks.append((dot(normed, kv_weight, ((1,), (0,))) + kv_add).astype(bf16))
         queries.append((dot(normed, q_weight, ((1,), (0,))) + query_add).astype(bf16))
         infos.append(jnp.stack([cycle - 1 - here if late[s] else here, here]).astype(jnp.int32))
-    spreads = [spread(own_blocks[s], orders[s], late[s], queries) for s in range(seqs)]
-    queries = [mirrored(queries[s]) if late[s] else queries[s] for s in range(seqs)]
+    moved = [mirrored(queries[s]) if late[s] else queries[s] for s in range(seqs)]
+    spreads = [spread(own_blocks[s], orders[s], late[s], queries, moved) for s in range(seqs)]
+    queries = moved
     blocks = [blocks for blocks, _ in spreads]
     aparts = [apart for _, apart in spreads]
     saved = [None] * seqs
     attended_parts = [None] * seqs
     for s in reversed(range(seqs)):
-        att, *saved[s] = attend(shards, orders[s], infos[s], queries[s], blocks[s])
-        attended_parts[s] = mirrored(att) if late[s] else att
-    attended = after(jnp.concatenate(attended_parts, axis=2), fc_half)
+        attended_parts[s], *saved[s] = attend(shards, orders[s], infos[s], queries[s], blocks[s])
+    attended_parts = lax.optimization_barrier(tuple(attended_parts))
+    attended_parts = [
+        mirrored(part) if late[s] else part for s, part in enumerate(attended_parts)
+    ]
+    attended, weights = lax.optimization_barrier(
+        (jnp.concatenate(attended_parts, axis=2), weights)
+    )
+    proj_half = pair_joined(weights[:, :half_width], odd)
+    proj_full = jnp.stack(proj_half, axis=1).reshape(width, width)
+    fc_quarter = weights[:, half_width : half_width + local_width].reshape(width, -1)
+    fc_half = jnp.concatenate(joined(fc_quarter, FC_BIT, fc_side), axis=1)
+    out_half = jnp.stack(
+        joined(weights[:, half_width + local_width :], OUT_BIT, out_side), axis=1
+    ).reshape(-1, width)
     attended = lax.all_to_all(attended, "shard", 0, 0, tiled=True).reshape(padded, tokens)[:width]
-    out_quarter = after(out_quarter, *attended_parts)
-    out_half = jnp.stack(joined(out_quarter, OUT_BIT, out_side), axis=1).reshape(-1, width)
 
     inputs32 = layer_input.reshape(tokens, width).astype(f32)
     grads_own = grad_output.reshape(tokens, width)
@@ -539,8 +549,7 @@
 
     query_low = [None] * seqs
     kv_parts = [None] * seqs
-    scattered = jnp.concatenate([added(fc_mine, fc_received), added(out_mine, out_received)], axis=1)
-    grad_heads = after(grad_heads, scattered)
+    grad_heads = after(grad_heads, fc_sent, out_sent)
     for s in range(seqs):
         heads_grad, first = grad_heads, s * piece
         if late[s]:
@@ -548,8 +557,16 @@
         low, *kv_parts[s] = attend_back(
             shards, orders[s], first, infos[s], queries[s], *saved[s], heads_grad, blocks[s]
         )
-        query_low[s] = mirrored(low) if late[s] else low
-
+        query_low[s] = low
+
+    ended = [parts[0] for parts in kv_parts]
+    query_low = [
+        mirrored(after(low, *ended)) if late[s] else low for s, low in enumerate(query_low)
+    ]
+    scattered = jnp.concatenate(
+        [added(fc_mine, after(fc_received, *ended)), added(out_mine, after(out_received, *ended))],
+        axis=1,
+    )
     both = lax.psum_scatter(scattered, "shard", scatter_dimension=0, tiled=False)
 
     kv_low = [None] * seqs
@@ -557,7 +574,7 @@
     gain_one_grad = jnp.zeros((width,), f32)
     shift_one_grad = jnp.zeros((width,), f32)
     for s in range(seqs):
-        kv_low[s] = returned(*kv_parts[s], aparts[s], orders[s], late[s])
+        kv_low[s] = returned(*kv_parts[s], aparts[s], orders[s], late[s], query_low + [scattered])
         part = dot(query_low[s], q_weight, ((1,), (1,))) + dot(kv_low[s], kv_weight, ((1,), (1,)))
         gain_one_grad = gain_one_grad + jnp.sum(part * group_norms[s], axis=0)
         shift_one_grad = shift_one_grad + jnp.sum(part, axis=0)
@@ -596,6 +613,7 @@
         + [jnp.pad(vectors, ((0, 0), (0, 16 - vector_rows), (0, width - local_width)))],
         axis=1,
     )
+    normed_parts = after(normed_parts, both)
     summed = lax.psum_scatter(normed_parts, "shard", scatter_dimension=0, tiled=False).astype(f32)
     pull = jax.vjp(lambda v: normalized(v) * gain_one, inputs32)[1]
     input_grad = (grad_middle + pull(summed[:tokens])[0]).astype(bf16)
@@ -627,11 +645,17 @@
         normed = after(normed_one[s], normed_parts)
         low = jnp.concatenate([query_low[s], kv_low[s]], axis=1)
         grad.append(dot(normed, low, flat))
-    grad = sum(grad).astype(bf16).reshape(shards, 2, half_width, -1)
-    mine, sent = parted(grad[:, 0], grad[:, 1], odd)
-    grad = lax.all_to_all(added(mine, swapped(sent, 0)), "shard", 0, 0, tiled=True)
+    grad = sum(grad).astype(bf16).reshape(shards, local_width, -1)
+    for bit in joins[::-1]:
+        cut = grad.shape[1] // 2
+        mine, sent = parted(grad[:, :cut], grad[:, cut:], (here >> bit) & 1)
+        grad = added(mine, swapped(sent, bit))
+    grad = lax.all_to_all(grad, "shard", 0, 0, tiled=True)
     grad = jnp.concatenate([grad[z] for z in range(shards)], axis=1)
-    grad = jnp.concatenate(pair_joined(summed_over_chips(grad, chip_bits), odd))
+    for turn, bit in enumerate(joins):
+        if turn == 1:
+            grad = after(grad, summed)
+        grad = jnp.concatenate(joined(grad, bit, (here >> bit) & 1))
     thirds = [
         jnp.concatenate(
             [
@@ -642,7 +666,7 @@
         )[:, :width]
         for third in range(3)
     ]
-    qkv_grad = jnp.concatenate(thirds, axis=1)
+    qkv_grad = jnp.concatenate(thirds, axis=1).astype(f32)
 
     return (
         layer_output.reshape(seqs, piece, width),

time: 473 us -> 489 us (1.034)
  waiting for transfers between devices: 169 us -> 237 us
  blocking collectives: 37.7 us -> 0 us
  local copies, waits for them, and re-layouts: 44 us -> 29.3 us
    reduce_scatter x1, waiting for transfers between devices: 0.01 us -> 38.1 us  [body(): lax.psum_scatter(scattered, 'shard', scatter_dimension=0, tiled=False)]
    ppermute x4, waiting for transfers between devices: 6.73 us -> 44.9 us  [mirrored(): return lax.ppermute(block, 'ctx', [(i, n - 1 - i) for i in range(n)])]
    all_to_all x2 -> x0, blocking collectives: 37.7 us -> none  [the longest x1 20.1 us: body(): lax.all_to_all(jnp.concatenate([by_heads(weight_share), jnp.broadcast_to(...]
    all_gather x2 -> x1, waiting for transfers between devices: 24.7 us -> 0.01 us  [body(): lax.all_gather(jnp.concatenate([proj_half, fc_quarter, out_quarter]), 'sh...]
    all_to_all x0 -> x2, waiting for transfers between devices: none -> 22.8 us  [the longest x1 12.7 us: body(): lax.all_to_all(jnp.concatenate([by_heads(weight_share), jnp.broadcast_to(...]
    ppermute x2, waiting for transfers between devices: 13.4 us -> 0.01 us  [spread(): lax.ppermute(held, 'ctx', tree_pairs(aparts, bit, order[-1:], late, False))]
    all_gather x2 -> x1, starting transfers between devices: 11.9 us -> 0.01 us  [body(): lax.all_gather(jnp.concatenate([proj_half, fc_quarter, out_quarter]), 'sh...]
    all_to_all x0 -> x2, starting transfers between devices: none -> 10.8 us  [the longest x1 6.32 us: body(): lax.all_to_all(jnp.concatenate([by_heads(weight_share), jnp.broadcast_to(...]
  transfers between devices with their start and end apart: 52 -> 55, of which waited for: 26 -> 30; matrix products, arithmetic and copies ran while one was open for 24% -> 19% of each run, Pallas kernels for 11% -> 11%
where the time goes in v2:
time: 489 us; the launch traced here: 480 us
  waiting for transfers between devices  237 us (48%)
  starting transfers between devices  61.7 us (13%)
  other arithmetic  54.6 us (11%)
  Pallas kernels  52.8 us (11%)
  local copies, waits for them, and re-layouts  29.3 us (6%)
  matrix products  29.2 us (6%)
  between operations  15.6 us (3%)
    ppermute x35, waiting for transfers between devices, swapped(): return lax.ppermute(block, 'ctx', [(i, i ^ 1 << bit) for i in range(n)])  85.5 us
    ppermute x4, waiting for transfers between devices, mirrored(): return lax.ppermute(block, 'ctx', [(i, n - 1 - i) for i in range(n)])  44.9 us
    reduce_scatter x1, waiting for transfers between devices, body(): lax.psum_scatter(scattered, 'shard', scatter_dimension=0, tiled=False)  38.1 us
    pallas_call x2, Pallas kernels, attend_back(): pl.pallas_call(functools.partial(backward_kernel, heads, shards, order, f...  30.3 us
    dot_general x19, matrix products, dot(): lax.dot_general(a, b, ((contract[0], contract[1]), ((), ())), preferred_e...  29.2 us
    ppermute x35, starting transfers between devices, swapped(): return lax.ppermute(block, 'ctx', [(i, i ^ 1 << bit) for i in range(n)])  23.4 us
    pallas_call x2, Pallas kernels, attend(): pl.pallas_call(functools.partial(forward_kernel, heads, shards, order), o...  22.5 us
    ppermute x2, waiting for transfers between devices, returned(): lax.ppermute(middle, 'ctx', pairs)  16.4 us
  transfers between devices with their start and end apart: 55, of which 30 were waited for; matrix products, arithmetic and copies ran while one was open for 19% of the time, Pallas kernels for 11%

profile of v2, /device:TPU:0, one launch (start us, length us, event | category | flops | bytes accessed | tf_op | source)
XLA Modules:
  0.0 479.8 jit_solution(12658168751358316988)
XLA Ops:
  15.9 6.3 %all-to-all-start = ((bf16[4,40,576]{2,1,0:T(8,128)(2,1)}), bf16[4,40,576]{2,1,0:T(8,128)(2,1)S(1)}, u32[]{:S(2)}, u32[]{:S(2)}) async-start(bf16[4,40,576]{2,1,0:T(8,128)(2,1)} %pad_maximum_fusion.28), calls=%async_computation | async-start | bytes 409600 | tf_op jit(solution)/shard_map/all_to_all | solution.py:412
  23.4 12.7 %all-to-all-done = bf16[4,40,576]{2,1,0:T(8,128)(2,1)S(1)} async-done(((bf16[4,40,576]{2,1,0:T(8,128)(2,1)}), bf16[4,40,576]{2,1,0:T(8,128)(2,1)S(1)}, u32[]{:S(2)}, u32[]{:S(2)}) %all-to-all-start) | async-done | bytes 184352 | tf_op jit(solution)/shard_map/all_to_all | solution.py:412
  47.5 6.4 %all-gather.5.cloned.1.call-done = bf16[8,128,768]{2,1,0:T(8,128)(2,1)} async-done(((bf16[2,128,768]{2,1,0:T(8,128)(2,1)}), bf16[8,128,768]{2,1,0:T(8,128)(2,1)}) %all-gather.5.cloned.1.call-update) | async-done | bytes 1572880 | tf_op jit(solution)/shard_map/all_gather | solution.py:383
  66.2 6.0 %collective-permute-done.3 = bf16[1,512,384]{2,1,0:T(8,128)(2,1)S(1)} collective-permute-done((bf16[1,512,384]{2,1,0:T(8,128)(2,1)S(1)}, bf16[1,512,384]{2,1,0:T(8,128)(2,1)S(1)}, u32[]{:S(2)}, u32[]{:S(2)}) %collective-permute-start.3) | collective-permute-done | bytes 393248 | tf_op jit(solution)/shard_map/ppermute | solution.py:58
  78.2 21.7 %collective-permute-done.5.q_ref = bf16[512,192]{1,0:T(8,128)(2,1)S(1)} collective-permute-done((bf16[512,192]{1,0:T(8,128)(2,1)S(1)}, bf16[512,192]{1,0:T(8,128)(2,1)S(1)}, u32[]{:S(2)}, u32[]{:S(2)}) %collective-permute-start.5) | collective-permute-done | bytes 196640 | tf_op jit(solution)/shard_map/ppermute | solution.py:92
  103.0 5.0 %attention_forward.2 = (bf16[4,192,128]{2,1,0:T(8,128)(2,1)}, f32[192,512]{1,0:T(8,128)}, f32[3,1,512]{2,1,0:T(1,128)}) custom-call(s32[2]{0:T(128)} %pad_add_fusion.info, bf16[512,192]{1,0:T(8,128)(2,1)} %fusion.16.q_ref, bf16[2,512,384]{2,1,0:T(8,128)(2,1)} %copy-done.27, bf16[2,512,384]{2,1,0:T(8,128)(2,1)} %collective-permute-done.4.refs_1_, ...), custom_call_target="tpu_custom_call" | custom-call | flops 3623878656 | bytes 3932160 | tf_op jit(solution)/shard_map/attention_forward/pallas_call | solution.py:290
  108.1 17.5 %attention_forward.3 = (bf16[4,192,128]{2,1,0:T(8,128)(2,1)}, f32[192,512]{1,0:T(8,128)}, f32[3,1,512]{2,1,0:T(1,128)}) custom-call(s32[2]{0:T(128)} %pad_add_fusion.1.info, bf16[512,192]{1,0:T(8,128)(2,1)} %copy-done.47, bf16[2,512,384]{2,1,0:T(8,128)(2,1)} %copy-done.26, bf16[2,512,384]{2,1,0:T(8,128)(2,1)} %collective-permute-done.9.refs_1_, ...), custom_call_target="tpu_custom_call" | custom-call | flops 3623878656 | bytes 3932160 | tf_op jit(solution)/shard_map/attention_forward/pallas_call | solution.py:290
  128.8 5.4 %collective-permute-done.12 = bf16[4,192,128]{2,1,0:T(8,128)(2,1)S(1)} collective-permute-done((bf16[4,192,128]{2,1,0:T(8,128)(2,1)}, bf16[4,192,128]{2,1,0:T(8,128)(2,1)S(1)}, u32[]{:S(2)}, u32[]{:S(2)}) %collective-permute-start.12) | collective-permute-done | bytes 196640 | tf_op jit(solution)/shard_map/ppermute | solution.py:92
  149.5 16.2 %collective-permute-done.16 = bf16[4,192,768]{2,1,0:T(8,128)(2,1)} collective-permute-done((bf16[4,192,768]{2,1,0:T(8,128)(2,1)}, bf16[4,192,768]{2,1,0:T(8,128)(2,1)}, u32[]{:S(2)}, u32[]{:S(2)}) %collective-permute-start.16) | collective-permute-done | bytes 1179680 | tf_op jit(solution)/shard_map/ppermute | solution.py:37
  173.9 22.2 %collective-permute-done.15 = bf16[768,768]{1,0:T(8,128)(2,1)} collective-permute-done((bf16[768,768]{1,0:T(8,128)(2,1)S(1)}, bf16[768,768]{1,0:T(8,128)(2,1)}, u32[]{:S(2)}, u32[]{:S(2)}) %collective-permute-start.15) | collective-permute-done | bytes 1179680 | tf_op jit(solution)/shard_map/ppermute | solution.py:37
  200.9 5.0 %convert_reduce_fusion = (bf16[1536]{0:T(1024)(128)(2,1)}, bf16[512,1536]{1,0:T(8,128)(2,1)S(1)}) fusion(f32[512,1536]{1,0:T(8,128)S(1)} %convolution_add_fusion, bf16[1536,768]{1,0:T(8,128)(2,1)S(1)} %bitcast.239, bf16[256,768]{1,0:T(8,128)(2,1)} %collective-permute-done.18, bf16[256,768]{1,0:T(8,128)(2,1)S(1)} %bitcast.236), kind=kOutput, calls=%fused_computation.12 | convolution fusion | flops 1226832384 | bytes 7867392 | tf_op jit(solution)/shard_map/dot_general | solution.py:101
  232.8 7.7 %all-to-all-done.2.go_ref = bf16[4,192,256]{2,1,0:T(8,128)(2,1)} async-done(((bf16[4,192,256]{2,1,0:T(8,128)(2,1)}), bf16[4,192,256]{2,1,0:T(8,128)(2,1)}, u32[]{:S(2)}, u32[]{:S(2)}) %all-to-all-start.2) | async-done | bytes 393248 | tf_op jit(solution)/shard_map/all_to_all | solution.py:528
  242.5 7.8 %attention_backward.2 = (bf16[512,192]{1,0:T(8,128)(2,1)}, bf16[2,512,384]{2,1,0:T(8,128)(2,1)}, bf16[2,512,384]{2,1,0:T(8,128)(2,1)}, bf16[4,512,384]{2,1,0:T(8,128)(2,1)}) custom-call(s32[2]{0:T(128)} %pad_add_fusion.info, bf16[512,192]{1,0:T(8,128)(2,1)} %fusion.16.q_ref, f32[192,512]{1,0:T(8,128)} %get-tuple-element.58.out_ref, ...), custom_call_target="tpu_custom_call" | custom-call | flops 2264924160 | bytes 7864320 | tf_op jit(solution)/shard_map/attention_backward/pallas_call | solution.py:322
  253.3 16.6 %collective-permute-done.22.go_ref = bf16[4,192,128]{2,1,0:T(8,128)(2,1)S(1)} collective-permute-done((bf16[4,192,128]{2,1,0:T(8,128)(2,1)S(1)}, bf16[4,192,128]{2,1,0:T(8,128)(2,1)S(1)}, u32[]{:S(2)}, u32[]{:S(2)}) %collective-permute-start.22) | collective-permute-done | bytes 196640 | tf_op jit(solution)/shard_map/ppermute | solution.py:92
  270.5 22.5 %attention_backward.3 = (bf16[512,192]{1,0:T(8,128)(2,1)}, bf16[2,512,384]{2,1,0:T(8,128)(2,1)}, bf16[2,512,384]{2,1,0:T(8,128)(2,1)}, bf16[4,512,384]{2,1,0:T(8,128)(2,1)}) custom-call(s32[2]{0:T(128)} %pad_add_fusion.1.info, bf16[512,192]{1,0:T(8,128)(2,1)} %copy-done.47, f32[192,512]{1,0:T(8,128)} %get-tuple-element.65.out_ref, ...), custom_call_target="tpu_custom_call" | custom-call | flops 2264924160 | bytes 7864320 | tf_op jit(solution)/shard_map/attention_backward/pallas_call | solution.py:322
  308.1 16.4 %collective-permute-done.26 = bf16[2,512,384]{2,1,0:T(8,128)(2,1)} collective-permute-done((bf16[2,512,384]{2,1,0:T(8,128)(2,1)}, bf16[2,512,384]{2,1,0:T(8,128)(2,1)}, u32[]{:S(2)}, u32[]{:S(2)}) %collective-permute-start.26) | collective-permute-done | bytes 786464 | tf_op jit(solution)/shard_map/ppermute | solution.py:78
  331.8 8.2 %collective-permute-done.27 = bf16[1,512,384]{2,1,0:T(8,128)(2,1)} collective-permute-done((bf16[1,512,384]{2,1,0:T(8,128)(2,1)}, bf16[1,512,384]{2,1,0:T(8,128)(2,1)}, u32[]{:S(2)}, u32[]{:S(2)}) %collective-permute-start.27) | collective-permute-done | bytes 393248 | tf_op jit(solution)/shard_map/ppermute | solution.py:82
  357.9 6.9 %collective-permute-done.35 = bf16[4,48,576]{2,1,0:T(8,128)(2,1)S(1)} collective-permute-done((bf16[4,48,576]{2,1,0:T(8,128)(2,1)S(1)}, bf16[4,48,576]{2,1,0:T(8,128)(2,1)S(1)}, u32[]{:S(2)}, u32[]{:S(2)}) %collective-permute-start.35) | collective-permute-done | bytes 221216 | tf_op jit(solution)/shard_map/ppermute | solution.py:37
  365.1 4.7 collective-permute-done.36
  370.6 4.5 all-to-all-start.3
  375.1 10.2 %all-to-all-done.3 = bf16[4,24,576]{2,1,0:T(8,128)(2,1)S(1)} async-done(((bf16[4,24,576]{2,1,0:T(8,128)(2,1)}), bf16[4,24,576]{2,1,0:T(8,128)(2,1)S(1)}, u32[]{:S(2)}, u32[]{:S(2)}) %all-to-all-start.3) | async-done | bytes 110624 | tf_op jit(solution)/shard_map/all_to_all | solution.py:653
  385.7 4.5 collective-permute-done.37
  404.1 38.1 %reduce-scatter.5.cloned.1.call-done = bf16[1,432,768]{2,1,0:T(8,128)(2,1)} async-done(((bf16[4,432,768]{2,1,0:T(8,128)(2,1)}), bf16[1,432,768]{2,1,0:T(8,128)(2,1)}) %reduce-scatter.5.cloned.1.call-update) | async-done | bytes 663568 | tf_op jit(solution)/shard_map/reduce_scatter | solution.py:570
  448.4 6.5 %collective-permute-done.44 = bf16[192,768]{1,0:T(8,128)(2,1)S(1)} collective-permute-done((bf16[192,768]{1,0:T(8,128)(2,1)S(1)}, bf16[192,768]{1,0:T(8,128)(2,1)S(1)}, u32[]{:S(2)}, u32[]{:S(2)}) %collective-permute-start.44) | collective-permute-done | bytes 294944 | tf_op jit(solution)/shard_map/ppermute | solution.py:37
  (395 shorter events, 185.5 us)
Async XLA Ops:
  7.2 46.6 %all-gather.5.cloned.1.call-start = ((), (), s32[]{:S(2)}) async-start(), calls=%async_computation.8 | async-start | bytes 1966080 | tf_op jit(solution)/shard_map/all_gather | solution.py:383
  15.9 20.1 %all-to-all-start = ((bf16[4,40,576]{2,1,0:T(8,128)(2,1)}), bf16[4,40,576]{2,1,0:T(8,128)(2,1)S(1)}, u32[]{:S(2)}, u32[]{:S(2)}) async-start(bf16[4,40,576]{2,1,0:T(8,128)(2,1)} %pad_maximum_fusion.28), calls=%async_computation | async-start | bytes 409600 | tf_op jit(solution)/shard_map/all_to_all | solution.py:412
  22.3 112.7 %all-gather.7.cloned.1.call-start = ((), (), s32[]{:S(2)}) async-start(), calls=%async_computation.9 | async-start | bytes 3686400 | tf_op jit(solution)/shard_map/all_gather | solution.py:462
  72.3 27.7 %collective-permute-start.4 = (bf16[2,512,384]{2,1,0:T(8,128)(2,1)S(1)}, bf16[2,512,384]{2,1,0:T(8,128)(2,1)}, u32[]{:S(2)}, u32[]{:S(2)}) collective-permute-start(bf16[2,512,384]{2,1,0:T(8,128)(2,1)S(1)} %pad_maximum_fusion.10.refs_0_), channel_id=1, source_target_pairs={{0,16},{4,20},{8,24},{12,28},{1,17},{5,21},{9,25},{13,29},{2,18},{... | collective-permute-start | bytes 2359304 | tf_op jit(solution)/shard_map/ppermute | solution.py:62
  75.7 24.8 %collective-permute-start.9 = (bf16[2,512,384]{2,1,0:T(8,128)(2,1)S(1)}, bf16[2,512,384]{2,1,0:T(8,128)(2,1)}, u32[]{:S(2)}, u32[]{:S(2)}) collective-permute-start(bf16[2,512,384]{2,1,0:T(8,128)(2,1)S(1)} %pad_maximum_fusion.11.refs_0_), channel_id=1, source_target_pairs={{0,8},{4,12},{8,0},{12,4},{16,24},{20,28},{24,16},{28,20},{1,9},{5... | collective-permute-start | bytes 2359304 | tf_op jit(solution)/shard_map/ppermute | solution.py:62
  78.2 21.7 %collective-permute-start.5 = (bf16[512,192]{1,0:T(8,128)(2,1)S(1)}, bf16[512,192]{1,0:T(8,128)(2,1)S(1)}, u32[]{:S(2)}, u32[]{:S(2)}) collective-permute-start(bf16[512,192]{1,0:T(8,128)(2,1)S(1)} %fusion.17), channel_id=1, source_target_pairs={{0,28},{4,24},{8,20},{12,16},{16,12},{20,8},{24,4},{28,0},{1,29},{... | collective-permute-start | bytes 589832 | tf_op jit(solution)/shard_map/ppermute | solution.py:92
  78.2 23.5 %collective-permute-start.6 = (bf16[2,512,384]{2,1,0:T(8,128)(2,1)S(1)}, bf16[2,512,384]{2,1,0:T(8,128)(2,1)}, u32[]{:S(2)}, u32[]{:S(2)}) collective-permute-start(bf16[2,512,384]{2,1,0:T(8,128)(2,1)S(1)} %pad_maximum_fusion.10.refs_0_), channel_id=1, source_target_pairs={{0,4},{4,0},{8,12},{12,8},{16,20},{20,16},{24,28},{28,24},{1,5},{5... | collective-permute-start | bytes 2359304 | tf_op jit(solution)/shard_map/ppermute | solution.py:37
  137.4 28.3 %collective-permute-start.16 = (bf16[4,192,768]{2,1,0:T(8,128)(2,1)}, bf16[4,192,768]{2,1,0:T(8,128)(2,1)}, u32[]{:S(2)}, u32[]{:S(2)}) collective-permute-start(bf16[4,192,768]{2,1,0:T(8,128)(2,1)} %slice.348), channel_id=1, source_target_pairs={{0,16},{4,20},{8,24},{12,28},{16,0},{20,4},{24,8},{28,12},{1,17},{... | collective-permute-start | bytes 3538952 | tf_op jit(solution)/shard_map/ppermute | solution.py:37
  139.9 61.0 %collective-permute-start.18 = (bf16[256,768]{1,0:T(8,128)(2,1)S(1)}, bf16[256,768]{1,0:T(8,128)(2,1)}, u32[]{:S(2)}, u32[]{:S(2)}) collective-permute-start(bf16[256,768]{1,0:T(8,128)(2,1)S(1)} %bitcast.235), channel_id=1, source_target_pairs={{0,4},{4,0},{8,12},{12,8},{16,20},{20,16},{24,28},{28,24},{1,5},{5... | collective-permute-start | bytes 1179656 | tf_op jit(solution)/shard_map/ppermute | solution.py:37
  142.8 27.3 %all-to-all-start.1 = ((bf16[4,192,256]{2,1,0:T(8,128)(2,1)}), bf16[4,192,256]{2,1,0:T(8,128)(2,1)}, u32[]{:S(2)}, u32[]{:S(2)}) async-start(bf16[4,192,256]{2,1,0:T(8,128)(2,1)} %pad_maximum_fusion.25), calls=%async_computation.1 | async-start | bytes 786432 | tf_op jit(solution)/shard_map/all_to_all | solution.py:500
  168.6 27.5 %collective-permute-start.15 = (bf16[768,768]{1,0:T(8,128)(2,1)S(1)}, bf16[768,768]{1,0:T(8,128)(2,1)}, u32[]{:S(2)}, u32[]{:S(2)}) collective-permute-start(bf16[768,768]{1,0:T(8,128)(2,1)S(1)} %bitcast.232), channel_id=1, source_target_pairs={{0,8},{4,12},{8,0},{12,4},{16,24},{20,28},{24,16},{28,20},{1,9},{5... | collective-permute-start | bytes 3538952 | tf_op jit(solution)/shard_map/ppermute | solution.py:37
  172.7 24.9 %collective-permute-start.14 = (bf16[256,768]{1,0:T(8,128)(2,1)S(1)}, bf16[256,768]{1,0:T(8,128)(2,1)S(1)}, u32[]{:S(2)}, u32[]{:S(2)}) collective-permute-start(bf16[256,768]{1,0:T(8,128)(2,1)S(1)} %add_convert_fusion.14), channel_id=1, source_target_pairs={{0,4},{4,0},{8,12},{12,8},{16,20},{20,16},{24,28},{28,24},{1,5},{5... | collective-permute-start | bytes 1179656 | tf_op jit(solution)/shard_map/ppermute | solution.py:37
  212.6 80.6 %collective-permute-start.25 = (bf16[4,192,768]{2,1,0:T(8,128)(2,1)}, bf16[4,192,768]{2,1,0:T(8,128)(2,1)}, u32[]{:S(2)}, u32[]{:S(2)}) collective-permute-start(bf16[4,192,768]{2,1,0:T(8,128)(2,1)} %select_bitcast_fusion), channel_id=1, source_target_pairs={{0,16},{4,20},{8,24},{12,28},{16,0},{20,4},{24,8},{28,12},{1,17},{... | collective-permute-start | bytes 3538952 | tf_op jit(solution)/shard_map/ppermute | solution.py:37
  223.7 16.8 %all-to-all-start.2 = ((bf16[4,192,256]{2,1,0:T(8,128)(2,1)}), bf16[4,192,256]{2,1,0:T(8,128)(2,1)}, u32[]{:S(2)}, u32[]{:S(2)}) async-start(bf16[4,192,256]{2,1,0:T(8,128)(2,1)} %bitcast.245), calls=%async_computation.2 | async-start | bytes 786432 | tf_op jit(solution)/shard_map/all_to_all | solution.py:528
  227.8 162.5 %reduce-scatter.3.cloned.1.call-start = ((), (), s32[]{:S(2)}) async-start(), calls=%async_computation.6 | async-start | bytes 2088960 | tf_op jit(solution)/shard_map/reduce_scatter | solution.py:617
  231.1 64.0 %collective-permute-start.24 = (bf16[4,240,768]{2,1,0:T(8,128)(2,1)}, bf16[4,240,768]{2,1,0:T(8,128)(2,1)}, u32[]{:S(2)}, u32[]{:S(2)}) collective-permute-start(bf16[4,240,768]{2,1,0:T(8,128)(2,1)} %broadcast_select_fusion), channel_id=1, source_target_pairs={{0,8},{4,12},{8,0},{12,4},{16,24},{20,28},{24,16},{28,20},{1,9},{5... | collective-permute-start | bytes 4423688 | tf_op jit(solution)/shard_map/ppermute | solution.py:37
  241.4 28.4 %collective-permute-start.22 = (bf16[4,192,128]{2,1,0:T(8,128)(2,1)S(1)}, bf16[4,192,128]{2,1,0:T(8,128)(2,1)S(1)}, u32[]{:S(2)}, u32[]{:S(2)}) collective-permute-start(bf16[4,192,128]{2,1,0:T(8,128)(2,1)S(1)} %slice.364), channel_id=1, source_target_pairs={{0,28},{4,24},{8,20},{12,16},{16,12},{20,8},{24,4},{28,0},{1,29},{... | collective-permute-start | bytes 589832 | tf_op jit(solution)/shard_map/ppermute | solution.py:92
  250.3 48.4 %collective-permute-start.21 = (bf16[4,512,384]{2,1,0:T(8,128)(2,1)}, bf16[4,512,384]{2,1,0:T(8,128)(2,1)}, u32[]{:S(2)}, u32[]{:S(2)}) collective-permute-start(bf16[4,512,384]{2,1,0:T(8,128)(2,1)} %get-tuple-element.63), channel_id=1, source_target_pairs={{0,4},{4,0},{8,12},{12,8},{16,20},{20,16},{24,28},{28,24},{1,5},{5... | collective-permute-start | bytes 4718600 | tf_op jit(solution)/shard_map/ppermute | solution.py:37
  302.4 22.0 %collective-permute-start.26 = (bf16[2,512,384]{2,1,0:T(8,128)(2,1)}, bf16[2,512,384]{2,1,0:T(8,128)(2,1)}, u32[]{:S(2)}, u32[]{:S(2)}) collective-permute-start(bf16[2,512,384]{2,1,0:T(8,128)(2,1)} %add_convert_fusion.6), channel_id=1, source_target_pairs={{16,0},{20,4},{24,8},{28,12},{17,1},{21,5},{25,9},{29,13},{18,2},{... | collective-permute-start | bytes 2359304 | tf_op jit(solution)/shard_map/ppermute | solution.py:78
  306.4 22.9 %collective-permute-start.29 = (bf16[2,512,384]{2,1,0:T(8,128)(2,1)}, bf16[2,512,384]{2,1,0:T(8,128)(2,1)}, u32[]{:S(2)}, u32[]{:S(2)}) collective-permute-start(bf16[2,512,384]{2,1,0:T(8,128)(2,1)} %add_convert_fusion.3), channel_id=1, source_target_pairs={{8,0},{12,4},{0,8},{4,12},{24,16},{28,20},{16,24},{20,28},{9,1},{1... | collective-permute-start | bytes 2359304 | tf_op jit(solution)/shard_map/ppermute | solution.py:78
  349.9 92.4 %reduce-scatter.5.cloned.1.call-start = ((), (), s32[]{:S(2)}) async-start(), calls=%async_computation.7 | async-start | bytes 3317760 | tf_op jit(solution)/shard_map/reduce_scatter | solution.py:570
  370.6 14.7 %all-to-all-start.3 = ((bf16[4,24,576]{2,1,0:T(8,128)(2,1)}), bf16[4,24,576]{2,1,0:T(8,128)(2,1)S(1)}, u32[]{:S(2)}, u32[]{:S(2)}) async-start(bf16[4,24,576]{2,1,0:T(8,128)(2,1)} %add_convert_fusion.18), calls=%async_computation.4 | async-start | bytes 245760 | tf_op jit(solution)/shard_map/all_to_all | solution.py:653
  404.0 44.0 %collective-permute-start.39 = (bf16[96,2304]{1,0:T(8,128)(2,1)S(1)}, bf16[96,2304]{1,0:T(8,128)(2,1)S(1)}, u32[]{:S(2)}, u32[]{:S(2)}) collective-permute-start(bf16[96,2304]{1,0:T(8,128)(2,1)S(1)} %pad_maximum_fusion.24), channel_id=1, source_target_pairs={{0,4},{4,0},{8,12},{12,8},{16,20},{20,16},{24,28},{28,24},{1,5},{5... | collective-permute-start | bytes 1327112 | tf_op jit(solution)/shard_map/ppermute | solution.py:37
  444.0 13.5 %collective-permute-start.40 = (bf16[240,768]{1,0:T(8,128)(2,1)}, bf16[240,768]{1,0:T(8,128)(2,1)S(1)}, u32[]{:S(2)}, u32[]{:S(2)}) collective-permute-start(bf16[240,768]{1,0:T(8,128)(2,1)} %slice_bitcast_fusion.7), channel_id=1, source_target_pairs={{0,16},{4,20},{8,24},{12,28},{16,0},{20,4},{24,8},{28,12},{1,17},{... | collective-permute-start | bytes 1105928 | tf_op jit(solution)/shard_map/ppermute | solution.py:37
  (80 other events, 558.0 us)
Sparse Core Ops, SparseCore 0:
  9.6 44.1 all-gather.4
  56.0 59.0 all-gather.6
  350.0 38.2 reduce-scatter.2
  390.5 51.6 reduce-scatter.4

commit v3 on v2

--- a/solution.py
+++ b/solution.py
@@ -42,16 +42,16 @@
     reach = [0]
     for other in later:
         reach += [r ^ (1 << other) for r in reach]
+    place = (lambda i: n - 1 - i) if late else (lambda i: i)
     pairs = []
     for i in range(n):
         target = i ^ (1 << bit)
-        queries = [n - 1 - (target ^ r) if late else target ^ r for r in reach]
-        if any(i ^ apart <= max(queries) for apart in aparts):
+        if any(place(i ^ apart) <= place(target ^ r) for r in reach for apart in aparts):
             pairs.append((target, i) if back else (i, target))
     return pairs
 
 
-def spread(own, order, late, before, beside):
+def spread(own, order, late, before):
     held, aparts = own[None], [0]
     for bit in order[:-2]:
         pairs = tree_pairs(aparts, bit, order[order.index(bit) + 1 :], late, False)
@@ -61,7 +61,6 @@
     held = after(held, *before)
     received = lax.ppermute(held, "ctx", tree_pairs(aparts, bit, order[-1:], late, False))
     aparts = aparts + [apart ^ (1 << bit) for apart in aparts]
-    received = after(received, *beside)
     blocks = [held, received, swapped(held, 0), swapped(received, 0)]
     return blocks, aparts + [apart ^ 1 for apart in aparts]
 
@@ -175,12 +174,12 @@
                 m_ref[h] = m
 
         for key_part in range(per):
-            step(slot_of(info[0], info[1], order), key_part, True, key_part == 0)
+            step(slot_of(info[0], info[0], order), key_part, True, key_part == 0)
 
         @pl.loop(0, info[0])
         def _(j):
             for key_part in range(per):
-                step(slot_of(j, info[1], order), key_part, False, False)
+                step(slot_of(j, info[0], order), key_part, False, False)
 
         for h in range(heads):
             total = l_ref[h]
@@ -208,7 +207,7 @@
 
     @pl.loop(info[0] + 1, count)
     def _(j):
-        sums[slot_of(j, info[1], order)] = jnp.zeros((rows, 2 * width), bf16)
+        sums[slot_of(j, info[0], order)] = jnp.zeros((rows, 2 * width), bf16)
 
     for copy in copies:
         copy.wait()
@@ -254,12 +253,12 @@
                     acc_ref[h] += dq
 
         for key_part in range(per):
-            step(slot_of(info[0], info[1], order), key_part, True, key_part == 0)
+            step(slot_of(info[0], info[0], order), key_part, True, key_part == 0)
 
         @pl.loop(0, info[0])
         def _(j):
             for key_part in range(per):
-                step(slot_of(j, info[1], order), key_part, False, False)
+                step(slot_of(j, info[0], order), key_part, False, False)
 
         for h in range(heads):
             dq_ref[span, h * HEAD : (h + 1) * HEAD] = (acc_ref[h] * 0.125).T.astype(bf16)
@@ -380,6 +379,12 @@
     late = [seq >= (seqs + 1) // 2 for seq in range(seqs)]
     tokens = seqs * piece
 
+
+    def mirror_late(held):
+        return jnp.stack([mirrored(held[s]) if late[s] else held[s] for s in range(seqs)])
+
+    layer_input = mirror_late(layer_input)
+    grad_output = mirror_late(grad_output)
     gathered = lax.all_gather(layer_input, "shard", axis=0)
 
     def by_heads(weight):
@@ -422,7 +427,7 @@
     qkv_own = moved[:, :share]
     for bit in joins:
         if bit == 0:
-            qkv_own = after(qkv_own, gathered)
+            qkv_own, grad_output, _ = lax.optimization_barrier((qkv_own, grad_output, gathered))
         qkv_own = jnp.concatenate(joined(qkv_own, bit, (here >> bit) & 1), axis=1)
     qkv_own = qkv_own.reshape(width, 3 * group)
     q_weight = qkv_own[:, :group]
@@ -473,35 +478,32 @@
         normed_one.append(normed)
         own_blocks.append((dot(normed, kv_weight, ((1,), (0,))) + kv_add).astype(bf16))
         queries.append((dot(normed, q_weight, ((1,), (0,))) + query_add).astype(bf16))
-        infos.append(jnp.stack([cycle - 1 - here if late[s] else here, here]).astype(jnp.int32))
-    moved = [mirrored(queries[s]) if late[s] else queries[s] for s in range(seqs)]
-    spreads = [spread(own_blocks[s], orders[s], late[s], queries, moved) for s in range(seqs)]
-    queries = moved
+        infos.append(jnp.reshape(cycle - 1 - here if late[s] else here, (1,)).astype(jnp.int32))
+    spreads = [spread(own_blocks[s], orders[s], late[s], queries) for s in range(seqs)]
     blocks = [blocks for blocks, _ in spreads]
     aparts = [apart for _, apart in spreads]
     saved = [None] * seqs
     attended_parts = [None] * seqs
     for s in reversed(range(seqs)):
         attended_parts[s], *saved[s] = attend(shards, orders[s], infos[s], queries[s], blocks[s])
-    attended_parts = lax.optimization_barrier(tuple(attended_parts))
-    attended_parts = [
-        mirrored(part) if late[s] else part for s, part in enumerate(attended_parts)
-    ]
     attended, weights = lax.optimization_barrier(
         (jnp.concatenate(attended_parts, axis=2), weights)
     )
-    proj_half = pair_joined(weights[:, :half_width], odd)
+    cut = half_width + local_width
+    proj_half, fc_quarter, out_quarter = lax.optimization_barrier(
+        (weights[:, :half_width], weights[:, half_width:cut], weights[:, cut:])
+    )
+    proj_half = pair_joined(proj_half, odd)
     proj_full = jnp.stack(proj_half, axis=1).reshape(width, width)
-    fc_quarter = weights[:, half_width : half_width + local_width].reshape(width, -1)
+    fc_quarter = fc_quarter.reshape(width, -1)
     fc_half = jnp.concatenate(joined(fc_quarter, FC_BIT, fc_side), axis=1)
-    out_half = jnp.stack(
-        joined(weights[:, half_width + local_width :], OUT_BIT, out_side), axis=1
-    ).reshape(-1, width)
+    out_half = jnp.stack(joined(out_quarter, OUT_BIT, out_side), axis=1).reshape(-1, width)
     attended = lax.all_to_all(attended, "shard", 0, 0, tiled=True).reshape(padded, tokens)[:width]
 
     inputs32 = layer_input.reshape(tokens, width).astype(f32)
     grads_own = grad_output.reshape(tokens, width)
     grads32 = grads_own.astype(f32)
+    attended, fc_half = lax.optimization_barrier((attended, fc_half))
     middle = inputs32 + dot(attended, proj_full, ((0,), (0,))) + proj_add
     normed_two = layer_norm(middle, gain_two, shift_two).astype(bf16)
 
@@ -551,18 +553,11 @@
     kv_parts = [None] * seqs
     grad_heads = after(grad_heads, fc_sent, out_sent)
     for s in range(seqs):
-        heads_grad, first = grad_heads, s * piece
-        if late[s]:
-            heads_grad, first = mirrored(grad_heads[:, :, s * piece : (s + 1) * piece]), 0
-        low, *kv_parts[s] = attend_back(
-            shards, orders[s], first, infos[s], queries[s], *saved[s], heads_grad, blocks[s]
+        query_low[s], *kv_parts[s] = attend_back(
+            shards, orders[s], s * piece, infos[s], queries[s], *saved[s], grad_heads, blocks[s]
         )
-        query_low[s] = low
 
     ended = [parts[0] for parts in kv_parts]
-    query_low = [
-        mirrored(after(low, *ended)) if late[s] else low for s, low in enumerate(query_low)
-    ]
     scattered = jnp.concatenate(
         [added(fc_mine, after(fc_received, *ended)), added(out_mine, after(out_received, *ended))],
         axis=1,
@@ -574,7 +569,7 @@
     gain_one_grad = jnp.zeros((width,), f32)
     shift_one_grad = jnp.zeros((width,), f32)
     for s in range(seqs):
-        kv_low[s] = returned(*kv_parts[s], aparts[s], orders[s], late[s], query_low + [scattered])
+        kv_low[s] = returned(*kv_parts[s], aparts[s], orders[s], late[s], [scattered])
         part = dot(query_low[s], q_weight, ((1,), (1,))) + dot(kv_low[s], kv_weight, ((1,), (1,)))
         gain_one_grad = gain_one_grad + jnp.sum(part * group_norms[s], axis=0)
         shift_one_grad = shift_one_grad + jnp.sum(part, axis=0)
@@ -608,12 +603,11 @@
         ],
         axis=1,
     ).astype(bf16)
-    normed_parts = jnp.concatenate(
-        normed_parts
-        + [jnp.pad(vectors, ((0, 0), (0, 16 - vector_rows), (0, width - local_width)))],
-        axis=1,
-    )
-    normed_parts = after(normed_parts, both)
+    vectors = jnp.pad(vectors, ((0, 0), (0, 16 - vector_rows), (0, width - local_width)))
+    vectors = lax.dynamic_update_slice(
+        vectors, jnp.broadcast_to(both[:1, :1], (shards, 1, 1)), (0, 15, 0)
+    )
+    normed_parts = jnp.concatenate(normed_parts + [vectors], axis=1)
     summed = lax.psum_scatter(normed_parts, "shard", scatter_dimension=0, tiled=False).astype(f32)
     pull = jax.vjp(lambda v: normalized(v) * gain_one, inputs32)[1]
     input_grad = (grad_middle + pull(summed[:tokens])[0]).astype(bf16)
@@ -669,8 +663,8 @@
     qkv_grad = jnp.concatenate(thirds, axis=1).astype(f32)
 
     return (
-        layer_output.reshape(seqs, piece, width),
-        input_grad.reshape(seqs, piece, width),
+        mirror_late(layer_output.reshape(seqs, piece, width)),
+        mirror_late(input_grad.reshape(seqs, piece, width)),
         sums[0],
         sums[1],
         qkv_grad,

time: 489 us -> 425 us (0.87)
  waiting for transfers between devices: 237 us -> 126 us
  blocking collectives: 0 us -> 15.6 us
  starting transfers between devices: 61.7 us -> 75.6 us
  Pallas kernels: 52.8 us -> 63.6 us
  other arithmetic: 54.6 us -> 64.3 us
    reduce_scatter x1, waiting for transfers between devices: 38.1 us -> 0.02 us  [body(): lax.psum_scatter(scattered, 'shard', scatter_dimension=0, tiled=False)]
    ppermute x35, waiting for transfers between devices: 85.5 us -> 54.2 us  [swapped(): return lax.ppermute(block, 'ctx', [(i, i ^ 1 << bit) for i in range(n)])]
    ppermute x4, waiting for transfers between devices: 44.9 us -> 26.4 us  [mirrored(): return lax.ppermute(block, 'ctx', [(i, n - 1 - i) for i in range(n)])]
    ppermute x2, waiting for transfers between devices: 16.4 us -> 0.01 us  [returned(): lax.ppermute(middle, 'ctx', pairs)]
    all_to_all x0 -> x1, blocking collectives: none -> 15.6 us  [body(): grad_heads = lax.all_to_all(grad_attended, 'shard', 0, 0, tiled=True)]
    ppermute x2, waiting for transfers between devices: 0.01 us -> 14.9 us  [spread(): lax.ppermute(held, 'ctx', tree_pairs(aparts, bit, order[-1:], late, False))]
    pallas_call x2, Pallas kernels: 22.5 us -> 33.1 us  [attend(): pl.pallas_call(functools.partial(forward_kernel, heads, shards, order), o...]
    all_to_all x1 -> x0, waiting for transfers between devices: 7.7 us -> none  [body(): grad_heads = lax.all_to_all(grad_attended, 'shard', 0, 0, tiled=True)]
  transfers between devices with their start and end apart: 55 -> 54, of which waited for: 30 -> 25; matrix products, arithmetic and copies ran while one was open for 19% -> 23% of each run, Pallas kernels for 11% -> 15%
where the time goes in v3:
time: 425 us; the launch traced here: 420 us
  waiting for transfers between devices  126 us (30%)
  starting transfers between devices  75.6 us (18%)
  other arithmetic  64.3 us (15%)
  Pallas kernels  63.6 us (15%)
  local copies, waits for them, and re-layouts  32.6 us (8%)
  matrix products  26.4 us (6%)
  blocking collectives  15.6 us (4%)
  between operations  15.5 us (4%)
    ppermute x35, waiting for transfers between devices, swapped(): return lax.ppermute(block, 'ctx', [(i, i ^ 1 << bit) for i in range(n)])  54.2 us
    pallas_call x2, Pallas kernels, attend(): pl.pallas_call(functools.partial(forward_kernel, heads, shards, order), o...  33.1 us
    pallas_call x2, Pallas kernels, attend_back(): pl.pallas_call(functools.partial(backward_kernel, heads, shards, order, f...  30.6 us
    ppermute x35, starting transfers between devices, swapped(): return lax.ppermute(block, 'ctx', [(i, i ^ 1 << bit) for i in range(n)])  29.2 us
    dot_general x19, matrix products, dot(): lax.dot_general(a, b, ((contract[0], contract[1]), ((), ())), preferred_e...  26.4 us
    ppermute x4, waiting for transfers between devices, mirrored(): return lax.ppermute(block, 'ctx', [(i, n - 1 - i) for i in range(n)])  26.4 us
    all_to_all x1, blocking collectives, body(): grad_heads = lax.all_to_all(grad_attended, 'shard', 0, 0, tiled=True)  15.6 us
    ppermute x2, waiting for transfers between devices, spread(): lax.ppermute(held, 'ctx', tree_pairs(aparts, bit, order[-1:], late, False))  14.9 us
  transfers between devices with their start and end apart: 54, of which 25 were waited for; matrix products, arithmetic and copies ran while one was open for 23% of the time, Pallas kernels for 15%

profile of v3, /device:TPU:0, one launch (start us, length us, event | category | flops | bytes accessed | tf_op | source)
XLA Modules:
  0.0 419.9 jit_solution(15649621643606411278)
XLA Ops:
  11.9 5.3 %collective-permute-done = bf16[128,768]{1,0:T(8,128)(2,1)S(1)} collective-permute-done((bf16[128,768]{1,0:T(8,128)(2,1)S(1)}, bf16[128,768]{1,0:T(8,128)(2,1)S(1)}, u32[]{:S(2)}, u32[]{:S(2)}) %collective-permute-start) | collective-permute-done | bytes 196640 | tf_op jit(solution)/shard_map/ppermute | solution.py:91
  20.5 5.7 %all-to-all-start = ((bf16[4,40,576]{2,1,0:T(8,128)(2,1)}), bf16[4,40,576]{2,1,0:T(8,128)(2,1)S(1)}, u32[]{:S(2)}, u32[]{:S(2)}) async-start(bf16[4,40,576]{2,1,0:T(8,128)(2,1)} %pad_maximum_fusion.30), calls=%async_computation | async-start | bytes 409600 | tf_op jit(solution)/shard_map/all_to_all | solution.py:417
  30.4 7.5 %all-to-all-done = bf16[4,40,576]{2,1,0:T(8,128)(2,1)S(1)} async-done(((bf16[4,40,576]{2,1,0:T(8,128)(2,1)}), bf16[4,40,576]{2,1,0:T(8,128)(2,1)S(1)}, u32[]{:S(2)}, u32[]{:S(2)}) %all-to-all-start) | async-done | bytes 184352 | tf_op jit(solution)/shard_map/all_to_all | solution.py:417
  45.3 3.9 collective-permute-done.2
  50.2 10.0 %all-gather.5.cloned.1.call-done = bf16[8,128,768]{2,1,0:T(8,128)(2,1)} async-done(((bf16[2,128,768]{2,1,0:T(8,128)(2,1)}), bf16[8,128,768]{2,1,0:T(8,128)(2,1)}) %all-gather.5.cloned.1.call-update) | async-done | bytes 1572880 | tf_op jit(solution)/shard_map/all_gather | solution.py:388
  68.7 3.5 collective-permute-start.5
  74.3 5.4 %collective-permute-done.9 = bf16[1,512,384]{2,1,0:T(8,128)(2,1)S(1)} collective-permute-done((bf16[1,512,384]{2,1,0:T(8,128)(2,1)S(1)}, bf16[1,512,384]{2,1,0:T(8,128)(2,1)S(1)}, u32[]{:S(2)}, u32[]{:S(2)}) %collective-permute-start.9) | collective-permute-done | bytes 393248 | tf_op jit(solution)/shard_map/ppermute | solution.py:58
  79.9 3.5 collective-permute-start.10
  87.0 13.7 %collective-permute-done.10.refs_1_ = bf16[2,512,384]{2,1,0:T(8,128)(2,1)} collective-permute-done((bf16[2,512,384]{2,1,0:T(8,128)(2,1)S(1)}, bf16[2,512,384]{2,1,0:T(8,128)(2,1)}, u32[]{:S(2)}, u32[]{:S(2)}) %collective-permute-start.10) | collective-permute-done | bytes 786464 | tf_op jit(solution)/shard_map/ppermute | solution.py:62
  103.3 16.9 %attention_forward.3 = (bf16[4,192,128]{2,1,0:T(8,128)(2,1)}, f32[192,512]{1,0:T(8,128)}, f32[3,1,512]{2,1,0:T(1,128)}) custom-call(s32[1]{0:T(128)} %bitcast.19.info, bf16[512,192]{1,0:T(8,128)(2,1)} %fusion.16.q_ref, bf16[2,512,384]{2,1,0:T(8,128)(2,1)} %copy-done.28, bf16[2,512,384]{2,1,0:T(8,128)(2,1)} %collective-permute-done.10.refs_1_, ...), custom_call_target="tpu_custom_call" | custom-call | flops 3623878656 | bytes 3932160 | tf_op jit(solution)/shard_map/attention_forward/pallas_call | solution.py:289
  120.3 16.2 %attention_forward.2 = (bf16[4,192,128]{2,1,0:T(8,128)(2,1)}, f32[192,512]{1,0:T(8,128)}, f32[3,1,512]{2,1,0:T(1,128)}) custom-call(s32[1]{0:T(128)} %bitcast.3.info, bf16[512,192]{1,0:T(8,128)(2,1)} %fusion.15.q_ref, bf16[2,512,384]{2,1,0:T(8,128)(2,1)} %pad_maximum_fusion.8.refs_0_, bf16[2,512,384]{2,1,0:T(8,128)(2,1)} %collective-permute-done.6.refs_1_, ...), custom_call_target="tpu_custom_call" | custom-call | flops 3623878656 | bytes 3932160 | tf_op jit(solution)/shard_map/attention_forward/pallas_call | solution.py:289
  146.2 3.5 all-to-all-start.1
  154.6 16.6 %collective-permute-done.13 = bf16[768,768]{1,0:T(8,128)(2,1)} collective-permute-done((bf16[768,768]{1,0:T(8,128)(2,1)}, bf16[768,768]{1,0:T(8,128)(2,1)}, u32[]{:S(2)}, u32[]{:S(2)}) %collective-permute-start.13) | collective-permute-done | bytes 1179680 | tf_op jit(solution)/shard_map/ppermute | solution.py:37
  185.6 4.8 %convert_reduce_fusion = (bf16[1536]{0:T(1024)(128)(2,1)}, bf16[512,1536]{1,0:T(8,128)(2,1)S(1)}) fusion(f32[512,1536]{1,0:T(8,128)S(1)} %convolution_add_fusion, bf16[1536,768]{1,0:T(8,128)(2,1)S(1)} %bitcast.258, bf16[256,768]{1,0:T(8,128)(2,1)} %collective-permute-done.19, bf16[256,768]{1,0:T(8,128)(2,1)S(1)} %bitcast.247), kind=kOutput, calls=%fused_computation.12 | convolution fusion | flops 1226832384 | bytes 7867392 | tf_op jit(solution)/shard_map/dot_general | solution.py:100
  207.2 15.6 %all_to_all.20.go_ref = bf16[4,192,256]{2,1,0:T(8,128)(2,1)} all-to-all(bf16[4,192,256]{2,1,0:T(8,128)(2,1)S(1)} %bitcast.262), channel_id=1, replica_groups=mesh['ctx'=8,'shard'=4] {'shard'}, dimensions={0} | all-to-all | bytes 786432 | tf_op jit(solution)/shard_map/all_to_all | solution.py:530
  222.7 8.1 %attention_backward.2 = (bf16[512,192]{1,0:T(8,128)(2,1)}, bf16[2,512,384]{2,1,0:T(8,128)(2,1)}, bf16[2,512,384]{2,1,0:T(8,128)(2,1)}, bf16[4,512,384]{2,1,0:T(8,128)(2,1)}) custom-call(s32[1]{0:T(128)} %bitcast.3.info, bf16[512,192]{1,0:T(8,128)(2,1)} %fusion.15.q_ref, f32[192,512]{1,0:T(8,128)} %get-tuple-element.61.out_ref, ...), custom_call_target="tpu_custom_call" | custom-call | flops 2264924160 | bytes 7864320 | tf_op jit(solution)/shard_map/attention_backward/pallas_call | solution.py:321
  232.1 22.4 %attention_backward.3 = (bf16[512,192]{1,0:T(8,128)(2,1)}, bf16[2,512,384]{2,1,0:T(8,128)(2,1)}, bf16[2,512,384]{2,1,0:T(8,128)(2,1)}, bf16[4,512,384]{2,1,0:T(8,128)(2,1)}) custom-call(s32[1]{0:T(128)} %bitcast.19.info, bf16[512,192]{1,0:T(8,128)(2,1)} %fusion.16.q_ref, f32[192,512]{1,0:T(8,128)} %get-tuple-element.68.out_ref, ...), custom_call_target="tpu_custom_call" | custom-call | flops 2264924160 | bytes 7864320 | tf_op jit(solution)/shard_map/attention_backward/pallas_call | solution.py:321
  276.5 16.9 %collective-permute-done.18 = bf16[128,768]{1,0:T(8,128)(2,1)} collective-permute-done((bf16[128,768]{1,0:T(8,128)(2,1)}, bf16[128,768]{1,0:T(8,128)(2,1)}, u32[]{:S(2)}, u32[]{:S(2)}) %collective-permute-start.18) | collective-permute-done | bytes 196640 | tf_op jit(solution)/shard_map/ppermute | solution.py:91
  298.0 6.5 %collective-permute-start.26 = (bf16[1,512,384]{2,1,0:T(8,128)(2,1)S(1)}, bf16[1,512,384]{2,1,0:T(8,128)(2,1)}, u32[]{:S(2)}, u32[]{:S(2)}) collective-permute-start(bf16[1,512,384]{2,1,0:T(8,128)(2,1)S(1)} %slice.499), channel_id=1, source_target_pairs={{8,0},{12,4},{0,8},{4,12},{24,16},{28,20},{9,1},{13,5},{1,9},{5,13... | collective-permute-start | bytes 1179656 | tf_op jit(solution)/shard_map/ppermute | solution.py:81
  356.8 7.7 %collective-permute-done.35 = bf16[4,48,576]{2,1,0:T(8,128)(2,1)S(1)} collective-permute-done((bf16[4,48,576]{2,1,0:T(8,128)(2,1)S(1)}, bf16[4,48,576]{2,1,0:T(8,128)(2,1)S(1)}, u32[]{:S(2)}, u32[]{:S(2)}) %collective-permute-start.35) | collective-permute-done | bytes 221216 | tf_op jit(solution)/shard_map/ppermute | solution.py:37
  370.2 3.5 all-to-all-start.3
  373.8 5.8 %all-to-all-done.3 = bf16[4,24,576]{2,1,0:T(8,128)(2,1)S(1)} async-done(((bf16[4,24,576]{2,1,0:T(8,128)(2,1)}), bf16[4,24,576]{2,1,0:T(8,128)(2,1)S(1)}, u32[]{:S(2)}, u32[]{:S(2)}) %all-to-all-start.3) | async-done | bytes 110624 | tf_op jit(solution)/shard_map/all_to_all | solution.py:647
  395.2 5.6 %collective-permute-done.32 = f32[12,192]{1,0:T(8,128)S(1)} collective-permute-done((f32[12,192]{1,0:T(8,128)S(1)}, f32[12,192]{1,0:T(8,128)S(1)}, u32[]{:S(2)}, u32[]{:S(2)}) %collective-permute-start.32) | collective-permute-done | bytes 9248 | tf_op jit(solution)/shard_map/ppermute | solution.py:37
  405.9 4.2 collective-permute-done.30
  (427 shorter events, 191.7 us)
Async XLA Ops:
  7.3 52.9 %all-gather.5.cloned.1.call-start = ((), (), s32[]{:S(2)}) async-start(), calls=%async_computation.8 | async-start | bytes 1966080 | tf_op jit(solution)/shard_map/all_gather | solution.py:388
  20.5 17.4 %all-to-all-start = ((bf16[4,40,576]{2,1,0:T(8,128)(2,1)}), bf16[4,40,576]{2,1,0:T(8,128)(2,1)S(1)}, u32[]{:S(2)}, u32[]{:S(2)}) async-start(bf16[4,40,576]{2,1,0:T(8,128)(2,1)} %pad_maximum_fusion.30), calls=%async_computation | async-start | bytes 409600 | tf_op jit(solution)/shard_map/all_to_all | solution.py:417
  26.2 112.0 %all-gather.7.cloned.1.call-start = ((), (), s32[]{:S(2)}) async-start(), calls=%async_computation.9 | async-start | bytes 3686400 | tf_op jit(solution)/shard_map/all_gather | solution.py:467
  79.9 20.9 %collective-permute-start.10 = (bf16[2,512,384]{2,1,0:T(8,128)(2,1)S(1)}, bf16[2,512,384]{2,1,0:T(8,128)(2,1)}, u32[]{:S(2)}, u32[]{:S(2)}) collective-permute-start(bf16[2,512,384]{2,1,0:T(8,128)(2,1)S(1)} %pad_maximum_fusion.9.refs_0_), channel_id=1, source_target_pairs={{0,8},{4,12},{8,0},{12,4},{24,16},{28,20},{1,9},{5,13},{9,1},{13,5... | collective-permute-start | bytes 2359304 | tf_op jit(solution)/shard_map/ppermute | solution.py:62
  84.3 18.0 %collective-permute-start.6 = (bf16[2,512,384]{2,1,0:T(8,128)(2,1)}, bf16[2,512,384]{2,1,0:T(8,128)(2,1)}, u32[]{:S(2)}, u32[]{:S(2)}) collective-permute-start(bf16[2,512,384]{2,1,0:T(8,128)(2,1)} %pad_maximum_fusion.8.refs_0_), channel_id=1, source_target_pairs={{0,16},{4,20},{8,24},{12,28},{1,17},{5,21},{9,25},{13,29},{2,18},{... | collective-permute-start | bytes 2359304 | tf_op jit(solution)/shard_map/ppermute | solution.py:62
  87.0 15.4 %collective-permute-start.11 = (bf16[2,512,384]{2,1,0:T(8,128)(2,1)S(1)}, bf16[2,512,384]{2,1,0:T(8,128)(2,1)}, u32[]{:S(2)}, u32[]{:S(2)}) collective-permute-start(bf16[2,512,384]{2,1,0:T(8,128)(2,1)S(1)} %pad_maximum_fusion.9.refs_0_), channel_id=1, source_target_pairs={{0,4},{4,0},{8,12},{12,8},{16,20},{20,16},{24,28},{28,24},{1,5},{5... | collective-permute-start | bytes 2359304 | tf_op jit(solution)/shard_map/ppermute | solution.py:37
  100.7 19.5 %collective-permute-start.7 = (bf16[2,512,384]{2,1,0:T(8,128)(2,1)}, bf16[2,512,384]{2,1,0:T(8,128)(2,1)}, u32[]{:S(2)}, u32[]{:S(2)}) collective-permute-start(bf16[2,512,384]{2,1,0:T(8,128)(2,1)} %pad_maximum_fusion.8.refs_0_), channel_id=1, source_target_pairs={{0,4},{4,0},{8,12},{12,8},{16,20},{20,16},{24,28},{28,24},{1,5},{5... | collective-permute-start | bytes 2359304 | tf_op jit(solution)/shard_map/ppermute | solution.py:37
  102.3 17.9 %collective-permute-start.8 = (bf16[2,512,384]{2,1,0:T(8,128)(2,1)}, bf16[2,512,384]{2,1,0:T(8,128)(2,1)}, u32[]{:S(2)}, u32[]{:S(2)}) collective-permute-start(bf16[2,512,384]{2,1,0:T(8,128)(2,1)} %collective-permute-done.6.refs_1_), channel_id=1, source_target_pairs={{0,4},{4,0},{8,12},{12,8},{16,20},{20,16},{24,28},{28,24},{1,5},{5... | collective-permute-start | bytes 2359304 | tf_op jit(solution)/shard_map/ppermute | solution.py:37
  142.5 28.6 %collective-permute-start.13 = (bf16[768,768]{1,0:T(8,128)(2,1)}, bf16[768,768]{1,0:T(8,128)(2,1)}, u32[]{:S(2)}, u32[]{:S(2)}) collective-permute-start(bf16[768,768]{1,0:T(8,128)(2,1)} %bitcast.23), channel_id=1, source_target_pairs={{0,8},{4,12},{8,0},{12,4},{16,24},{20,28},{24,16},{28,20},{1,9},{5... | collective-permute-start | bytes 3538952 | tf_op jit(solution)/shard_map/ppermute | solution.py:37
  146.0 39.7 %collective-permute-start.19 = (bf16[256,768]{1,0:T(8,128)(2,1)S(1)}, bf16[256,768]{1,0:T(8,128)(2,1)}, u32[]{:S(2)}, u32[]{:S(2)}) collective-permute-start(bf16[256,768]{1,0:T(8,128)(2,1)S(1)} %bitcast.246), channel_id=1, source_target_pairs={{0,4},{4,0},{8,12},{12,8},{16,20},{20,16},{24,28},{28,24},{1,5},{5... | collective-permute-start | bytes 1179656 | tf_op jit(solution)/shard_map/ppermute | solution.py:37
  146.2 28.3 %all-to-all-start.1 = ((bf16[4,192,256]{2,1,0:T(8,128)(2,1)}), bf16[4,192,256]{2,1,0:T(8,128)(2,1)S(1)}, u32[]{:S(2)}, u32[]{:S(2)}) async-start(bf16[4,192,256]{2,1,0:T(8,128)(2,1)} %pad_maximum_fusion.25), calls=%async_computation.1 | async-start | bytes 786432 | tf_op jit(solution)/shard_map/all_to_all | solution.py:501
  149.7 178.6 %reduce-scatter.3.cloned.1.call-start = ((), (), s32[]{:S(2)}) async-start(), calls=%async_computation.6 | async-start | bytes 3317760 | tf_op jit(solution)/shard_map/reduce_scatter | solution.py:565
  149.7 29.2 %collective-permute-start.16 = (bf16[4,192,768]{2,1,0:T(8,128)(2,1)}, bf16[4,192,768]{2,1,0:T(8,128)(2,1)}, u32[]{:S(2)}, u32[]{:S(2)}) collective-permute-start(bf16[4,192,768]{2,1,0:T(8,128)(2,1)} %get-tuple-element.59), channel_id=1, source_target_pairs={{0,16},{4,20},{8,24},{12,28},{16,0},{20,4},{24,8},{28,12},{1,17},{... | collective-permute-start | bytes 3538952 | tf_op jit(solution)/shard_map/ppermute | solution.py:37
  196.6 58.0 %collective-permute-start.24 = (bf16[4,192,768]{2,1,0:T(8,128)(2,1)}, bf16[4,192,768]{2,1,0:T(8,128)(2,1)}, u32[]{:S(2)}, u32[]{:S(2)}) collective-permute-start(bf16[4,192,768]{2,1,0:T(8,128)(2,1)} %select_bitcast_fusion), channel_id=1, source_target_pairs={{0,16},{4,20},{8,24},{12,28},{16,0},{20,4},{24,8},{28,12},{1,17},{... | collective-permute-start | bytes 3538952 | tf_op jit(solution)/shard_map/ppermute | solution.py:37
  205.5 50.8 %collective-permute-start.23 = (bf16[4,240,768]{2,1,0:T(8,128)(2,1)}, bf16[4,240,768]{2,1,0:T(8,128)(2,1)}, u32[]{:S(2)}, u32[]{:S(2)}) collective-permute-start(bf16[4,240,768]{2,1,0:T(8,128)(2,1)} %broadcast_select_fusion), channel_id=1, source_target_pairs={{0,8},{4,12},{8,0},{12,4},{16,24},{20,28},{24,16},{28,20},{1,9},{5... | collective-permute-start | bytes 4423688 | tf_op jit(solution)/shard_map/ppermute | solution.py:37
  230.9 31.2 %collective-permute-start.22 = (bf16[4,512,384]{2,1,0:T(8,128)(2,1)}, bf16[4,512,384]{2,1,0:T(8,128)(2,1)}, u32[]{:S(2)}, u32[]{:S(2)}) collective-permute-start(bf16[4,512,384]{2,1,0:T(8,128)(2,1)} %get-tuple-element.66), channel_id=1, source_target_pairs={{0,4},{4,0},{8,12},{12,8},{16,20},{20,16},{24,28},{28,24},{1,5},{5... | collective-permute-start | bytes 4718600 | tf_op jit(solution)/shard_map/ppermute | solution.py:37
  260.0 130.7 %reduce-scatter.5.cloned.1.call-start = ((), (), s32[]{:S(2)}) async-start(), calls=%async_computation.7 | async-start | bytes 2088960 | tf_op jit(solution)/shard_map/reduce_scatter | solution.py:611
  264.6 30.7 %collective-permute-start.25 = (bf16[2,512,384]{2,1,0:T(8,128)(2,1)}, bf16[2,512,384]{2,1,0:T(8,128)(2,1)}, u32[]{:S(2)}, u32[]{:S(2)}) collective-permute-start(bf16[2,512,384]{2,1,0:T(8,128)(2,1)} %add_convert_fusion.6), channel_id=1, source_target_pairs={{16,0},{20,4},{24,8},{28,12},{17,1},{21,5},{25,9},{29,13},{18,2},{... | collective-permute-start | bytes 2359304 | tf_op jit(solution)/shard_map/ppermute | solution.py:77
  268.3 36.2 %collective-permute-start.28 = (bf16[2,512,384]{2,1,0:T(8,128)(2,1)}, bf16[2,512,384]{2,1,0:T(8,128)(2,1)}, u32[]{:S(2)}, u32[]{:S(2)}) collective-permute-start(bf16[2,512,384]{2,1,0:T(8,128)(2,1)} %add_convert_fusion.3), channel_id=1, source_target_pairs={{8,0},{12,4},{0,8},{4,12},{16,24},{20,28},{9,1},{13,5},{1,9},{5,13... | collective-permute-start | bytes 2359304 | tf_op jit(solution)/shard_map/ppermute | solution.py:77
  272.2 21.2 %collective-permute-start.18 = (bf16[128,768]{1,0:T(8,128)(2,1)}, bf16[128,768]{1,0:T(8,128)(2,1)}, u32[]{:S(2)}, u32[]{:S(2)}) collective-permute-start(bf16[128,768]{1,0:T(8,128)(2,1)} %get-tuple-element.169), channel_id=1, source_target_pairs={{0,28},{4,24},{8,20},{12,16},{16,12},{20,8},{24,4},{28,0},{1,29},{... | collective-permute-start | bytes 589832 | tf_op jit(solution)/shard_map/ppermute | solution.py:91
  298.0 17.2 %collective-permute-start.26 = (bf16[1,512,384]{2,1,0:T(8,128)(2,1)S(1)}, bf16[1,512,384]{2,1,0:T(8,128)(2,1)}, u32[]{:S(2)}, u32[]{:S(2)}) collective-permute-start(bf16[1,512,384]{2,1,0:T(8,128)(2,1)S(1)} %slice.499), channel_id=1, source_target_pairs={{8,0},{12,4},{0,8},{4,12},{24,16},{28,20},{9,1},{13,5},{1,9},{5,13... | collective-permute-start | bytes 1179656 | tf_op jit(solution)/shard_map/ppermute | solution.py:81
  350.9 15.2 %collective-permute-start.41 = (bf16[240,768]{1,0:T(8,128)(2,1)S(1)}, bf16[240,768]{1,0:T(8,128)(2,1)S(1)}, u32[]{:S(2)}, u32[]{:S(2)}) collective-permute-start(bf16[240,768]{1,0:T(8,128)(2,1)S(1)} %add_convert_fusion.15), channel_id=1, source_target_pairs={{0,8},{4,12},{8,0},{12,4},{16,24},{20,28},{24,16},{28,20},{1,9},{5... | collective-permute-start | bytes 1105928 | tf_op jit(solution)/shard_map/ppermute | solution.py:37
  356.8 27.8 %collective-permute-start.46 = (bf16[384,768]{1,0:T(8,128)(2,1)}, bf16[384,768]{1,0:T(8,128)(2,1)}, u32[]{:S(2)}, u32[]{:S(2)}) collective-permute-start(bf16[384,768]{1,0:T(8,128)(2,1)} %pad_maximum_fusion.14), channel_id=1, source_target_pairs={{0,4},{4,0},{8,12},{12,8},{16,20},{20,16},{24,28},{28,24},{1,5},{5... | collective-permute-start | bytes 1769480 | tf_op jit(solution)/shard_map/ppermute | solution.py:37
  367.2 20.3 %collective-permute-start.43 = (bf16[192,1536]{1,0:T(8,128)(2,1)}, bf16[192,1536]{1,0:T(8,128)(2,1)}, u32[]{:S(2)}, u32[]{:S(2)}) collective-permute-start(bf16[192,1536]{1,0:T(8,128)(2,1)} %pad_maximum_fusion.13), channel_id=1, source_target_pairs={{0,4},{4,0},{8,12},{12,8},{16,20},{20,16},{24,28},{28,24},{1,5},{5... | collective-permute-start | bytes 1769480 | tf_op jit(solution)/shard_map/ppermute | solution.py:37
  (91 other events, 611.5 us)
Sparse Core Ops, SparseCore 0:
  18.4 41.6 all-gather.4
  62.3 59.3 all-gather.6
  260.1 51.3 reduce-scatter.2
  333.0 36.8 reduce-scatter.4

commit v4 on v3

--- a/solution.py
+++ b/solution.py
@@ -533,6 +533,9 @@
     def parted(first, second, side):
         return jnp.where(side, second, first), jnp.where(side, first, second)
 
+    hidden, normed_pair, attended = [
+        after(held, grad_attended) for held in (hidden, normed_pair, attended)
+    ]
     proj_grad = dot(attended, grad_branch, ((1,), (0,))).astype(bf16)
     proj_grad = proj_grad.reshape(shards, 2, half_width, width)
     mine, sent = parted(proj_grad[:, 0], proj_grad[:, 1], odd)
@@ -612,15 +615,22 @@
     pull = jax.vjp(lambda v: normalized(v) * gain_one, inputs32)[1]
     input_grad = (grad_middle + pull(summed[:tokens])[0]).astype(bf16)
     sums = summed[tokens : tokens + vector_rows, :local_width]
-    for bit in range(cycle.bit_length() - 1):
+    sums = sums + swapped(sums, 0)
+    sums = after(sums, input_grad)
+    for bit in chip_bits:
         sums = sums + swapped(sums, bit)
+
+    layer_output = after(layer_output, normed_parts).reshape(seqs, piece, width)
+    layer_output = mirror_late(layer_output)
 
     cut = both.shape[0] - quarter
     out_grad = summed_over_chips(both[cut:], [bit for bit in chip_bits if bit != OUT_BIT])
     out_grad = jnp.concatenate(joined(out_grad.astype(bf16), OUT_BIT, out_side))
+    out_grad = after(out_grad, summed)
     out_grad = jnp.concatenate(pair_joined(out_grad, odd)).astype(f32)
     rest = summed_over_chips(both[:cut], [bit for bit in chip_bits if bit != FC_BIT])
     first, second = joined(rest.astype(bf16), FC_BIT, fc_side)
+    first, second = after(first, summed), after(second, summed)
     proj_grad = jnp.concatenate([first[local_width:], second[local_width:]])
     proj_grad = jnp.concatenate(pair_joined(proj_grad, odd)).astype(f32)
     fc_grad = jnp.concatenate([first[:local_width], second[:local_width]], axis=1)
@@ -663,7 +673,7 @@
     qkv_grad = jnp.concatenate(thirds, axis=1).astype(f32)
 
     return (
-        mirror_late(layer_output.reshape(seqs, piece, width)),
+        layer_output,
         mirror_late(input_grad.reshape(seqs, piece, width)),
         sums[0],
         sums[1],

time: 425 us -> 422 us (level)
  local copies, waits for them, and re-layouts: 32.6 us -> 43.1 us
  starting transfers between devices: 75.6 us -> 65.6 us
  waiting for transfers between devices: 126 us -> 121 us
    ppermute x4, waiting for transfers between devices: 26.4 us -> 15.3 us  [mirrored(): return lax.ppermute(block, 'ctx', [(i, n - 1 - i) for i in range(n)])]
    ppermute x35, waiting for transfers between devices: 54.2 us -> 43.7 us  [swapped(): return lax.ppermute(block, 'ctx', [(i, i ^ 1 << bit) for i in range(n)])]
    ppermute x2, waiting for transfers between devices: 0.01 us -> 10.2 us  [returned(): lax.ppermute(middle, 'ctx', pairs)]
    ppermute x35, starting transfers between devices: 29.2 us -> 21 us  [swapped(): return lax.ppermute(block, 'ctx', [(i, i ^ 1 << bit) for i in range(n)])]
    unnamed x129 -> x161, local copies, waits for them, and re-layouts: 5.82 us -> 9.89 us
  transfers between devices with their start and end apart: 54 -> 54, of which waited for: 25 -> 22; matrix products, arithmetic and copies ran while one was open for 23% -> 24% of each run, Pallas kernels for 15% -> 15%
where the time goes in v4:
time: 422 us; the launch traced here: 417 us
  waiting for transfers between devices  121 us (29%)
  starting transfers between devices  65.6 us (16%)
  other arithmetic  64.9 us (15%)
  Pallas kernels  63.6 us (15%)
  local copies, waits for them, and re-layouts  43.1 us (10%)
  matrix products  27.9 us (7%)
  between operations  15.7 us (4%)
  blocking collectives  15.2 us (4%)
    ppermute x35, waiting for transfers between devices, swapped(): return lax.ppermute(block, 'ctx', [(i, i ^ 1 << bit) for i in range(n)])  43.7 us
    pallas_call x2, Pallas kernels, attend(): pl.pallas_call(functools.partial(forward_kernel, heads, shards, order), o...  33 us
    pallas_call x2, Pallas kernels, attend_back(): pl.pallas_call(functools.partial(backward_kernel, heads, shards, order, f...  30.6 us
    dot_general x19, matrix products, dot(): lax.dot_general(a, b, ((contract[0], contract[1]), ((), ())), preferred_e...  27.9 us
    ppermute x35, starting transfers between devices, swapped(): return lax.ppermute(block, 'ctx', [(i, i ^ 1 << bit) for i in range(n)])  21 us
    ppermute x2, waiting for transfers between devices, spread(): lax.ppermute(held, 'ctx', tree_pairs(aparts, bit, order[-1:], late, False))  16.2 us
    ppermute x4, waiting for transfers between devices, mirrored(): return lax.ppermute(block, 'ctx', [(i, n - 1 - i) for i in range(n)])  15.3 us
    all_to_all x1, blocking collectives, body(): grad_heads = lax.all_to_all(grad_attended, 'shard', 0, 0, tiled=True)  15.2 us
  transfers between devices with their start and end apart: 54, of which 22 were waited for; matrix products, arithmetic and copies ran while one was open for 24% of the time, Pallas kernels for 15%

profile of v4, /device:TPU:0, one launch (start us, length us, event | category | flops | bytes accessed | tf_op | source)
XLA Modules:
  0.0 416.7 jit_solution(6308038558293245627)
XLA Ops:
  11.9 5.3 %collective-permute-done = bf16[128,768]{1,0:T(8,128)(2,1)S(1)} collective-permute-done((bf16[128,768]{1,0:T(8,128)(2,1)S(1)}, bf16[128,768]{1,0:T(8,128)(2,1)S(1)}, u32[]{:S(2)}, u32[]{:S(2)}) %collective-permute-start) | collective-permute-done | bytes 196640 | tf_op jit(solution)/shard_map/ppermute | solution.py:91
  20.5 5.7 %all-to-all-start = ((bf16[4,40,576]{2,1,0:T(8,128)(2,1)}), bf16[4,40,576]{2,1,0:T(8,128)(2,1)S(1)}, u32[]{:S(2)}, u32[]{:S(2)}) async-start(bf16[4,40,576]{2,1,0:T(8,128)(2,1)} %pad_maximum_fusion.28), calls=%async_computation | async-start | bytes 409600 | tf_op jit(solution)/shard_map/all_to_all | solution.py:417
  31.3 6.6 %all-to-all-done = bf16[4,40,576]{2,1,0:T(8,128)(2,1)S(1)} async-done(((bf16[4,40,576]{2,1,0:T(8,128)(2,1)}), bf16[4,40,576]{2,1,0:T(8,128)(2,1)S(1)}, u32[]{:S(2)}, u32[]{:S(2)}) %all-to-all-start) | async-done | bytes 184352 | tf_op jit(solution)/shard_map/all_to_all | solution.py:417
  49.4 10.8 %all-gather.5.cloned.1.call-done = bf16[8,128,768]{2,1,0:T(8,128)(2,1)} async-done(((bf16[2,128,768]{2,1,0:T(8,128)(2,1)}), bf16[8,128,768]{2,1,0:T(8,128)(2,1)}) %all-gather.5.cloned.1.call-update) | async-done | bytes 1572880 | tf_op jit(solution)/shard_map/all_gather | solution.py:388
  67.4 3.5 collective-permute-start.5
  73.0 7.4 %collective-permute-done.5 = bf16[1,512,384]{2,1,0:T(8,128)(2,1)S(1)} collective-permute-done((bf16[1,512,384]{2,1,0:T(8,128)(2,1)S(1)}, bf16[1,512,384]{2,1,0:T(8,128)(2,1)S(1)}, u32[]{:S(2)}, u32[]{:S(2)}) %collective-permute-start.5) | collective-permute-done | bytes 393248 | tf_op jit(solution)/shard_map/ppermute | solution.py:58
  80.6 4.3 %collective-permute-start.6 = (bf16[2,512,384]{2,1,0:T(8,128)(2,1)S(1)}, bf16[2,512,384]{2,1,0:T(8,128)(2,1)}, u32[]{:S(2)}, u32[]{:S(2)}) collective-permute-start(bf16[2,512,384]{2,1,0:T(8,128)(2,1)S(1)} %pad_maximum_fusion.8.refs_0_), channel_id=1, source_target_pairs={{0,16},{4,20},{8,24},{12,28},{1,17},{5,21},{9,25},{13,29},{2,18},{... | collective-permute-start | bytes 2359304 | tf_op jit(solution)/shard_map/ppermute | solution.py:62
  85.9 4.4 %collective-permute-start.10 = (bf16[2,512,384]{2,1,0:T(8,128)(2,1)}, bf16[2,512,384]{2,1,0:T(8,128)(2,1)}, u32[]{:S(2)}, u32[]{:S(2)}) collective-permute-start(bf16[2,512,384]{2,1,0:T(8,128)(2,1)} %pad_maximum_fusion.9.refs_0_), channel_id=1, source_target_pairs={{0,8},{4,12},{8,0},{12,4},{24,16},{28,20},{1,9},{5,13},{9,1},{13,5... | collective-permute-start | bytes 2359304 | tf_op jit(solution)/shard_map/ppermute | solution.py:62
  90.4 9.5 %collective-permute-done.6.refs_1_ = bf16[2,512,384]{2,1,0:T(8,128)(2,1)} collective-permute-done((bf16[2,512,384]{2,1,0:T(8,128)(2,1)S(1)}, bf16[2,512,384]{2,1,0:T(8,128)(2,1)}, u32[]{:S(2)}, u32[]{:S(2)}) %collective-permute-start.6) | collective-permute-done | bytes 786464 | tf_op jit(solution)/shard_map/ppermute | solution.py:62
  100.4 6.7 %collective-permute-done.10.refs_1_ = bf16[2,512,384]{2,1,0:T(8,128)(2,1)} collective-permute-done((bf16[2,512,384]{2,1,0:T(8,128)(2,1)}, bf16[2,512,384]{2,1,0:T(8,128)(2,1)}, u32[]{:S(2)}, u32[]{:S(2)}) %collective-permute-start.10) | collective-permute-done | bytes 786464 | tf_op jit(solution)/shard_map/ppermute | solution.py:62
  107.1 5.0 %attention_forward.2 = (bf16[4,192,128]{2,1,0:T(8,128)(2,1)}, f32[192,512]{1,0:T(8,128)}, f32[3,1,512]{2,1,0:T(1,128)}) custom-call(s32[1]{0:T(128)} %bitcast.3.info, bf16[512,192]{1,0:T(8,128)(2,1)} %fusion.15.q_ref, bf16[2,512,384]{2,1,0:T(8,128)(2,1)} %copy-done.33, bf16[2,512,384]{2,1,0:T(8,128)(2,1)} %collective-permute-done.6.refs_1_, ...), custom_call_target="tpu_custom_call" | custom-call | flops 3623878656 | bytes 3932160 | tf_op jit(solution)/shard_map/attention_forward/pallas_call | solution.py:289
  112.2 28.0 %attention_forward.3 = (bf16[4,192,128]{2,1,0:T(8,128)(2,1)}, f32[192,512]{1,0:T(8,128)}, f32[3,1,512]{2,1,0:T(1,128)}) custom-call(s32[1]{0:T(128)} %bitcast.19.info, bf16[512,192]{1,0:T(8,128)(2,1)} %fusion.16.q_ref, bf16[2,512,384]{2,1,0:T(8,128)(2,1)} %pad_maximum_fusion.9.refs_0_, bf16[2,512,384]{2,1,0:T(8,128)(2,1)} %collective-permute-done.10.refs_1_, ...), custom_call_target="tpu_custom_call" | custom-call | flops 3623878656 | bytes 3932160 | tf_op jit(solution)/shard_map/attention_forward/pallas_call | solution.py:289
  155.9 19.0 %collective-permute-done.13 = bf16[768,768]{1,0:T(8,128)(2,1)} collective-permute-done((bf16[768,768]{1,0:T(8,128)(2,1)}, bf16[768,768]{1,0:T(8,128)(2,1)}, u32[]{:S(2)}, u32[]{:S(2)}) %collective-permute-start.13) | collective-permute-done | bytes 1179680 | tf_op jit(solution)/shard_map/ppermute | solution.py:37
  187.3 5.1 %convert_reduce_fusion = (bf16[1536]{0:T(1024)(128)(2,1)}, bf16[512,1536]{1,0:T(8,128)(2,1)S(1)}) fusion(f32[512,1536]{1,0:T(8,128)S(1)} %get-tuple-element.221, bf16[1536,768]{1,0:T(8,128)(2,1)S(1)} %bitcast.260, bf16[256,768]{1,0:T(8,128)(2,1)} %collective-permute-done.18, bf16[256,768]{1,0:T(8,128)(2,1)S(1)} %bitcast.250), kind=kOutput, calls=%fused_computation.12 | convolution fusion | flops 1226832384 | bytes 7867392 | tf_op jit(solution)/shard_map/dot_general | solution.py:100
  218.5 15.2 %all_to_all.20.go_ref = bf16[4,192,256]{2,1,0:T(8,128)(2,1)} all-to-all(bf16[4,192,256]{2,1,0:T(8,128)(2,1)S(1)} %bitcast.265), channel_id=1, replica_groups=mesh['ctx'=8,'shard'=4] {'shard'}, dimensions={0} | all-to-all | bytes 786432 | tf_op jit(solution)/shard_map/all_to_all | solution.py:530
  233.7 22.8 %attention_backward.3 = (bf16[512,192]{1,0:T(8,128)(2,1)}, bf16[2,512,384]{2,1,0:T(8,128)(2,1)}, bf16[2,512,384]{2,1,0:T(8,128)(2,1)}, bf16[4,512,384]{2,1,0:T(8,128)(2,1)}) custom-call(s32[1]{0:T(128)} %bitcast.19.info, bf16[512,192]{1,0:T(8,128)(2,1)} %fusion.16.q_ref, f32[192,512]{1,0:T(8,128)} %get-tuple-element.79.out_ref, ...), custom_call_target="tpu_custom_call" | custom-call | flops 2264924160 | bytes 7864320 | tf_op jit(solution)/shard_map/attention_backward/pallas_call | solution.py:321
  256.6 7.8 %attention_backward.2 = (bf16[512,192]{1,0:T(8,128)(2,1)}, bf16[2,512,384]{2,1,0:T(8,128)(2,1)}, bf16[2,512,384]{2,1,0:T(8,128)(2,1)}, bf16[4,512,384]{2,1,0:T(8,128)(2,1)}) custom-call(s32[1]{0:T(128)} %bitcast.3.info, bf16[512,192]{1,0:T(8,128)(2,1)} %fusion.15.q_ref, f32[192,512]{1,0:T(8,128)} %get-tuple-element.68.out_ref, ...), custom_call_target="tpu_custom_call" | custom-call | flops 2264924160 | bytes 7864320 | tf_op jit(solution)/shard_map/attention_backward/pallas_call | solution.py:321
  287.9 9.6 %collective-permute-done.27 = bf16[2,512,384]{2,1,0:T(8,128)(2,1)} collective-permute-done((bf16[2,512,384]{2,1,0:T(8,128)(2,1)}, bf16[2,512,384]{2,1,0:T(8,128)(2,1)}, u32[]{:S(2)}, u32[]{:S(2)}) %collective-permute-start.27) | collective-permute-done | bytes 786464 | tf_op jit(solution)/shard_map/ppermute | solution.py:77
  305.5 4.0 collective-permute-start.25
  312.9 4.7 %collective-permute-done.25 = bf16[1,512,384]{2,1,0:T(8,128)(2,1)} collective-permute-done((bf16[1,512,384]{2,1,0:T(8,128)(2,1)S(1)}, bf16[1,512,384]{2,1,0:T(8,128)(2,1)}, u32[]{:S(2)}, u32[]{:S(2)}) %collective-permute-start.25) | collective-permute-done | bytes 393248 | tf_op jit(solution)/shard_map/ppermute | solution.py:81
  345.3 7.1 %collective-permute-done.29 = bf16[128,768]{1,0:T(8,128)(2,1)S(1)} collective-permute-done((bf16[128,768]{1,0:T(8,128)(2,1)S(1)}, bf16[128,768]{1,0:T(8,128)(2,1)S(1)}, u32[]{:S(2)}, u32[]{:S(2)}) %collective-permute-start.29) | collective-permute-done | bytes 196640 | tf_op jit(solution)/shard_map/ppermute | solution.py:91
  354.9 6.3 %collective-permute-done.35 = bf16[4,48,576]{2,1,0:T(8,128)(2,1)S(1)} collective-permute-done((bf16[4,48,576]{2,1,0:T(8,128)(2,1)S(1)}, bf16[4,48,576]{2,1,0:T(8,128)(2,1)S(1)}, u32[]{:S(2)}, u32[]{:S(2)}) %collective-permute-start.35) | collective-permute-done | bytes 221216 | tf_op jit(solution)/shard_map/ppermute | solution.py:37
  362.7 5.4 %collective-permute-done.36 = bf16[4,24,576]{2,1,0:T(8,128)(2,1)S(1)} collective-permute-done((bf16[4,24,576]{2,1,0:T(8,128)(2,1)S(1)}, bf16[4,24,576]{2,1,0:T(8,128)(2,1)S(1)}, u32[]{:S(2)}, u32[]{:S(2)}) %collective-permute-start.36) | collective-permute-done | bytes 110624 | tf_op jit(solution)/shard_map/ppermute | solution.py:37
  372.2 5.8 %all-to-all-done.3 = bf16[4,24,576]{2,1,0:T(8,128)(2,1)S(1)} async-done(((bf16[4,24,576]{2,1,0:T(8,128)(2,1)}), bf16[4,24,576]{2,1,0:T(8,128)(2,1)S(1)}, u32[]{:S(2)}, u32[]{:S(2)}) %all-to-all-start.3) | async-done | bytes 110624 | tf_op jit(solution)/shard_map/all_to_all | solution.py:657
  (460 shorter events, 191.1 us)
Async XLA Ops:
  7.3 52.8 %all-gather.5.cloned.1.call-start = ((), (), s32[]{:S(2)}) async-start(), calls=%async_computation.8 | async-start | bytes 1966080 | tf_op jit(solution)/shard_map/all_gather | solution.py:388
  20.5 17.4 %all-to-all-start = ((bf16[4,40,576]{2,1,0:T(8,128)(2,1)}), bf16[4,40,576]{2,1,0:T(8,128)(2,1)S(1)}, u32[]{:S(2)}, u32[]{:S(2)}) async-start(bf16[4,40,576]{2,1,0:T(8,128)(2,1)} %pad_maximum_fusion.28), calls=%async_computation | async-start | bytes 409600 | tf_op jit(solution)/shard_map/all_to_all | solution.py:417
  26.2 115.7 %all-gather.7.cloned.1.call-start = ((), (), s32[]{:S(2)}) async-start(), calls=%async_computation.9 | async-start | bytes 3686400 | tf_op jit(solution)/shard_map/all_gather | solution.py:467
  65.4 19.4 %collective-permute-start.9 = (bf16[1,512,384]{2,1,0:T(8,128)(2,1)S(1)}, bf16[1,512,384]{2,1,0:T(8,128)(2,1)S(1)}, u32[]{:S(2)}, u32[]{:S(2)}) collective-permute-start(bf16[1,512,384]{2,1,0:T(8,128)(2,1)S(1)} %fusion.13), channel_id=1, source_target_pairs={{16,0},{20,4},{24,8},{28,12},{17,1},{21,5},{25,9},{29,13},{18,2},{... | collective-permute-start | bytes 1179656 | tf_op jit(solution)/shard_map/ppermute | solution.py:58
  80.6 19.3 %collective-permute-start.6 = (bf16[2,512,384]{2,1,0:T(8,128)(2,1)S(1)}, bf16[2,512,384]{2,1,0:T(8,128)(2,1)}, u32[]{:S(2)}, u32[]{:S(2)}) collective-permute-start(bf16[2,512,384]{2,1,0:T(8,128)(2,1)S(1)} %pad_maximum_fusion.8.refs_0_), channel_id=1, source_target_pairs={{0,16},{4,20},{8,24},{12,28},{1,17},{5,21},{9,25},{13,29},{2,18},{... | collective-permute-start | bytes 2359304 | tf_op jit(solution)/shard_map/ppermute | solution.py:62
  85.9 21.2 %collective-permute-start.10 = (bf16[2,512,384]{2,1,0:T(8,128)(2,1)}, bf16[2,512,384]{2,1,0:T(8,128)(2,1)}, u32[]{:S(2)}, u32[]{:S(2)}) collective-permute-start(bf16[2,512,384]{2,1,0:T(8,128)(2,1)} %pad_maximum_fusion.9.refs_0_), channel_id=1, source_target_pairs={{0,8},{4,12},{8,0},{12,4},{24,16},{28,20},{1,9},{5,13},{9,1},{13,5... | collective-permute-start | bytes 2359304 | tf_op jit(solution)/shard_map/ppermute | solution.py:62
  90.3 16.8 %collective-permute-start.7 = (bf16[2,512,384]{2,1,0:T(8,128)(2,1)S(1)}, bf16[2,512,384]{2,1,0:T(8,128)(2,1)}, u32[]{:S(2)}, u32[]{:S(2)}) collective-permute-start(bf16[2,512,384]{2,1,0:T(8,128)(2,1)S(1)} %pad_maximum_fusion.8.refs_0_), channel_id=1, source_target_pairs={{0,4},{4,0},{8,12},{12,8},{16,20},{20,16},{24,28},{28,24},{1,5},{5... | collective-permute-start | bytes 2359304 | tf_op jit(solution)/shard_map/ppermute | solution.py:37
  146.2 28.7 %collective-permute-start.13 = (bf16[768,768]{1,0:T(8,128)(2,1)}, bf16[768,768]{1,0:T(8,128)(2,1)}, u32[]{:S(2)}, u32[]{:S(2)}) collective-permute-start(bf16[768,768]{1,0:T(8,128)(2,1)} %bitcast.23), channel_id=1, source_target_pairs={{0,8},{4,12},{8,0},{12,4},{16,24},{20,28},{24,16},{28,20},{1,9},{5... | collective-permute-start | bytes 3538952 | tf_op jit(solution)/shard_map/ppermute | solution.py:37
  149.7 37.6 %collective-permute-start.18 = (bf16[256,768]{1,0:T(8,128)(2,1)S(1)}, bf16[256,768]{1,0:T(8,128)(2,1)}, u32[]{:S(2)}, u32[]{:S(2)}) collective-permute-start(bf16[256,768]{1,0:T(8,128)(2,1)S(1)} %bitcast.249), channel_id=1, source_target_pairs={{0,4},{4,0},{8,12},{12,8},{16,20},{20,16},{24,28},{28,24},{1,5},{5... | collective-permute-start | bytes 1179656 | tf_op jit(solution)/shard_map/ppermute | solution.py:37
  150.0 28.3 %all-to-all-start.1 = ((bf16[4,192,256]{2,1,0:T(8,128)(2,1)}), bf16[4,192,256]{2,1,0:T(8,128)(2,1)S(1)}, u32[]{:S(2)}, u32[]{:S(2)}) async-start(bf16[4,192,256]{2,1,0:T(8,128)(2,1)} %pad_maximum_fusion.23), calls=%async_computation.1 | async-start | bytes 786432 | tf_op jit(solution)/shard_map/all_to_all | solution.py:501
  153.5 178.7 %reduce-scatter.3.cloned.1.call-start = ((), (), s32[]{:S(2)}) async-start(), calls=%async_computation.6 | async-start | bytes 3317760 | tf_op jit(solution)/shard_map/reduce_scatter | solution.py:568
  153.5 28.5 %collective-permute-start.16 = (bf16[4,192,768]{2,1,0:T(8,128)(2,1)}, bf16[4,192,768]{2,1,0:T(8,128)(2,1)}, u32[]{:S(2)}, u32[]{:S(2)}) collective-permute-start(bf16[4,192,768]{2,1,0:T(8,128)(2,1)} %get-tuple-element.67), channel_id=1, source_target_pairs={{0,16},{4,20},{8,24},{12,28},{16,0},{20,4},{24,8},{28,12},{1,17},{... | collective-permute-start | bytes 3538952 | tf_op jit(solution)/shard_map/ppermute | solution.py:37
  213.0 54.1 %collective-permute-start.23 = (bf16[4,192,768]{2,1,0:T(8,128)(2,1)}, bf16[4,192,768]{2,1,0:T(8,128)(2,1)}, u32[]{:S(2)}, u32[]{:S(2)}) collective-permute-start(bf16[4,192,768]{2,1,0:T(8,128)(2,1)} %select_bitcast_fusion), channel_id=1, source_target_pairs={{0,16},{4,20},{8,24},{12,28},{16,0},{20,4},{24,8},{28,12},{1,17},{... | collective-permute-start | bytes 3538952 | tf_op jit(solution)/shard_map/ppermute | solution.py:37
  216.9 51.8 %collective-permute-start.22 = (bf16[4,240,768]{2,1,0:T(8,128)(2,1)}, bf16[4,240,768]{2,1,0:T(8,128)(2,1)}, u32[]{:S(2)}, u32[]{:S(2)}) collective-permute-start(bf16[4,240,768]{2,1,0:T(8,128)(2,1)} %broadcast_select_fusion), channel_id=1, source_target_pairs={{0,8},{4,12},{8,0},{12,4},{16,24},{20,28},{24,16},{28,20},{1,9},{5... | collective-permute-start | bytes 4423688 | tf_op jit(solution)/shard_map/ppermute | solution.py:37
  256.6 16.8 %collective-permute-start.26 = (bf16[4,512,384]{2,1,0:T(8,128)(2,1)}, bf16[4,512,384]{2,1,0:T(8,128)(2,1)}, u32[]{:S(2)}, u32[]{:S(2)}) collective-permute-start(bf16[4,512,384]{2,1,0:T(8,128)(2,1)} %get-tuple-element.86), channel_id=1, source_target_pairs={{0,4},{4,0},{8,12},{12,8},{16,20},{20,16},{24,28},{28,24},{1,5},{5... | collective-permute-start | bytes 4718600 | tf_op jit(solution)/shard_map/ppermute | solution.py:37
  264.4 14.8 %collective-permute-start.21 = (bf16[4,512,384]{2,1,0:T(8,128)(2,1)}, bf16[4,512,384]{2,1,0:T(8,128)(2,1)}, u32[]{:S(2)}, u32[]{:S(2)}) collective-permute-start(bf16[4,512,384]{2,1,0:T(8,128)(2,1)} %get-tuple-element.77), channel_id=1, source_target_pairs={{0,4},{4,0},{8,12},{12,8},{16,20},{20,16},{24,28},{28,24},{1,5},{5... | collective-permute-start | bytes 4718600 | tf_op jit(solution)/shard_map/ppermute | solution.py:37
  272.4 111.2 %reduce-scatter.5.cloned.1.call-start = ((), (), s32[]{:S(2)}) async-start(), calls=%async_computation.7 | async-start | bytes 2088960 | tf_op jit(solution)/shard_map/reduce_scatter | solution.py:614
  275.7 21.8 %collective-permute-start.27 = (bf16[2,512,384]{2,1,0:T(8,128)(2,1)}, bf16[2,512,384]{2,1,0:T(8,128)(2,1)}, u32[]{:S(2)}, u32[]{:S(2)}) collective-permute-start(bf16[2,512,384]{2,1,0:T(8,128)(2,1)} %add_convert_fusion.3), channel_id=1, source_target_pairs={{8,0},{12,4},{0,8},{4,12},{16,24},{20,28},{9,1},{13,5},{1,9},{5,13... | collective-permute-start | bytes 2359304 | tf_op jit(solution)/shard_map/ppermute | solution.py:77
  281.5 21.4 %collective-permute-start.24 = (bf16[2,512,384]{2,1,0:T(8,128)(2,1)}, bf16[2,512,384]{2,1,0:T(8,128)(2,1)}, u32[]{:S(2)}, u32[]{:S(2)}) collective-permute-start(bf16[2,512,384]{2,1,0:T(8,128)(2,1)} %add_convert_fusion.6), channel_id=1, source_target_pairs={{16,0},{20,4},{24,8},{28,12},{17,1},{21,5},{25,9},{29,13},{18,2},{... | collective-permute-start | bytes 2359304 | tf_op jit(solution)/shard_map/ppermute | solution.py:77
  338.6 15.0 %collective-permute-start.44 = (bf16[192,768]{1,0:T(8,128)(2,1)}, bf16[192,768]{1,0:T(8,128)(2,1)}, u32[]{:S(2)}, u32[]{:S(2)}) collective-permute-start(bf16[192,768]{1,0:T(8,128)(2,1)} %slice_bitcast_fusion.8), channel_id=1, source_target_pairs={{0,8},{4,12},{8,0},{12,4},{16,24},{20,28},{24,16},{28,20},{1,9},{5... | collective-permute-start | bytes 884744 | tf_op jit(solution)/shard_map/ppermute | solution.py:37
  344.5 16.9 %collective-permute-start.40 = (bf16[240,768]{1,0:T(8,128)(2,1)S(1)}, bf16[240,768]{1,0:T(8,128)(2,1)S(1)}, u32[]{:S(2)}, u32[]{:S(2)}) collective-permute-start(bf16[240,768]{1,0:T(8,128)(2,1)S(1)} %slice_bitcast_fusion.7), channel_id=1, source_target_pairs={{0,16},{4,20},{8,24},{12,28},{16,0},{20,4},{24,8},{28,12},{1,17},{... | collective-permute-start | bytes 1105928 | tf_op jit(solution)/shard_map/ppermute | solution.py:37
  354.6 17.5 %collective-permute-start.45 = (bf16[192,768]{1,0:T(8,128)(2,1)S(1)}, bf16[192,768]{1,0:T(8,128)(2,1)S(1)}, u32[]{:S(2)}, u32[]{:S(2)}) collective-permute-start(bf16[192,768]{1,0:T(8,128)(2,1)S(1)} %add_convert_fusion.16), channel_id=1, source_target_pairs={{0,16},{4,20},{8,24},{12,28},{16,0},{20,4},{24,8},{28,12},{1,17},{... | collective-permute-start | bytes 884744 | tf_op jit(solution)/shard_map/ppermute | solution.py:37
  361.5 17.4 %collective-permute-start.41 = (bf16[240,768]{1,0:T(8,128)(2,1)S(1)}, bf16[240,768]{1,0:T(8,128)(2,1)}, u32[]{:S(2)}, u32[]{:S(2)}) collective-permute-start(bf16[240,768]{1,0:T(8,128)(2,1)S(1)} %add_convert_fusion.15), channel_id=1, source_target_pairs={{0,8},{4,12},{8,0},{12,4},{16,24},{20,28},{24,16},{28,20},{1,9},{5... | collective-permute-start | bytes 1105928 | tf_op jit(solution)/shard_map/ppermute | solution.py:37
  389.9 13.5 %collective-permute-start.38 = (bf16[48,2304]{1,0:T(8,128)(2,1)S(1)}, bf16[48,2304]{1,0:T(8,128)(2,1)S(1)}, u32[]{:S(2)}, u32[]{:S(2)}) collective-permute-start(bf16[48,2304]{1,0:T(8,128)(2,1)S(1)} %copy-done.32), channel_id=1, source_target_pairs={{0,8},{4,12},{8,0},{12,4},{16,24},{20,28},{24,16},{28,20},{1,9},{5... | collective-permute-start | bytes 663560 | tf_op jit(solution)/shard_map/ppermute | solution.py:37
  (107 other events, 769.0 us)
Sparse Core Ops, SparseCore 0:
  18.4 41.6 all-gather.4
  62.3 59.3 all-gather.6
  272.6 51.1 reduce-scatter.2
  336.9 35.2 reduce-scatter.4

commit v5 on v4

--- a/solution.py
+++ b/solution.py
@@ -72,13 +72,14 @@
 def returned(near, middle, far, aparts, order, late, before):
     received = swapped(far, 0)
     count = near.shape[0]
-    middle = after(added(middle, received[count:]), *before)
+    middle = added(middle, received[count:])
     pairs = tree_pairs(aparts[:count], order[-2], order[-1:], late, True)
     near = added(added(near, received[:count]), lax.ppermute(middle, "ctx", pairs))
     for bit in order[:-2][::-1]:
         count = near.shape[0] // 2
         pairs = tree_pairs(aparts[:count], bit, order[order.index(bit) + 1 :], late, True)
-        near = added(near[:count], lax.ppermute(near[count:], "ctx", pairs))
+        sent = after(near[count:], *before)
+        near = added(near[:count], lax.ppermute(sent, "ctx", pairs))
     return near[0]
 
 
@@ -384,8 +385,6 @@
         return jnp.stack([mirrored(held[s]) if late[s] else held[s] for s in range(seqs)])
 
     layer_input = mirror_late(layer_input)
-    grad_output = mirror_late(grad_output)
-    gathered = lax.all_gather(layer_input, "shard", axis=0)
 
     def by_heads(weight):
         parts = []
@@ -414,15 +413,13 @@
     )
     vector_rows = packed.shape[0]
     packed = jnp.pad(packed, ((0, 16 - vector_rows), (0, 3 * group - local_width)))
-    moved = lax.all_to_all(
-        jnp.concatenate(
-            [by_heads(weight_share), jnp.broadcast_to(packed, (shards,) + packed.shape)], axis=1
-        ),
-        "shard",
-        0,
-        0,
-        tiled=True,
-    )
+    moved = jnp.concatenate(
+        [by_heads(weight_share), jnp.broadcast_to(packed, (shards,) + packed.shape)], axis=1
+    )
+    layer_input, grad_output, moved = lax.optimization_barrier((layer_input, grad_output, moved))
+    grad_output = mirror_late(grad_output)
+    gathered = lax.all_gather(layer_input, "shard", axis=0)
+    moved = lax.all_to_all(moved, "shard", 0, 0, tiled=True)
     small = moved[:, share : share + vector_rows, :local_width].astype(f32)
     qkv_own = moved[:, :share]
     for bit in joins:
@@ -581,29 +578,24 @@
     fc_add_part = jnp.where(jnp.arange(2)[None, :, None] == odd, fc_add_part, 0.0)
 
     def all_heads(vector):
-        return lax.dynamic_update_slice_in_dim(
-            jnp.zeros((padded,), f32), vector, shard_at * group, 0
-        )[:width]
+        own = jnp.arange(shards)[:, None] == shard_at
+        return jnp.where(own, vector[None, :], 0.0).reshape(padded)[:width]
 
     query_sum = sum(jnp.sum(low.astype(f32), axis=0) for low in query_low)
     value_sum = sum(jnp.sum(low[:, group:].astype(f32), axis=0) for low in kv_low)
-    vectors = jnp.stack(
-        [
-            gain_one_grad,
-            shift_one_grad,
-            all_heads(query_sum),
-            all_heads(value_sum),
-            jnp.sum(grad_branch.astype(f32), axis=0),
-            gain_two_grad,
-            shift_two_grad,
-            jnp.sum(grads32, axis=0),
-        ]
-    )
+    vectors = [
+        gain_one_grad,
+        shift_one_grad,
+        all_heads(query_sum),
+        all_heads(value_sum),
+        jnp.sum(grad_branch.astype(f32), axis=0),
+        gain_two_grad,
+        shift_two_grad,
+        jnp.sum(grads32, axis=0),
+    ]
     vectors = jnp.concatenate(
-        [
-            vectors.reshape(8, shards, local_width).transpose(1, 0, 2),
-            fc_add_part.reshape(shards, -1, local_width),
-        ],
+        [vector.reshape(shards, 1, local_width) for vector in vectors]
+        + [fc_add_part.reshape(shards, -1, local_width)],
         axis=1,
     ).astype(bf16)
     vectors = jnp.pad(vectors, ((0, 0), (0, 16 - vector_rows), (0, width - local_width)))
@@ -620,8 +612,10 @@
     for bit in chip_bits:
         sums = sums + swapped(sums, bit)
 
-    layer_output = after(layer_output, normed_parts).reshape(seqs, piece, width)
-    layer_output = mirror_late(layer_output)
+    results = jnp.stack(
+        [part.reshape(seqs, piece, width) for part in (layer_output, input_grad)], axis=1
+    )
+    results = [mirrored(results[s]) if late[s] else results[s] for s in range(seqs)]
 
     cut = both.shape[0] - quarter
     out_grad = summed_over_chips(both[cut:], [bit for bit in chip_bits if bit != OUT_BIT])
@@ -673,8 +667,8 @@
     qkv_grad = jnp.concatenate(thirds, axis=1).astype(f32)
 
     return (
-        layer_output,
-        mirror_late(input_grad.reshape(seqs, piece, width)),
+        jnp.stack([part[0] for part in results]),
+        jnp.stack([part[1] for part in results]),
         sums[0],
         sums[1],
         qkv_grad,

time: 422 us -> 419 us (level)
  waiting for transfers between devices: 121 us -> 127 us
  starting transfers between devices: 65.6 us -> 60.5 us
    ppermute x4 -> x3, waiting for transfers between devices: 15.3 us -> 0.01 us  [mirrored(): return lax.ppermute(block, 'ctx', [(i, n - 1 - i) for i in range(n)])]
    ppermute x35, waiting for transfers between devices: 43.7 us -> 57 us  [swapped(): return lax.ppermute(block, 'ctx', [(i, i ^ 1 << bit) for i in range(n)])]
    another operation x11 -> x0, local copies, waits for them, and re-layouts: 8.65 us -> none  [the longest x9 6.77 us: body(): jnp.stack([gain_one_grad, shift_one_grad, all_heads(query_sum), all_heads...]
    another operation x8, local copies, waits for them, and re-layouts: 0.04 us -> 5.26 us  [body(): jnp.stack([attn_gain, attn_shift, query_bias, value_bias, proj_bias, mlp_...]
    reshape x0 -> x4, local copies, waits for them, and re-layouts: none -> 4.68 us  [body(): vector.reshape(shards, 1, local_width)]
    unnamed x161 -> x133, local copies, waits for them, and re-layouts: 9.89 us -> 9.46 us
  transfers between devices with their start and end apart: 54 -> 53, of which waited for: 22 -> 21; matrix products, arithmetic and copies ran while one was open for 24% -> 23% of each run, Pallas kernels for 15% -> 15%
where the time goes in v5:
time: 419 us; the launch traced here: 414 us
  waiting for transfers between devices  127 us (30%)
  Pallas kernels  63.6 us (15%)
  other arithmetic  62.4 us (15%)
  starting transfers between devices  60.5 us (14%)
  local copies, waits for them, and re-layouts  43.1 us (10%)
  matrix products  26.4 us (6%)
  blocking collectives  15.8 us (4%)
  between operations  15.5 us (4%)
    ppermute x35, waiting for transfers between devices, swapped(): return lax.ppermute(block, 'ctx', [(i, i ^ 1 << bit) for i in range(n)])  57 us
    pallas_call x2, Pallas kernels, attend(): pl.pallas_call(functools.partial(forward_kernel, heads, shards, order), o...  33 us
    pallas_call x2, Pallas kernels, attend_back(): pl.pallas_call(functools.partial(backward_kernel, heads, shards, order, f...  30.6 us
    dot_general x19, matrix products, dot(): lax.dot_general(a, b, ((contract[0], contract[1]), ((), ())), preferred_e...  26.4 us
    ppermute x35, starting transfers between devices, swapped(): return lax.ppermute(block, 'ctx', [(i, i ^ 1 << bit) for i in range(n)])  20.8 us
    ppermute x2, waiting for transfers between devices, spread(): lax.ppermute(held, 'ctx', tree_pairs(aparts, bit, order[-1:], late, False))  16.2 us
    all_to_all x1, blocking collectives, body(): grad_heads = lax.all_to_all(grad_attended, 'shard', 0, 0, tiled=True)  15.8 us
    convert_element_type x10, other arithmetic, added(): return (first.astype(f32) + second.astype(f32)).astype(bf16)  12.9 us
  transfers between devices with their start and end apart: 53, of which 21 were waited for; matrix products, arithmetic and copies ran while one was open for 23% of the time, Pallas kernels for 15%

profile of v5, /device:TPU:0, one launch (start us, length us, event | category | flops | bytes accessed | tf_op | source)
XLA Modules:
  0.0 413.8 jit_solution(17912018137164975600)
XLA Ops:
  21.7 4.9 %all-to-all-start = ((bf16[4,40,576]{2,1,0:T(8,128)(2,1)}), bf16[4,40,576]{2,1,0:T(8,128)(2,1)S(1)}, u32[]{:S(2)}, u32[]{:S(2)}) async-start(bf16[4,40,576]{2,1,0:T(8,128)(2,1)} %pad_maximum_fusion.29), calls=%async_computation | async-start | bytes 409600 | tf_op jit(solution)/shard_map/all_to_all | solution.py:422
  28.1 10.8 %all-to-all-done = bf16[4,40,576]{2,1,0:T(8,128)(2,1)S(1)} async-done(((bf16[4,40,576]{2,1,0:T(8,128)(2,1)}), bf16[4,40,576]{2,1,0:T(8,128)(2,1)S(1)}, u32[]{:S(2)}, u32[]{:S(2)}) %all-to-all-start) | async-done | bytes 184352 | tf_op jit(solution)/shard_map/all_to_all | solution.py:422
  39.3 4.7 %collective-permute-done.1 = bf16[4,24,576]{2,1,0:T(8,128)(2,1)S(1)} collective-permute-done((bf16[4,24,576]{2,1,0:T(8,128)(2,1)S(1)}, bf16[4,24,576]{2,1,0:T(8,128)(2,1)S(1)}, u32[]{:S(2)}, u32[]{:S(2)}) %collective-permute-start.1) | collective-permute-done | bytes 110624 | tf_op jit(solution)/shard_map/ppermute | solution.py:37
  45.5 4.8 %collective-permute-done.2 = bf16[4,48,576]{2,1,0:T(8,128)(2,1)S(1)} collective-permute-done((bf16[4,48,576]{2,1,0:T(8,128)(2,1)S(1)}, bf16[4,48,576]{2,1,0:T(8,128)(2,1)S(1)}, u32[]{:S(2)}, u32[]{:S(2)}) %collective-permute-start.2) | collective-permute-done | bytes 221216 | tf_op jit(solution)/shard_map/ppermute | solution.py:37
  50.4 10.6 %all-gather.5.cloned.1.call-done = bf16[8,128,768]{2,1,0:T(8,128)(2,1)} async-done(((bf16[2,128,768]{2,1,0:T(8,128)(2,1)}), bf16[8,128,768]{2,1,0:T(8,128)(2,1)}) %all-gather.5.cloned.1.call-update) | async-done | bytes 1572880 | tf_op jit(solution)/shard_map/all_gather | solution.py:421
  72.9 8.4 %collective-permute-done.5 = bf16[1,512,384]{2,1,0:T(8,128)(2,1)S(1)} collective-permute-done((bf16[1,512,384]{2,1,0:T(8,128)(2,1)S(1)}, bf16[1,512,384]{2,1,0:T(8,128)(2,1)S(1)}, u32[]{:S(2)}, u32[]{:S(2)}) %collective-permute-start.5) | collective-permute-done | bytes 393248 | tf_op jit(solution)/shard_map/ppermute | solution.py:58
  85.8 4.4 %collective-permute-start.10 = (bf16[2,512,384]{2,1,0:T(8,128)(2,1)}, bf16[2,512,384]{2,1,0:T(8,128)(2,1)}, u32[]{:S(2)}, u32[]{:S(2)}) collective-permute-start(bf16[2,512,384]{2,1,0:T(8,128)(2,1)} %pad_maximum_fusion.9.refs_0_), channel_id=1, source_target_pairs={{0,8},{4,12},{8,0},{12,4},{24,16},{28,20},{1,9},{5,13},{9,1},{13,5... | collective-permute-start | bytes 2359304 | tf_op jit(solution)/shard_map/ppermute | solution.py:62
  90.3 9.5 %collective-permute-done.6.refs_1_ = bf16[2,512,384]{2,1,0:T(8,128)(2,1)} collective-permute-done((bf16[2,512,384]{2,1,0:T(8,128)(2,1)S(1)}, bf16[2,512,384]{2,1,0:T(8,128)(2,1)}, u32[]{:S(2)}, u32[]{:S(2)}) %collective-permute-start.6) | collective-permute-done | bytes 786464 | tf_op jit(solution)/shard_map/ppermute | solution.py:62
  100.3 6.7 %collective-permute-done.10.refs_1_ = bf16[2,512,384]{2,1,0:T(8,128)(2,1)} collective-permute-done((bf16[2,512,384]{2,1,0:T(8,128)(2,1)}, bf16[2,512,384]{2,1,0:T(8,128)(2,1)}, u32[]{:S(2)}, u32[]{:S(2)}) %collective-permute-start.10) | collective-permute-done | bytes 786464 | tf_op jit(solution)/shard_map/ppermute | solution.py:62
  107.0 5.0 %attention_forward.2 = (bf16[4,192,128]{2,1,0:T(8,128)(2,1)}, f32[192,512]{1,0:T(8,128)}, f32[3,1,512]{2,1,0:T(1,128)}) custom-call(s32[1]{0:T(128)} %bitcast.7.info, bf16[512,192]{1,0:T(8,128)(2,1)} %fusion.15.q_ref, bf16[2,512,384]{2,1,0:T(8,128)(2,1)} %copy-done.30, bf16[2,512,384]{2,1,0:T(8,128)(2,1)} %collective-permute-done.6.refs_1_, ...), custom_call_target="tpu_custom_call" | custom-call | flops 3623878656 | bytes 3932160 | tf_op jit(solution)/shard_map/attention_forward/pallas_call | solution.py:290
  112.1 28.0 %attention_forward.3 = (bf16[4,192,128]{2,1,0:T(8,128)(2,1)}, f32[192,512]{1,0:T(8,128)}, f32[3,1,512]{2,1,0:T(1,128)}) custom-call(s32[1]{0:T(128)} %bitcast.19.info, bf16[512,192]{1,0:T(8,128)(2,1)} %fusion.16.q_ref, bf16[2,512,384]{2,1,0:T(8,128)(2,1)} %pad_maximum_fusion.9.refs_0_, bf16[2,512,384]{2,1,0:T(8,128)(2,1)} %collective-permute-done.10.refs_1_, ...), custom_call_target="tpu_custom_call" | custom-call | flops 3623878656 | bytes 3932160 | tf_op jit(solution)/shard_map/attention_forward/pallas_call | solution.py:290
  156.6 18.3 %collective-permute-done.13 = bf16[768,768]{1,0:T(8,128)(2,1)} collective-permute-done((bf16[768,768]{1,0:T(8,128)(2,1)}, bf16[768,768]{1,0:T(8,128)(2,1)}, u32[]{:S(2)}, u32[]{:S(2)}) %collective-permute-start.13) | collective-permute-done | bytes 1179680 | tf_op jit(solution)/shard_map/ppermute | solution.py:37
  188.0 5.1 %convert_reduce_fusion = (bf16[1536]{0:T(1024)(128)(2,1)}, bf16[512,1536]{1,0:T(8,128)(2,1)S(1)}) fusion(f32[512,1536]{1,0:T(8,128)S(1)} %get-tuple-element.223, bf16[1536,768]{1,0:T(8,128)(2,1)S(1)} %bitcast.260, bf16[256,768]{1,0:T(8,128)(2,1)} %collective-permute-done.18, bf16[256,768]{1,0:T(8,128)(2,1)S(1)} %bitcast.249), kind=kOutput, calls=%fused_computation.12 | convolution fusion | flops 1226832384 | bytes 7867392 | tf_op jit(solution)/shard_map/dot_general | solution.py:101
  218.1 15.8 %all_to_all.20.go_ref = bf16[4,192,256]{2,1,0:T(8,128)(2,1)} all-to-all(bf16[4,192,256]{2,1,0:T(8,128)(2,1)S(1)} %bitcast.265), channel_id=1, replica_groups=mesh['ctx'=8,'shard'=4] {'shard'}, dimensions={0} | all-to-all | bytes 786432 | tf_op jit(solution)/shard_map/all_to_all | solution.py:527
  234.0 22.8 %attention_backward.3 = (bf16[512,192]{1,0:T(8,128)(2,1)}, bf16[2,512,384]{2,1,0:T(8,128)(2,1)}, bf16[2,512,384]{2,1,0:T(8,128)(2,1)}, bf16[4,512,384]{2,1,0:T(8,128)(2,1)}) custom-call(s32[1]{0:T(128)} %bitcast.19.info, bf16[512,192]{1,0:T(8,128)(2,1)} %fusion.16.q_ref, f32[192,512]{1,0:T(8,128)} %get-tuple-element.84.out_ref, ...), custom_call_target="tpu_custom_call" | custom-call | flops 2264924160 | bytes 7864320 | tf_op jit(solution)/shard_map/attention_backward/pallas_call | solution.py:322
  256.9 7.8 %attention_backward.2 = (bf16[512,192]{1,0:T(8,128)(2,1)}, bf16[2,512,384]{2,1,0:T(8,128)(2,1)}, bf16[2,512,384]{2,1,0:T(8,128)(2,1)}, bf16[4,512,384]{2,1,0:T(8,128)(2,1)}) custom-call(s32[1]{0:T(128)} %bitcast.7.info, bf16[512,192]{1,0:T(8,128)(2,1)} %fusion.15.q_ref, f32[192,512]{1,0:T(8,128)} %get-tuple-element.74.out_ref, ...), custom_call_target="tpu_custom_call" | custom-call | flops 2264924160 | bytes 7864320 | tf_op jit(solution)/shard_map/attention_backward/pallas_call | solution.py:322
  276.3 3.8 collective-permute-start.27
  290.8 7.3 %collective-permute-done.27 = bf16[2,512,384]{2,1,0:T(8,128)(2,1)} collective-permute-done((bf16[2,512,384]{2,1,0:T(8,128)(2,1)}, bf16[2,512,384]{2,1,0:T(8,128)(2,1)}, u32[]{:S(2)}, u32[]{:S(2)}) %collective-permute-start.27) | collective-permute-done | bytes 786464 | tf_op jit(solution)/shard_map/ppermute | solution.py:77
  310.3 7.1 %collective-permute-done.25 = bf16[1,512,384]{2,1,0:T(8,128)(2,1)S(1)} collective-permute-done((bf16[1,512,384]{2,1,0:T(8,128)(2,1)S(1)}, bf16[1,512,384]{2,1,0:T(8,128)(2,1)S(1)}, u32[]{:S(2)}, u32[]{:S(2)}) %collective-permute-start.25) | collective-permute-done | bytes 393248 | tf_op jit(solution)/shard_map/ppermute | solution.py:82
  338.0 6.7 %collective-permute-done.43 = bf16[192,768]{1,0:T(8,128)(2,1)S(1)} collective-permute-done((bf16[192,768]{1,0:T(8,128)(2,1)S(1)}, bf16[192,768]{1,0:T(8,128)(2,1)S(1)}, u32[]{:S(2)}, u32[]{:S(2)}) %collective-permute-start.43) | collective-permute-done | bytes 294944 | tf_op jit(solution)/shard_map/ppermute | solution.py:37
  351.3 3.6 collective-permute-done.35
  359.9 7.1 %all-to-all-done.3 = bf16[4,24,576]{2,1,0:T(8,128)(2,1)S(1)} async-done(((bf16[4,24,576]{2,1,0:T(8,128)(2,1)}), bf16[4,24,576]{2,1,0:T(8,128)(2,1)S(1)}, u32[]{:S(2)}, u32[]{:S(2)}) %all-to-all-start.3) | async-done | bytes 110624 | tf_op jit(solution)/shard_map/all_to_all | solution.py:651
  380.5 4.0 collective-permute-done.31
  387.1 6.5 %collective-permute-done.32 = f32[12,192]{1,0:T(8,128)S(1)} collective-permute-done((f32[12,192]{1,0:T(8,128)S(1)}, f32[12,192]{1,0:T(8,128)S(1)}, u32[]{:S(2)}, u32[]{:S(2)}) %collective-permute-start.32) | collective-permute-done | bytes 9248 | tf_op jit(solution)/shard_map/ppermute | solution.py:37
  (427 shorter events, 184.7 us)
Async XLA Ops:
  7.2 53.8 %all-gather.5.cloned.1.call-start = ((), (), s32[]{:S(2)}) async-start(), calls=%async_computation.8 | async-start | bytes 1966080 | tf_op jit(solution)/shard_map/all_gather | solution.py:421
  21.7 17.3 %all-to-all-start = ((bf16[4,40,576]{2,1,0:T(8,128)(2,1)}), bf16[4,40,576]{2,1,0:T(8,128)(2,1)S(1)}, u32[]{:S(2)}, u32[]{:S(2)}) async-start(bf16[4,40,576]{2,1,0:T(8,128)(2,1)} %pad_maximum_fusion.29), calls=%async_computation | async-start | bytes 409600 | tf_op jit(solution)/shard_map/all_to_all | solution.py:422
  26.6 115.3 %all-gather.7.cloned.1.call-start = ((), (), s32[]{:S(2)}) async-start(), calls=%async_computation.9 | async-start | bytes 3686400 | tf_op jit(solution)/shard_map/all_gather | solution.py:464
  66.3 18.4 %collective-permute-start.9 = (bf16[1,512,384]{2,1,0:T(8,128)(2,1)S(1)}, bf16[1,512,384]{2,1,0:T(8,128)(2,1)S(1)}, u32[]{:S(2)}, u32[]{:S(2)}) collective-permute-start(bf16[1,512,384]{2,1,0:T(8,128)(2,1)S(1)} %fusion.13), channel_id=1, source_target_pairs={{16,0},{20,4},{24,8},{28,12},{17,1},{21,5},{25,9},{29,13},{18,2},{... | collective-permute-start | bytes 1179656 | tf_op jit(solution)/shard_map/ppermute | solution.py:58
  81.4 18.3 %collective-permute-start.6 = (bf16[2,512,384]{2,1,0:T(8,128)(2,1)S(1)}, bf16[2,512,384]{2,1,0:T(8,128)(2,1)}, u32[]{:S(2)}, u32[]{:S(2)}) collective-permute-start(bf16[2,512,384]{2,1,0:T(8,128)(2,1)S(1)} %pad_maximum_fusion.8.refs_0_), channel_id=1, source_target_pairs={{0,16},{4,20},{8,24},{12,28},{1,17},{5,21},{9,25},{13,29},{2,18},{... | collective-permute-start | bytes 2359304 | tf_op jit(solution)/shard_map/ppermute | solution.py:62
  85.8 21.2 %collective-permute-start.10 = (bf16[2,512,384]{2,1,0:T(8,128)(2,1)}, bf16[2,512,384]{2,1,0:T(8,128)(2,1)}, u32[]{:S(2)}, u32[]{:S(2)}) collective-permute-start(bf16[2,512,384]{2,1,0:T(8,128)(2,1)} %pad_maximum_fusion.9.refs_0_), channel_id=1, source_target_pairs={{0,8},{4,12},{8,0},{12,4},{24,16},{28,20},{1,9},{5,13},{9,1},{13,5... | collective-permute-start | bytes 2359304 | tf_op jit(solution)/shard_map/ppermute | solution.py:62
  90.2 16.8 %collective-permute-start.7 = (bf16[2,512,384]{2,1,0:T(8,128)(2,1)S(1)}, bf16[2,512,384]{2,1,0:T(8,128)(2,1)}, u32[]{:S(2)}, u32[]{:S(2)}) collective-permute-start(bf16[2,512,384]{2,1,0:T(8,128)(2,1)S(1)} %pad_maximum_fusion.8.refs_0_), channel_id=1, source_target_pairs={{0,4},{4,0},{8,12},{12,8},{16,20},{20,16},{24,28},{28,24},{1,5},{5... | collective-permute-start | bytes 2359304 | tf_op jit(solution)/shard_map/ppermute | solution.py:37
  146.1 28.7 %collective-permute-start.13 = (bf16[768,768]{1,0:T(8,128)(2,1)}, bf16[768,768]{1,0:T(8,128)(2,1)}, u32[]{:S(2)}, u32[]{:S(2)}) collective-permute-start(bf16[768,768]{1,0:T(8,128)(2,1)} %bitcast.23), channel_id=1, source_target_pairs={{0,8},{4,12},{8,0},{12,4},{16,24},{20,28},{24,16},{28,20},{1,9},{5... | collective-permute-start | bytes 3538952 | tf_op jit(solution)/shard_map/ppermute | solution.py:37
  150.4 37.6 %collective-permute-start.18 = (bf16[256,768]{1,0:T(8,128)(2,1)S(1)}, bf16[256,768]{1,0:T(8,128)(2,1)}, u32[]{:S(2)}, u32[]{:S(2)}) collective-permute-start(bf16[256,768]{1,0:T(8,128)(2,1)S(1)} %bitcast.248), channel_id=1, source_target_pairs={{0,4},{4,0},{8,12},{12,8},{16,20},{20,16},{24,28},{28,24},{1,5},{5... | collective-permute-start | bytes 1179656 | tf_op jit(solution)/shard_map/ppermute | solution.py:37
  150.6 27.6 %all-to-all-start.1 = ((bf16[4,192,256]{2,1,0:T(8,128)(2,1)}), bf16[4,192,256]{2,1,0:T(8,128)(2,1)S(1)}, u32[]{:S(2)}, u32[]{:S(2)}) async-start(bf16[4,192,256]{2,1,0:T(8,128)(2,1)} %pad_maximum_fusion.24), calls=%async_computation.1 | async-start | bytes 786432 | tf_op jit(solution)/shard_map/all_to_all | solution.py:498
  154.1 170.9 %reduce-scatter.3.cloned.1.call-start = ((), (), s32[]{:S(2)}) async-start(), calls=%async_computation.6 | async-start | bytes 3317760 | tf_op jit(solution)/shard_map/reduce_scatter | solution.py:565
  154.2 28.5 %collective-permute-start.16 = (bf16[4,192,768]{2,1,0:T(8,128)(2,1)}, bf16[4,192,768]{2,1,0:T(8,128)(2,1)}, u32[]{:S(2)}, u32[]{:S(2)}) collective-permute-start(bf16[4,192,768]{2,1,0:T(8,128)(2,1)} %get-tuple-element.72), channel_id=1, source_target_pairs={{0,16},{4,20},{8,24},{12,28},{16,0},{20,4},{24,8},{28,12},{1,17},{... | collective-permute-start | bytes 3538952 | tf_op jit(solution)/shard_map/ppermute | solution.py:37
  213.6 53.7 %collective-permute-start.24 = (bf16[4,192,768]{2,1,0:T(8,128)(2,1)}, bf16[4,192,768]{2,1,0:T(8,128)(2,1)}, u32[]{:S(2)}, u32[]{:S(2)}) collective-permute-start(bf16[4,192,768]{2,1,0:T(8,128)(2,1)} %select_bitcast_fusion), channel_id=1, source_target_pairs={{0,16},{4,20},{8,24},{12,28},{16,0},{20,4},{24,8},{28,12},{1,17},{... | collective-permute-start | bytes 3538952 | tf_op jit(solution)/shard_map/ppermute | solution.py:37
  217.6 51.4 %collective-permute-start.23 = (bf16[4,240,768]{2,1,0:T(8,128)(2,1)}, bf16[4,240,768]{2,1,0:T(8,128)(2,1)}, u32[]{:S(2)}, u32[]{:S(2)}) collective-permute-start(bf16[4,240,768]{2,1,0:T(8,128)(2,1)} %broadcast_select_fusion), channel_id=1, source_target_pairs={{0,8},{4,12},{8,0},{12,4},{16,24},{20,28},{24,16},{28,20},{1,9},{5... | collective-permute-start | bytes 4423688 | tf_op jit(solution)/shard_map/ppermute | solution.py:37
  256.8 17.3 %collective-permute-start.26 = (bf16[4,512,384]{2,1,0:T(8,128)(2,1)}, bf16[4,512,384]{2,1,0:T(8,128)(2,1)}, u32[]{:S(2)}, u32[]{:S(2)}) collective-permute-start(bf16[4,512,384]{2,1,0:T(8,128)(2,1)} %get-tuple-element.91), channel_id=1, source_target_pairs={{0,4},{4,0},{8,12},{12,8},{16,20},{20,16},{24,28},{28,24},{1,5},{5... | collective-permute-start | bytes 4718600 | tf_op jit(solution)/shard_map/ppermute | solution.py:37
  264.6 15.5 %collective-permute-start.21 = (bf16[4,512,384]{2,1,0:T(8,128)(2,1)}, bf16[4,512,384]{2,1,0:T(8,128)(2,1)}, u32[]{:S(2)}, u32[]{:S(2)}) collective-permute-start(bf16[4,512,384]{2,1,0:T(8,128)(2,1)} %get-tuple-element.82), channel_id=1, source_target_pairs={{0,4},{4,0},{8,12},{12,8},{16,20},{20,16},{24,28},{28,24},{1,5},{5... | collective-permute-start | bytes 4718600 | tf_op jit(solution)/shard_map/ppermute | solution.py:37
  272.7 99.4 %reduce-scatter.5.cloned.1.call-start = ((), (), s32[]{:S(2)}) async-start(), calls=%async_computation.7 | async-start | bytes 2088960 | tf_op jit(solution)/shard_map/reduce_scatter | solution.py:606
  276.3 21.8 %collective-permute-start.27 = (bf16[2,512,384]{2,1,0:T(8,128)(2,1)}, bf16[2,512,384]{2,1,0:T(8,128)(2,1)}, u32[]{:S(2)}, u32[]{:S(2)}) collective-permute-start(bf16[2,512,384]{2,1,0:T(8,128)(2,1)} %add_convert_fusion.3), channel_id=1, source_target_pairs={{8,0},{12,4},{0,8},{4,12},{16,24},{20,28},{9,1},{13,5},{1,9},{5,13... | collective-permute-start | bytes 2359304 | tf_op jit(solution)/shard_map/ppermute | solution.py:77
  282.4 21.4 %collective-permute-start.22 = (bf16[2,512,384]{2,1,0:T(8,128)(2,1)}, bf16[2,512,384]{2,1,0:T(8,128)(2,1)}, u32[]{:S(2)}, u32[]{:S(2)}) collective-permute-start(bf16[2,512,384]{2,1,0:T(8,128)(2,1)} %add_convert_fusion.6), channel_id=1, source_target_pairs={{16,0},{20,4},{24,8},{28,12},{17,1},{21,5},{25,9},{29,13},{18,2},{... | collective-permute-start | bytes 2359304 | tf_op jit(solution)/shard_map/ppermute | solution.py:77
  344.8 14.1 %collective-permute-start.44 = (bf16[192,768]{1,0:T(8,128)(2,1)S(1)}, bf16[192,768]{1,0:T(8,128)(2,1)}, u32[]{:S(2)}, u32[]{:S(2)}) collective-permute-start(bf16[192,768]{1,0:T(8,128)(2,1)S(1)} %add_convert_fusion.16), channel_id=1, source_target_pairs={{0,16},{4,20},{8,24},{12,28},{16,0},{20,4},{24,8},{28,12},{1,17},{... | collective-permute-start | bytes 884744 | tf_op jit(solution)/shard_map/ppermute | solution.py:37
  349.7 19.1 %collective-permute-start.40 = (bf16[240,768]{1,0:T(8,128)(2,1)S(1)}, bf16[240,768]{1,0:T(8,128)(2,1)S(1)}, u32[]{:S(2)}, u32[]{:S(2)}) collective-permute-start(bf16[240,768]{1,0:T(8,128)(2,1)S(1)} %add_convert_fusion.15), channel_id=1, source_target_pairs={{0,8},{4,12},{8,0},{12,4},{16,24},{20,28},{24,16},{28,20},{1,9},{5... | collective-permute-start | bytes 1105928 | tf_op jit(solution)/shard_map/ppermute | solution.py:37
  375.5 19.3 %collective-permute-start.41 = (bf16[96,768]{1,0:T(8,128)(2,1)}, bf16[96,768]{1,0:T(8,128)(2,1)}, u32[]{:S(2)}, u32[]{:S(2)}) collective-permute-start(bf16[96,768]{1,0:T(8,128)(2,1)} %pad_maximum_fusion.30), channel_id=1, source_target_pairs={{0,4},{4,0},{8,12},{12,8},{16,20},{20,16},{24,28},{28,24},{1,5},{5... | collective-permute-start | bytes 442376 | tf_op jit(solution)/shard_map/ppermute | solution.py:37
  376.0 20.6 %collective-permute-start.37 = (bf16[48,2304]{1,0:T(8,128)(2,1)S(1)}, bf16[48,2304]{1,0:T(8,128)(2,1)}, u32[]{:S(2)}, u32[]{:S(2)}) collective-permute-start(bf16[48,2304]{1,0:T(8,128)(2,1)S(1)} %pad_maximum_fusion.28), channel_id=1, source_target_pairs={{0,8},{4,12},{8,0},{12,4},{16,24},{20,28},{24,16},{28,20},{1,9},{5... | collective-permute-start | bytes 663560 | tf_op jit(solution)/shard_map/ppermute | solution.py:37
  378.9 19.3 %collective-permute-start.29 = (bf16[2,128,768]{2,1,0:T(8,128)(2,1)}, bf16[2,128,768]{2,1,0:T(8,128)(2,1)}, u32[]{:S(2)}, u32[]{:S(2)}) collective-permute-start(bf16[2,128,768]{2,1,0:T(8,128)(2,1)} %fusion.33), channel_id=1, source_target_pairs={{0,28},{4,24},{8,20},{12,16},{16,12},{20,8},{24,4},{28,0},{1,29},{... | collective-permute-start | bytes 1179656 | tf_op jit(solution)/shard_map/ppermute | solution.py:92
  (92 other events, 663.3 us)
Sparse Core Ops, SparseCore 0:
  20.7 40.2 all-gather.4
  63.1 57.4 all-gather.6
  272.8 51.5 reduce-scatter.2
  329.8 37.3 reduce-scatter.4

commit v6 on v5

--- a/solution.py
+++ b/solution.py
@@ -620,11 +620,9 @@
     cut = both.shape[0] - quarter
     out_grad = summed_over_chips(both[cut:], [bit for bit in chip_bits if bit != OUT_BIT])
     out_grad = jnp.concatenate(joined(out_grad.astype(bf16), OUT_BIT, out_side))
-    out_grad = after(out_grad, summed)
     out_grad = jnp.concatenate(pair_joined(out_grad, odd)).astype(f32)
     rest = summed_over_chips(both[:cut], [bit for bit in chip_bits if bit != FC_BIT])
     first, second = joined(rest.astype(bf16), FC_BIT, fc_side)
-    first, second = after(first, summed), after(second, summed)
     proj_grad = jnp.concatenate([first[local_width:], second[local_width:]])
     proj_grad = jnp.concatenate(pair_joined(proj_grad, odd)).astype(f32)
     fc_grad = jnp.concatenate([first[:local_width], second[:local_width]], axis=1)

time: 419 us -> 421 us (level)
    ppermute x3, waiting for transfers between devices: 0.01 us -> 8.47 us  [mirrored(): return lax.ppermute(block, 'ctx', [(i, n - 1 - i) for i in range(n)])]
    ppermute x35, waiting for transfers between devices: 57 us -> 51.3 us  [swapped(): return lax.ppermute(block, 'ctx', [(i, i ^ 1 << bit) for i in range(n)])]
  transfers between devices with their start and end apart: 53 -> 53, of which waited for: 21 -> 25; matrix products, arithmetic and copies ran while one was open for 23% -> 24% of each run, Pallas kernels for 15% -> 15%
where the time goes in v6:
time: 421 us; the launch traced here: 416 us
  waiting for transfers between devices  127 us (30%)
  Pallas kernels  63.6 us (15%)
  other arithmetic  62.9 us (15%)
  starting transfers between devices  60.8 us (14%)
  local copies, waits for them, and re-layouts  43 us (10%)
  matrix products  27.4 us (7%)
  blocking collectives  15.8 us (4%)
  between operations  15.5 us (4%)
    ppermute x35, waiting for transfers between devices, swapped(): return lax.ppermute(block, 'ctx', [(i, i ^ 1 << bit) for i in range(n)])  51.3 us
    pallas_call x2, Pallas kernels, attend(): pl.pallas_call(functools.partial(forward_kernel, heads, shards, order), o...  33 us
    pallas_call x2, Pallas kernels, attend_back(): pl.pallas_call(functools.partial(backward_kernel, heads, shards, order, f...  30.6 us
    dot_general x19, matrix products, dot(): lax.dot_general(a, b, ((contract[0], contract[1]), ((), ())), preferred_e...  27.4 us
    ppermute x35, starting transfers between devices, swapped(): return lax.ppermute(block, 'ctx', [(i, i ^ 1 << bit) for i in range(n)])  21.7 us
    ppermute x2, waiting for transfers between devices, spread(): lax.ppermute(held, 'ctx', tree_pairs(aparts, bit, order[-1:], late, False))  16.2 us
    all_to_all x1, blocking collectives, body(): grad_heads = lax.all_to_all(grad_attended, 'shard', 0, 0, tiled=True)  15.8 us
    convert_element_type x10, other arithmetic, added(): return (first.astype(f32) + second.astype(f32)).astype(bf16)  12.9 us
  transfers between devices with their start and end apart: 53, of which 25 were waited for; matrix products, arithmetic and copies ran while one was open for 24% of the time, Pallas kernels for 15%

profile of v6, /device:TPU:0, one launch (start us, length us, event | category | flops | bytes accessed | tf_op | source)
XLA Modules:
  0.0 416.2 jit_solution(1708030437066174381)
XLA Ops:
  21.7 4.9 %all-to-all-start = ((bf16[4,40,576]{2,1,0:T(8,128)(2,1)}), bf16[4,40,576]{2,1,0:T(8,128)(2,1)S(1)}, u32[]{:S(2)}, u32[]{:S(2)}) async-start(bf16[4,40,576]{2,1,0:T(8,128)(2,1)} %pad_maximum_fusion.29), calls=%async_computation | async-start | bytes 409600 | tf_op jit(solution)/shard_map/all_to_all | solution.py:422
  28.1 10.8 %all-to-all-done = bf16[4,40,576]{2,1,0:T(8,128)(2,1)S(1)} async-done(((bf16[4,40,576]{2,1,0:T(8,128)(2,1)}), bf16[4,40,576]{2,1,0:T(8,128)(2,1)S(1)}, u32[]{:S(2)}, u32[]{:S(2)}) %all-to-all-start) | async-done | bytes 184352 | tf_op jit(solution)/shard_map/all_to_all | solution.py:422
  39.3 4.7 %collective-permute-done.1 = bf16[4,24,576]{2,1,0:T(8,128)(2,1)S(1)} collective-permute-done((bf16[4,24,576]{2,1,0:T(8,128)(2,1)S(1)}, bf16[4,24,576]{2,1,0:T(8,128)(2,1)S(1)}, u32[]{:S(2)}, u32[]{:S(2)}) %collective-permute-start.1) | collective-permute-done | bytes 110624 | tf_op jit(solution)/shard_map/ppermute | solution.py:37
  45.5 4.8 %collective-permute-done.2 = bf16[4,48,576]{2,1,0:T(8,128)(2,1)S(1)} collective-permute-done((bf16[4,48,576]{2,1,0:T(8,128)(2,1)S(1)}, bf16[4,48,576]{2,1,0:T(8,128)(2,1)S(1)}, u32[]{:S(2)}, u32[]{:S(2)}) %collective-permute-start.2) | collective-permute-done | bytes 221216 | tf_op jit(solution)/shard_map/ppermute | solution.py:37
  50.4 10.6 %all-gather.5.cloned.1.call-done = bf16[8,128,768]{2,1,0:T(8,128)(2,1)} async-done(((bf16[2,128,768]{2,1,0:T(8,128)(2,1)}), bf16[8,128,768]{2,1,0:T(8,128)(2,1)}) %all-gather.5.cloned.1.call-update) | async-done | bytes 1572880 | tf_op jit(solution)/shard_map/all_gather | solution.py:421
  73.0 8.4 %collective-permute-done.5 = bf16[1,512,384]{2,1,0:T(8,128)(2,1)S(1)} collective-permute-done((bf16[1,512,384]{2,1,0:T(8,128)(2,1)S(1)}, bf16[1,512,384]{2,1,0:T(8,128)(2,1)S(1)}, u32[]{:S(2)}, u32[]{:S(2)}) %collective-permute-start.5) | collective-permute-done | bytes 393248 | tf_op jit(solution)/shard_map/ppermute | solution.py:58
  85.7 4.4 %collective-permute-start.10 = (bf16[2,512,384]{2,1,0:T(8,128)(2,1)}, bf16[2,512,384]{2,1,0:T(8,128)(2,1)}, u32[]{:S(2)}, u32[]{:S(2)}) collective-permute-start(bf16[2,512,384]{2,1,0:T(8,128)(2,1)} %pad_maximum_fusion.9.refs_0_), channel_id=1, source_target_pairs={{0,8},{4,12},{8,0},{12,4},{24,16},{28,20},{1,9},{5,13},{9,1},{13,5... | collective-permute-start | bytes 2359304 | tf_op jit(solution)/shard_map/ppermute | solution.py:62
  90.2 9.6 %collective-permute-done.6.refs_1_ = bf16[2,512,384]{2,1,0:T(8,128)(2,1)} collective-permute-done((bf16[2,512,384]{2,1,0:T(8,128)(2,1)S(1)}, bf16[2,512,384]{2,1,0:T(8,128)(2,1)}, u32[]{:S(2)}, u32[]{:S(2)}) %collective-permute-start.6) | collective-permute-done | bytes 786464 | tf_op jit(solution)/shard_map/ppermute | solution.py:62
  100.3 6.6 %collective-permute-done.10.refs_1_ = bf16[2,512,384]{2,1,0:T(8,128)(2,1)} collective-permute-done((bf16[2,512,384]{2,1,0:T(8,128)(2,1)}, bf16[2,512,384]{2,1,0:T(8,128)(2,1)}, u32[]{:S(2)}, u32[]{:S(2)}) %collective-permute-start.10) | collective-permute-done | bytes 786464 | tf_op jit(solution)/shard_map/ppermute | solution.py:62
  106.9 5.0 %attention_forward.2 = (bf16[4,192,128]{2,1,0:T(8,128)(2,1)}, f32[192,512]{1,0:T(8,128)}, f32[3,1,512]{2,1,0:T(1,128)}) custom-call(s32[1]{0:T(128)} %bitcast.7.info, bf16[512,192]{1,0:T(8,128)(2,1)} %fusion.15.q_ref, bf16[2,512,384]{2,1,0:T(8,128)(2,1)} %copy-done.30, bf16[2,512,384]{2,1,0:T(8,128)(2,1)} %collective-permute-done.6.refs_1_, ...), custom_call_target="tpu_custom_call" | custom-call | flops 3623878656 | bytes 3932160 | tf_op jit(solution)/shard_map/attention_forward/pallas_call | solution.py:290
  112.0 28.0 %attention_forward.3 = (bf16[4,192,128]{2,1,0:T(8,128)(2,1)}, f32[192,512]{1,0:T(8,128)}, f32[3,1,512]{2,1,0:T(1,128)}) custom-call(s32[1]{0:T(128)} %bitcast.19.info, bf16[512,192]{1,0:T(8,128)(2,1)} %fusion.16.q_ref, bf16[2,512,384]{2,1,0:T(8,128)(2,1)} %pad_maximum_fusion.9.refs_0_, bf16[2,512,384]{2,1,0:T(8,128)(2,1)} %collective-permute-done.10.refs_1_, ...), custom_call_target="tpu_custom_call" | custom-call | flops 3623878656 | bytes 3932160 | tf_op jit(solution)/shard_map/attention_forward/pallas_call | solution.py:290
  150.5 3.5 all-to-all-start.1
  156.4 18.3 %collective-permute-done.13 = bf16[768,768]{1,0:T(8,128)(2,1)} collective-permute-done((bf16[768,768]{1,0:T(8,128)(2,1)}, bf16[768,768]{1,0:T(8,128)(2,1)}, u32[]{:S(2)}, u32[]{:S(2)}) %collective-permute-start.13) | collective-permute-done | bytes 1179680 | tf_op jit(solution)/shard_map/ppermute | solution.py:37
  187.9 5.1 %convert_reduce_fusion = (bf16[1536]{0:T(1024)(128)(2,1)}, bf16[512,1536]{1,0:T(8,128)(2,1)S(1)}) fusion(f32[512,1536]{1,0:T(8,128)S(1)} %get-tuple-element.217, bf16[1536,768]{1,0:T(8,128)(2,1)S(1)} %bitcast.260, bf16[256,768]{1,0:T(8,128)(2,1)} %collective-permute-done.18, bf16[256,768]{1,0:T(8,128)(2,1)S(1)} %bitcast.249), kind=kOutput, calls=%fused_computation.12 | convolution fusion | flops 1226832384 | bytes 7867392 | tf_op jit(solution)/shard_map/dot_general | solution.py:101
  218.1 15.8 %all_to_all.20.go_ref = bf16[4,192,256]{2,1,0:T(8,128)(2,1)} all-to-all(bf16[4,192,256]{2,1,0:T(8,128)(2,1)S(1)} %bitcast.265), channel_id=1, replica_groups=mesh['ctx'=8,'shard'=4] {'shard'}, dimensions={0} | all-to-all | bytes 786432 | tf_op jit(solution)/shard_map/all_to_all | solution.py:527
  234.0 22.8 %attention_backward.3 = (bf16[512,192]{1,0:T(8,128)(2,1)}, bf16[2,512,384]{2,1,0:T(8,128)(2,1)}, bf16[2,512,384]{2,1,0:T(8,128)(2,1)}, bf16[4,512,384]{2,1,0:T(8,128)(2,1)}) custom-call(s32[1]{0:T(128)} %bitcast.19.info, bf16[512,192]{1,0:T(8,128)(2,1)} %fusion.16.q_ref, f32[192,512]{1,0:T(8,128)} %get-tuple-element.81.out_ref, ...), custom_call_target="tpu_custom_call" | custom-call | flops 2264924160 | bytes 7864320 | tf_op jit(solution)/shard_map/attention_backward/pallas_call | solution.py:322
  256.9 7.8 %attention_backward.2 = (bf16[512,192]{1,0:T(8,128)(2,1)}, bf16[2,512,384]{2,1,0:T(8,128)(2,1)}, bf16[2,512,384]{2,1,0:T(8,128)(2,1)}, bf16[4,512,384]{2,1,0:T(8,128)(2,1)}) custom-call(s32[1]{0:T(128)} %bitcast.7.info, bf16[512,192]{1,0:T(8,128)(2,1)} %fusion.15.q_ref, f32[192,512]{1,0:T(8,128)} %get-tuple-element.71.out_ref, ...), custom_call_target="tpu_custom_call" | custom-call | flops 2264924160 | bytes 7864320 | tf_op jit(solution)/shard_map/attention_backward/pallas_call | solution.py:322
  276.2 3.8 collective-permute-start.27
  290.8 7.3 %collective-permute-done.27 = bf16[2,512,384]{2,1,0:T(8,128)(2,1)} collective-permute-done((bf16[2,512,384]{2,1,0:T(8,128)(2,1)}, bf16[2,512,384]{2,1,0:T(8,128)(2,1)}, u32[]{:S(2)}, u32[]{:S(2)}) %collective-permute-start.27) | collective-permute-done | bytes 786464 | tf_op jit(solution)/shard_map/ppermute | solution.py:77
  310.2 7.1 %collective-permute-done.25 = bf16[1,512,384]{2,1,0:T(8,128)(2,1)S(1)} collective-permute-done((bf16[1,512,384]{2,1,0:T(8,128)(2,1)S(1)}, bf16[1,512,384]{2,1,0:T(8,128)(2,1)S(1)}, u32[]{:S(2)}, u32[]{:S(2)}) %collective-permute-start.25) | collective-permute-done | bytes 393248 | tf_op jit(solution)/shard_map/ppermute | solution.py:82
  350.2 7.8 %collective-permute-done.34 = bf16[4,48,576]{2,1,0:T(8,128)(2,1)S(1)} collective-permute-done((bf16[4,48,576]{2,1,0:T(8,128)(2,1)S(1)}, bf16[4,48,576]{2,1,0:T(8,128)(2,1)S(1)}, u32[]{:S(2)}, u32[]{:S(2)}) %collective-permute-start.34) | collective-permute-done | bytes 221216 | tf_op jit(solution)/shard_map/ppermute | solution.py:37
  363.8 4.3 %all-to-all-start.3 = ((bf16[4,24,576]{2,1,0:T(8,128)(2,1)}), bf16[4,24,576]{2,1,0:T(8,128)(2,1)}, u32[]{:S(2)}, u32[]{:S(2)}) async-start(bf16[4,24,576]{2,1,0:T(8,128)(2,1)} %add_convert_fusion.18), calls=%async_computation.5 | async-start | bytes 245760 | tf_op jit(solution)/shard_map/all_to_all | solution.py:649
  369.0 5.0 %all-to-all-done.3 = bf16[4,24,576]{2,1,0:T(8,128)(2,1)} async-done(((bf16[4,24,576]{2,1,0:T(8,128)(2,1)}), bf16[4,24,576]{2,1,0:T(8,128)(2,1)}, u32[]{:S(2)}, u32[]{:S(2)}) %all-to-all-start.3) | async-done | bytes 110624 | tf_op jit(solution)/shard_map/all_to_all | solution.py:649
  397.0 8.5 %collective-permute-done.29 = bf16[2,128,768]{2,1,0:T(8,128)(2,1)S(1)} collective-permute-done((bf16[2,128,768]{2,1,0:T(8,128)(2,1)S(1)}, bf16[2,128,768]{2,1,0:T(8,128)(2,1)S(1)}, u32[]{:S(2)}, u32[]{:S(2)}) %collective-permute-start.29) | collective-permute-done | bytes 393248 | tf_op jit(solution)/shard_map/ppermute | solution.py:92
  (427 shorter events, 185.9 us)
Async XLA Ops:
  7.2 53.8 %all-gather.5.cloned.1.call-start = ((), (), s32[]{:S(2)}) async-start(), calls=%async_computation.8 | async-start | bytes 1966080 | tf_op jit(solution)/shard_map/all_gather | solution.py:421
  21.7 17.3 %all-to-all-start = ((bf16[4,40,576]{2,1,0:T(8,128)(2,1)}), bf16[4,40,576]{2,1,0:T(8,128)(2,1)S(1)}, u32[]{:S(2)}, u32[]{:S(2)}) async-start(bf16[4,40,576]{2,1,0:T(8,128)(2,1)} %pad_maximum_fusion.29), calls=%async_computation | async-start | bytes 409600 | tf_op jit(solution)/shard_map/all_to_all | solution.py:422
  26.6 115.2 %all-gather.7.cloned.1.call-start = ((), (), s32[]{:S(2)}) async-start(), calls=%async_computation.9 | async-start | bytes 3686400 | tf_op jit(solution)/shard_map/all_gather | solution.py:464
  66.3 18.4 %collective-permute-start.9 = (bf16[1,512,384]{2,1,0:T(8,128)(2,1)S(1)}, bf16[1,512,384]{2,1,0:T(8,128)(2,1)S(1)}, u32[]{:S(2)}, u32[]{:S(2)}) collective-permute-start(bf16[1,512,384]{2,1,0:T(8,128)(2,1)S(1)} %fusion.13), channel_id=1, source_target_pairs={{16,0},{20,4},{24,8},{28,12},{17,1},{21,5},{25,9},{29,13},{18,2},{... | collective-permute-start | bytes 1179656 | tf_op jit(solution)/shard_map/ppermute | solution.py:58
  68.3 13.1 %collective-permute-start.5 = (bf16[1,512,384]{2,1,0:T(8,128)(2,1)S(1)}, bf16[1,512,384]{2,1,0:T(8,128)(2,1)S(1)}, u32[]{:S(2)}, u32[]{:S(2)}) collective-permute-start(bf16[1,512,384]{2,1,0:T(8,128)(2,1)S(1)} %fusion.14), channel_id=1, source_target_pairs={{0,8},{4,12},{8,0},{12,4},{16,24},{20,28},{1,9},{5,13},{9,1},{13,5... | collective-permute-start | bytes 1179656 | tf_op jit(solution)/shard_map/ppermute | solution.py:58
  81.4 18.3 %collective-permute-start.6 = (bf16[2,512,384]{2,1,0:T(8,128)(2,1)S(1)}, bf16[2,512,384]{2,1,0:T(8,128)(2,1)}, u32[]{:S(2)}, u32[]{:S(2)}) collective-permute-start(bf16[2,512,384]{2,1,0:T(8,128)(2,1)S(1)} %pad_maximum_fusion.8.refs_0_), channel_id=1, source_target_pairs={{0,16},{4,20},{8,24},{12,28},{1,17},{5,21},{9,25},{13,29},{2,18},{... | collective-permute-start | bytes 2359304 | tf_op jit(solution)/shard_map/ppermute | solution.py:62
  85.7 21.2 %collective-permute-start.10 = (bf16[2,512,384]{2,1,0:T(8,128)(2,1)}, bf16[2,512,384]{2,1,0:T(8,128)(2,1)}, u32[]{:S(2)}, u32[]{:S(2)}) collective-permute-start(bf16[2,512,384]{2,1,0:T(8,128)(2,1)} %pad_maximum_fusion.9.refs_0_), channel_id=1, source_target_pairs={{0,8},{4,12},{8,0},{12,4},{24,16},{28,20},{1,9},{5,13},{9,1},{13,5... | collective-permute-start | bytes 2359304 | tf_op jit(solution)/shard_map/ppermute | solution.py:62
  90.1 16.8 %collective-permute-start.7 = (bf16[2,512,384]{2,1,0:T(8,128)(2,1)S(1)}, bf16[2,512,384]{2,1,0:T(8,128)(2,1)}, u32[]{:S(2)}, u32[]{:S(2)}) collective-permute-start(bf16[2,512,384]{2,1,0:T(8,128)(2,1)S(1)} %pad_maximum_fusion.8.refs_0_), channel_id=1, source_target_pairs={{0,4},{4,0},{8,12},{12,8},{16,20},{20,16},{24,28},{28,24},{1,5},{5... | collective-permute-start | bytes 2359304 | tf_op jit(solution)/shard_map/ppermute | solution.py:37
  146.0 28.7 %collective-permute-start.13 = (bf16[768,768]{1,0:T(8,128)(2,1)}, bf16[768,768]{1,0:T(8,128)(2,1)}, u32[]{:S(2)}, u32[]{:S(2)}) collective-permute-start(bf16[768,768]{1,0:T(8,128)(2,1)} %bitcast.23), channel_id=1, source_target_pairs={{0,8},{4,12},{8,0},{12,4},{16,24},{20,28},{24,16},{28,20},{1,9},{5... | collective-permute-start | bytes 3538952 | tf_op jit(solution)/shard_map/ppermute | solution.py:37
  150.3 37.6 %collective-permute-start.18 = (bf16[256,768]{1,0:T(8,128)(2,1)S(1)}, bf16[256,768]{1,0:T(8,128)(2,1)}, u32[]{:S(2)}, u32[]{:S(2)}) collective-permute-start(bf16[256,768]{1,0:T(8,128)(2,1)S(1)} %bitcast.248), channel_id=1, source_target_pairs={{0,4},{4,0},{8,12},{12,8},{16,20},{20,16},{24,28},{28,24},{1,5},{5... | collective-permute-start | bytes 1179656 | tf_op jit(solution)/shard_map/ppermute | solution.py:37
  150.5 27.6 %all-to-all-start.1 = ((bf16[4,192,256]{2,1,0:T(8,128)(2,1)}), bf16[4,192,256]{2,1,0:T(8,128)(2,1)S(1)}, u32[]{:S(2)}, u32[]{:S(2)}) async-start(bf16[4,192,256]{2,1,0:T(8,128)(2,1)} %pad_maximum_fusion.24), calls=%async_computation.1 | async-start | bytes 786432 | tf_op jit(solution)/shard_map/all_to_all | solution.py:498
  154.0 171.0 %reduce-scatter.3.cloned.1.call-start = ((), (), s32[]{:S(2)}) async-start(), calls=%async_computation.6 | async-start | bytes 3317760 | tf_op jit(solution)/shard_map/reduce_scatter | solution.py:565
  154.1 28.5 %collective-permute-start.16 = (bf16[4,192,768]{2,1,0:T(8,128)(2,1)}, bf16[4,192,768]{2,1,0:T(8,128)(2,1)}, u32[]{:S(2)}, u32[]{:S(2)}) collective-permute-start(bf16[4,192,768]{2,1,0:T(8,128)(2,1)} %get-tuple-element.69), channel_id=1, source_target_pairs={{0,16},{4,20},{8,24},{12,28},{16,0},{20,4},{24,8},{28,12},{1,17},{... | collective-permute-start | bytes 3538952 | tf_op jit(solution)/shard_map/ppermute | solution.py:37
  213.6 53.7 %collective-permute-start.24 = (bf16[4,192,768]{2,1,0:T(8,128)(2,1)}, bf16[4,192,768]{2,1,0:T(8,128)(2,1)}, u32[]{:S(2)}, u32[]{:S(2)}) collective-permute-start(bf16[4,192,768]{2,1,0:T(8,128)(2,1)} %select_bitcast_fusion), channel_id=1, source_target_pairs={{0,16},{4,20},{8,24},{12,28},{16,0},{20,4},{24,8},{28,12},{1,17},{... | collective-permute-start | bytes 3538952 | tf_op jit(solution)/shard_map/ppermute | solution.py:37
  217.5 51.4 %collective-permute-start.23 = (bf16[4,240,768]{2,1,0:T(8,128)(2,1)}, bf16[4,240,768]{2,1,0:T(8,128)(2,1)}, u32[]{:S(2)}, u32[]{:S(2)}) collective-permute-start(bf16[4,240,768]{2,1,0:T(8,128)(2,1)} %broadcast_select_fusion), channel_id=1, source_target_pairs={{0,8},{4,12},{8,0},{12,4},{16,24},{20,28},{24,16},{28,20},{1,9},{5... | collective-permute-start | bytes 4423688 | tf_op jit(solution)/shard_map/ppermute | solution.py:37
  256.8 17.2 %collective-permute-start.26 = (bf16[4,512,384]{2,1,0:T(8,128)(2,1)}, bf16[4,512,384]{2,1,0:T(8,128)(2,1)}, u32[]{:S(2)}, u32[]{:S(2)}) collective-permute-start(bf16[4,512,384]{2,1,0:T(8,128)(2,1)} %get-tuple-element.88), channel_id=1, source_target_pairs={{0,4},{4,0},{8,12},{12,8},{16,20},{20,16},{24,28},{28,24},{1,5},{5... | collective-permute-start | bytes 4718600 | tf_op jit(solution)/shard_map/ppermute | solution.py:37
  264.6 15.4 %collective-permute-start.21 = (bf16[4,512,384]{2,1,0:T(8,128)(2,1)}, bf16[4,512,384]{2,1,0:T(8,128)(2,1)}, u32[]{:S(2)}, u32[]{:S(2)}) collective-permute-start(bf16[4,512,384]{2,1,0:T(8,128)(2,1)} %get-tuple-element.79), channel_id=1, source_target_pairs={{0,4},{4,0},{8,12},{12,8},{16,20},{20,16},{24,28},{28,24},{1,5},{5... | collective-permute-start | bytes 4718600 | tf_op jit(solution)/shard_map/ppermute | solution.py:37
  272.6 112.3 %reduce-scatter.5.cloned.1.call-start = ((), (), s32[]{:S(2)}) async-start(), calls=%async_computation.7 | async-start | bytes 2088960 | tf_op jit(solution)/shard_map/reduce_scatter | solution.py:606
  276.2 21.8 %collective-permute-start.27 = (bf16[2,512,384]{2,1,0:T(8,128)(2,1)}, bf16[2,512,384]{2,1,0:T(8,128)(2,1)}, u32[]{:S(2)}, u32[]{:S(2)}) collective-permute-start(bf16[2,512,384]{2,1,0:T(8,128)(2,1)} %add_convert_fusion.3), channel_id=1, source_target_pairs={{8,0},{12,4},{0,8},{4,12},{16,24},{20,28},{9,1},{13,5},{1,9},{5,13... | collective-permute-start | bytes 2359304 | tf_op jit(solution)/shard_map/ppermute | solution.py:77
  282.3 21.4 %collective-permute-start.22 = (bf16[2,512,384]{2,1,0:T(8,128)(2,1)}, bf16[2,512,384]{2,1,0:T(8,128)(2,1)}, u32[]{:S(2)}, u32[]{:S(2)}) collective-permute-start(bf16[2,512,384]{2,1,0:T(8,128)(2,1)} %add_convert_fusion.6), channel_id=1, source_target_pairs={{16,0},{20,4},{24,8},{28,12},{17,1},{21,5},{25,9},{29,13},{18,2},{... | collective-permute-start | bytes 2359304 | tf_op jit(solution)/shard_map/ppermute | solution.py:77
  344.9 15.3 %collective-permute-start.40 = (bf16[240,768]{1,0:T(8,128)(2,1)S(1)}, bf16[240,768]{1,0:T(8,128)(2,1)S(1)}, u32[]{:S(2)}, u32[]{:S(2)}) collective-permute-start(bf16[240,768]{1,0:T(8,128)(2,1)S(1)} %add_convert_fusion.15), channel_id=1, source_target_pairs={{0,8},{4,12},{8,0},{12,4},{16,24},{20,28},{24,16},{28,20},{1,9},{5... | collective-permute-start | bytes 1105928 | tf_op jit(solution)/shard_map/ppermute | solution.py:37
  345.2 12.8 %collective-permute-start.34 = (bf16[4,48,576]{2,1,0:T(8,128)(2,1)S(1)}, bf16[4,48,576]{2,1,0:T(8,128)(2,1)S(1)}, u32[]{:S(2)}, u32[]{:S(2)}) collective-permute-start(bf16[4,48,576]{2,1,0:T(8,128)(2,1)S(1)} %broadcast_select_fusion.16), channel_id=1, source_target_pairs={{0,8},{4,12},{8,0},{12,4},{16,24},{20,28},{24,16},{28,20},{1,9},{5... | collective-permute-start | bytes 663560 | tf_op jit(solution)/shard_map/ppermute | solution.py:37
  350.2 29.7 %collective-permute-start.45 = (bf16[384,768]{1,0:T(8,128)(2,1)}, bf16[384,768]{1,0:T(8,128)(2,1)S(1)}, u32[]{:S(2)}, u32[]{:S(2)}) collective-permute-start(bf16[384,768]{1,0:T(8,128)(2,1)} %pad_maximum_fusion.14), channel_id=1, source_target_pairs={{0,4},{4,0},{8,12},{12,8},{16,20},{20,16},{24,28},{28,24},{1,5},{5... | collective-permute-start | bytes 1769480 | tf_op jit(solution)/shard_map/ppermute | solution.py:37
  361.2 20.5 %collective-permute-start.42 = (bf16[192,1536]{1,0:T(8,128)(2,1)}, bf16[192,1536]{1,0:T(8,128)(2,1)}, u32[]{:S(2)}, u32[]{:S(2)}) collective-permute-start(bf16[192,1536]{1,0:T(8,128)(2,1)} %pad_maximum_fusion.13), channel_id=1, source_target_pairs={{0,4},{4,0},{8,12},{12,8},{16,20},{20,16},{24,28},{28,24},{1,5},{5... | collective-permute-start | bytes 1769480 | tf_op jit(solution)/shard_map/ppermute | solution.py:37
  (92 other events, 658.4 us)
Sparse Core Ops, SparseCore 0:
  20.7 40.2 all-gather.4
  63.1 57.4 all-gather.6
  272.7 51.5 reduce-scatter.2
  329.7 35.8 reduce-scatter.4
